TPU v7x, 32 devices: a whole 2x2x4 slice. The times are simulated.
32 devices in a mesh: seq: 8 (over z, x), head: 4 (over y, core).
Axes of the slice: x: 2, y: 2, z: 4, core: 2. Of those that a mesh axis runs over, the one named last changes fastest.
Arguments:
- frames: bfloat16 [16384, 768], P(('seq', 'head')), may hold values from -6 to 6
- output_grad: bfloat16 [16384, 768], P(('seq', 'head')), may hold values from -6 to 6
- segment_ids: int32 [8, 2048], P('seq'), may hold values from 0 to 1, as said below
- qkv_weight: float32 [768, 2304], P(('seq', 'head')), may hold values from -0.21875 to 0.21875
- proj_weight: float32 [768, 768], P(('seq', 'head')), may hold values from -0.875 to 0.875
- up_weight: float32 [768, 3072], P(('seq', 'head')), may hold values from -0.21875 to 0.21875
- down_weight: float32 [3072, 768], P(('seq', 'head')), may hold values from -0.109375 to 0.109375
- conv_weight: float32 [128, 768, 48], P(None, ('seq', 'head')), may hold values from -0.078125 to 0.078125
- bias_gains: float32 [9, 768], P(None, ('seq', 'head')), may hold values from -1.2 to 2, as said below
- ffn_bias: float32 [3072], P(('seq', 'head')), may hold values from -1.2 to 1.2
- qkv_first: float32 [768, 2304], P(('seq', 'head')), may hold values from -0.00018310547 to 0.00018310547
- proj_first: float32 [768, 768], P(('seq', 'head')), may hold values from -0.00018310547 to 0.00018310547
- up_first: float32 [768, 3072], P(('seq', 'head')), may hold values from -0.00018310547 to 0.00018310547
- down_first: float32 [3072, 768], P(('seq', 'head')), may hold values from -0.00018310547 to 0.00018310547
- conv_first: float32 [128, 768, 48], P(None, ('seq', 'head')), may hold values from -0.00018310547 to 0.00018310547
- bias_gains_first: float32 [9, 768], P(None, ('seq', 'head')), may hold values from -0.00018310547 to 0.00018310547
- ffn_bias_first: float32 [3072], P(('seq', 'head')), may hold values from -0.00018310547 to 0.00018310547
- qkv_second: float32 [768, 2304], P(('seq', 'head')), may hold values from 8.4699366e-11 to 3.3879746e-10
- proj_second: float32 [768, 768], P(('seq', 'head')), may hold values from 8.4699366e-11 to 3.3879746e-10
- up_second: float32 [768, 3072], P(('seq', 'head')), may hold values from 8.4699366e-11 to 3.3879746e-10
- down_second: float32 [3072, 768], P(('seq', 'head')), may hold values from 8.4699366e-11 to 3.3879746e-10
- conv_second: float32 [128, 768, 48], P(None, ('seq', 'head')), may hold values from 8.4699366e-11 to 3.3879746e-10
- bias_gains_second: float32 [9, 768], P(None, ('seq', 'head')), may hold values from 8.4699366e-11 to 3.3879746e-10
- ffn_bias_second: float32 [3072], P(('seq', 'head')), may hold values from 8.4699366e-11 to 3.3879746e-10
Outputs:
- layer_out: bfloat16 [16384, 768], P(('seq', 'head'))
- frames_grad: float32 [16384, 768], P(('seq', 'head'))
- grad_norm: float32 [], replicated
- qkv_new: float32 [768, 2304], P(('seq', 'head'))
- proj_new: float32 [768, 768], P(('seq', 'head'))
- up_new: float32 [768, 3072], P(('seq', 'head'))
- down_new: float32 [3072, 768], P(('seq', 'head'))
- conv_new: float32 [128, 768, 48], P(None, ('seq', 'head'))
- bias_gains_new: float32 [9, 768], P(None, ('seq', 'head'))
- ffn_bias_new: float32 [3072], P(('seq', 'head'))
- qkv_first_new: float32 [768, 2304], P(('seq', 'head'))
- proj_first_new: float32 [768, 768], P(('seq', 'head'))
- up_first_new: float32 [768, 3072], P(('seq', 'head'))
- down_first_new: float32 [3072, 768], P(('seq', 'head'))
- conv_first_new: float32 [128, 768, 48], P(None, ('seq', 'head'))
- bias_gains_first_new: float32 [9, 768], P(None, ('seq', 'head'))
- ffn_bias_first_new: float32 [3072], P(('seq', 'head'))
- qkv_second_new: float32 [768, 2304], P(('seq', 'head'))
- proj_second_new: float32 [768, 768], P(('seq', 'head'))
- up_second_new: float32 [768, 3072], P(('seq', 'head'))
- down_second_new: float32 [3072, 768], P(('seq', 'head'))
- conv_second_new: float32 [128, 768, 48], P(None, ('seq', 'head'))
- bias_gains_second_new: float32 [9, 768], P(None, ('seq', 'head'))
- ffn_bias_second_new: float32 [3072], P(('seq', 'head'))
Inputs may be any that keep to these rules, and one draw needn't show every extreme that they name: `segment_ids`: each row of ids never falls and every id of 0 to 1 appears; an utterance has 1 to 1750 frames, and exactly one utterance of each row has exactly 1750. `bias_gains`: rows 4 and 7 are gains between 0.5 and 2; the other rows are biases.
All inputs are finite; a program needn't handle non-finite values.
Results may differ from a plain program's by a relative error of at most 0.015.
The roundings to bfloat16 on the way count: a program that leaves them out, or rounds other values in their place, can miss the bound.
Values may be sent and summed in bfloat16 or wider, within the bound.
A program may use at most 256 MiB of HBM per device.

v0:
```python
import jax
import jax.numpy as jnp
from jax import lax
from jax.sharding import PartitionSpec as P

HEADS = 12
HEAD_DIM = 64
STEP = 10


norm_eps = 1e-05
beta_first = 0.9
beta_second = 0.999
adam_eps = 1e-08
weight_rates = (0.02, 0.1, 0.02, 0.02, 0.02, 0.2, 0.2)
matrix_decay = 0.01
clip_bound = 1.0


def with_halo(cells, sides, width):
    for axis, dim in sides:
        count = lax.axis_size(axis)
        ends = count - 1
        head = lax.slice_in_dim(cells, 0, width, axis=dim)
        tail = lax.slice_in_dim(cells, cells.shape[dim] - width, cells.shape[dim], axis=dim)
        cells = jnp.concatenate(
            [
                lax.ppermute(tail, axis, [(i, (i + 1) % count) for i in range(ends)]),
                cells,
                lax.ppermute(head, axis, [((i + 1) % count, i) for i in range(ends)]),
            ],
            axis=dim,
        )
    return cells


def layer_norm(values, scale_gain, shift_row):
    center = values - jnp.mean(values, axis=-1, keepdims=True)
    spread = jnp.mean(center * center, axis=-1, keepdims=True)
    return center * lax.rsqrt(spread + norm_eps) * scale_gain + shift_row


def gelu_exact(values):
    return jax.nn.gelu(values, approximate=False)


def tap_rows(source, first_tap, row_count, tap_count, direction):
    return jnp.stack(
        [
            lax.dynamic_slice_in_dim(source, first_tap + direction * offset, row_count, 0)
            for offset in range(tap_count)
        ],
        axis=1,
    )


def conv_forward(window, seg_window, seg_mine, conv_w):
    row_count = seg_mine.shape[0]
    kernel_len, model_width, group_width = conv_w.shape
    group_count = model_width // group_width
    tap_count = 8

    def advance(running, block_index):
        first_tap = block_index * tap_count
        stacked = tap_rows(window, first_tap, row_count, tap_count, 1)
        linked = tap_rows(seg_window, first_tap, row_count, tap_count, 1) == seg_mine[:, None]
        stacked = jnp.where(linked[:, :, None], stacked, jnp.zeros((), stacked.dtype)).reshape(
            row_count, tap_count, group_count, group_width
        )
        kernel_block = lax.dynamic_slice_in_dim(conv_w, first_tap, tap_count, 0).reshape(
            tap_count, group_count, group_width, group_width
        )
        return (
            running
            + jnp.einsum(
                "tkgc,kgdc->tgd", stacked, kernel_block, preferred_element_type=jnp.float32
            ),
            None,
        )

    start = jnp.zeros((row_count, group_count, group_width), jnp.float32)
    running, unused = lax.scan(advance, start, jnp.arange(kernel_len // tap_count, dtype=jnp.int32))
    return running.reshape(row_count, model_width)


def conv_backward(window, grad_window, seg_window, seg_mine, grad_local, conv_w):
    row_count = seg_mine.shape[0]
    kernel_len, model_width, group_width = conv_w.shape
    group_count = model_width // group_width
    tap_count = 8
    grad_groups = grad_local.reshape(row_count, group_count, group_width)

    def advance(running, block_index):
        first_tap = block_index * tap_count
        stacked = tap_rows(window, first_tap, row_count, tap_count, 1)
        linked = tap_rows(seg_window, first_tap, row_count, tap_count, 1) == seg_mine[:, None]
        stacked = jnp.where(linked[:, :, None], stacked, jnp.zeros((), stacked.dtype)).reshape(
            row_count, tap_count, group_count, group_width
        )
        kernel_block = lax.dynamic_slice_in_dim(conv_w, first_tap, tap_count, 0).reshape(
            tap_count, group_count, group_width, group_width
        )
        weight_part = jnp.einsum(
            "tgd,tkgc->kgdc", grad_groups, stacked, preferred_element_type=jnp.float32
        )
        back_rows = tap_rows(grad_window, kernel_len - first_tap, row_count, tap_count, -1)
        back_linked = (
            tap_rows(seg_window, kernel_len - first_tap, row_count, tap_count, -1)
            == seg_mine[:, None]
        )
        back_rows = jnp.where(
            back_linked[:, :, None], back_rows, jnp.zeros((), back_rows.dtype)
        ).reshape(row_count, tap_count, group_count, group_width)
        running = running + jnp.einsum(
            "tkgd,kgdc->tgc", back_rows, kernel_block, preferred_element_type=jnp.float32
        )
        return (running, weight_part)

    start = jnp.zeros((row_count, group_count, group_width), jnp.float32)
    running, weight_parts = lax.scan(
        advance, start, jnp.arange(kernel_len // tap_count, dtype=jnp.int32)
    )
    return (
        running.reshape(row_count, model_width),
        weight_parts.reshape(kernel_len, model_width, group_width),
    )


def scores_block(query_block, keys_all, seg_block, seg_group, scale):
    scores = (
        jnp.einsum("qhe,khe->hqk", query_block, keys_all, preferred_element_type=jnp.float32)
        * scale
    )
    linked = (seg_block[:, None] == seg_group[None, :])[None]
    return jnp.where(linked, scores, -1e30)


def attend_heads(packed, seg_group):
    group_len, heads_here, triple = packed.shape
    head_dim = triple // 3
    queries = packed[:, :, :head_dim]
    keys_all = packed[:, :, head_dim : 2 * head_dim]
    values_all = packed[:, :, 2 * head_dim :]
    block_len = min(512, group_len)
    scale = head_dim ** (-0.5)

    def one_block(block_index):
        start = block_index * block_len
        query_block = lax.dynamic_slice_in_dim(queries, start, block_len, 0)
        seg_block = lax.dynamic_slice_in_dim(seg_group, start, block_len, 0)
        scores = scores_block(query_block, keys_all, seg_block, seg_group, scale)
        peak = jnp.max(scores, axis=-1, keepdims=True)
        expos = jnp.exp(scores - peak)
        denom = jnp.sum(expos, axis=-1, keepdims=True)
        prob = expos / denom
        context = jnp.einsum(
            "hqk,khe->qhe",
            prob.astype(jnp.bfloat16),
            values_all,
            preferred_element_type=jnp.float32,
        )
        return (context.astype(jnp.bfloat16), jnp.transpose(peak[..., 0] + jnp.log(denom[..., 0])))

    contexts, log_sums = lax.map(one_block, jnp.arange(group_len // block_len, dtype=jnp.int32))
    return (
        contexts.reshape(group_len, heads_here, head_dim),
        log_sums.reshape(group_len, heads_here),
    )


def attend_back(packed, log_sums, grad_context, seg_group):
    group_len, heads_here, triple = packed.shape
    head_dim = triple // 3
    queries = packed[:, :, :head_dim]
    keys_all = packed[:, :, head_dim : 2 * head_dim]
    values_all = packed[:, :, 2 * head_dim :]
    block_len = min(512, group_len)
    scale = head_dim ** (-0.5)

    def advance(carry, block_index):
        grad_keys, grad_values = carry
        start = block_index * block_len
        query_block = lax.dynamic_slice_in_dim(queries, start, block_len, 0)
        seg_block = lax.dynamic_slice_in_dim(seg_group, start, block_len, 0)
        lse_block = lax.dynamic_slice_in_dim(log_sums, start, block_len, 0)
        grad_block = lax.dynamic_slice_in_dim(grad_context, start, block_len, 0)
        scores = scores_block(query_block, keys_all, seg_block, seg_group, scale)
        prob = jnp.exp(scores - jnp.transpose(lse_block)[:, :, None])
        grad_prob = jnp.einsum(
            "qhe,khe->hqk", grad_block, values_all, preferred_element_type=jnp.float32
        )
        inner = jnp.sum(prob * grad_prob, axis=-1, keepdims=True)
        grad_scores = (prob * (grad_prob - inner)).astype(jnp.bfloat16)
        grad_query = (
            jnp.einsum("hqk,khe->qhe", grad_scores, keys_all, preferred_element_type=jnp.float32)
            * scale
        )
        grad_keys = (
            grad_keys
            + jnp.einsum(
                "hqk,qhe->khe", grad_scores, query_block, preferred_element_type=jnp.float32
            )
            * scale
        )
        grad_values = grad_values + jnp.einsum(
            "hqk,qhe->khe",
            prob.astype(jnp.bfloat16),
            grad_block,
            preferred_element_type=jnp.float32,
        )
        return ((grad_keys, grad_values), grad_query)

    zero_heads = jnp.zeros((group_len, heads_here, head_dim), jnp.float32)
    sums, grad_queries = lax.scan(
        advance, (zero_heads, zero_heads), jnp.arange(group_len // block_len, dtype=jnp.int32)
    )
    grad_queries = grad_queries.reshape(group_len, heads_here, head_dim)
    return jnp.concatenate([grad_queries, sums[0], sums[1]], axis=-1).astype(jnp.bfloat16)


def adam_update(weight, grad, first, second, rate, decay):
    first_new = beta_first * first + (1.0 - beta_first) * grad
    second_new = beta_second * second + (1.0 - beta_second) * grad * grad
    first_hat = first_new / (1.0 - beta_first**STEP)
    second_hat = second_new / (1.0 - beta_second**STEP)
    new_weight = weight - rate * (first_hat / (jnp.sqrt(second_hat) + adam_eps) + decay * weight)
    return (new_weight, first_new, second_new)


def shards(
    frames,
    output_grad,
    segment_ids,
    qkv_weight,
    proj_weight,
    up_weight,
    down_weight,
    conv_weight,
    bias_gains,
    ffn_bias,
    qkv_first,
    proj_first,
    up_first,
    down_first,
    conv_first,
    bias_gains_first,
    ffn_bias_first,
    qkv_second,
    proj_second,
    up_second,
    down_second,
    conv_second,
    bias_gains_second,
    ffn_bias_second,
):
    low_type = jnp.bfloat16
    full_qkv, full_proj, full_up, full_down, full_conv, full_vectors, full_ffn = (
        lax.all_gather(qkv_weight.astype(low_type), ("seq", "head"), axis=0, tiled=True),
        lax.all_gather(proj_weight.astype(low_type), ("seq", "head"), axis=0, tiled=True),
        lax.all_gather(up_weight.astype(low_type), ("seq", "head"), axis=0, tiled=True),
        lax.all_gather(down_weight.astype(low_type), ("seq", "head"), axis=0, tiled=True),
        lax.all_gather(conv_weight.astype(low_type), ("seq", "head"), axis=1, tiled=True),
        lax.all_gather(bias_gains.astype(low_type), ("seq", "head"), axis=1, tiled=True),
        lax.all_gather(ffn_bias.astype(low_type), ("seq", "head"), axis=0, tiled=True),
    )
    vectors = full_vectors.astype(jnp.float32)
    row_count = frames.shape[0]
    model_width = frames.shape[1]
    head_groups = lax.axis_size("head")
    heads_each = HEADS // head_groups
    half_kernel = full_conv.shape[0] // 2
    head_index = lax.axis_index("head")
    seg_group = segment_ids[0]
    start_row = head_index * row_count
    padded_seg = jnp.pad(seg_group, (half_kernel, half_kernel), constant_values=-1)
    seg_window = lax.dynamic_slice_in_dim(padded_seg, start_row, row_count + 2 * half_kernel, 0)
    seg_mine = lax.dynamic_slice_in_dim(seg_group, start_row, row_count, 0)
    window = with_halo(frames, (("head", 0),), half_kernel)
    conv_pre = conv_forward(window, seg_window, seg_mine, full_conv) + vectors[0]
    conv_act, conv_act_back = jax.vjp(gelu_exact, conv_pre)
    hidden_one = frames.astype(jnp.float32) + conv_act
    attn_in = hidden_one.astype(low_type)
    zero_part = jnp.zeros((HEADS, HEAD_DIM), jnp.float32)
    qkv_bias = jnp.stack(
        [vectors[1].reshape(HEADS, HEAD_DIM), zero_part, vectors[2].reshape(HEADS, HEAD_DIM)],
        axis=1,
    ).reshape(3 * model_width)
    packed = (
        (jnp.dot(attn_in, full_qkv, preferred_element_type=jnp.float32) + qkv_bias)
        .astype(low_type)
        .reshape(row_count, head_groups, heads_each, 3 * HEAD_DIM)
    )
    packed_part = lax.all_to_all(packed, "head", split_axis=1, concat_axis=0, tiled=True)
    heads_part = packed_part[:, 0]
    context_part, lse_part = attend_heads(heads_part, seg_group)
    context_heads = context_part[:, None]
    log_sums = lse_part[:, None]
    context = lax.all_to_all(
        context_heads, "head", split_axis=0, concat_axis=1, tiled=True
    ).reshape(row_count, model_width)
    attn_out = jnp.dot(context, full_proj, preferred_element_type=jnp.float32) + vectors[3]
    normed_one, norm_one_back = jax.vjp(layer_norm, hidden_one + attn_out, vectors[4], vectors[5])
    ffn_in = normed_one.astype(low_type)
    up_act, up_back = jax.vjp(
        gelu_exact,
        jnp.dot(ffn_in, full_up, preferred_element_type=jnp.float32) + full_ffn.astype(jnp.float32),
    )
    hidden_mid = up_act.astype(low_type)
    hidden_three = (
        normed_one + jnp.dot(hidden_mid, full_down, preferred_element_type=jnp.float32) + vectors[6]
    )
    layer_out_full, norm_two_back = jax.vjp(layer_norm, hidden_three, vectors[7], vectors[8])
    grad_three, grad_gain_two, grad_shift_two = norm_two_back(output_grad.astype(jnp.float32))
    grad_ffn = grad_three.astype(low_type)
    grad_down = jnp.einsum("tf,td->fd", hidden_mid, grad_ffn, preferred_element_type=jnp.float32)
    grad_down_bias = jnp.sum(grad_ffn.astype(jnp.float32), axis=0)
    (grad_up_pre,) = up_back(
        jnp.einsum("td,fd->tf", grad_ffn, full_down, preferred_element_type=jnp.float32)
    )
    grad_up_low = grad_up_pre.astype(low_type)
    grad_up = jnp.einsum("td,tf->df", ffn_in, grad_up_low, preferred_element_type=jnp.float32)
    grad_ffn_bias = jnp.sum(grad_up_low.astype(jnp.float32), axis=0)
    grad_normed = grad_three + jnp.einsum(
        "tf,df->td", grad_up_low, full_up, preferred_element_type=jnp.float32
    )
    grad_two, grad_gain_one, grad_shift_one = norm_one_back(grad_normed)
    grad_attn = grad_two.astype(low_type)
    grad_proj = jnp.einsum("te,td->ed", context, grad_attn, preferred_element_type=jnp.float32)
    grad_proj_bias = jnp.sum(grad_attn.astype(jnp.float32), axis=0)
    grad_context = (
        jnp.einsum("td,ed->te", grad_attn, full_proj, preferred_element_type=jnp.float32)
        .astype(low_type)
        .reshape(row_count, head_groups, heads_each, HEAD_DIM)
    )
    grad_context_heads = lax.all_to_all(
        grad_context, "head", split_axis=1, concat_axis=0, tiled=True
    )
    grad_packed_heads = attend_back(
        packed_part[:, 0], log_sums[:, 0], grad_context_heads[:, 0], seg_group
    )
    grad_packed = lax.all_to_all(
        grad_packed_heads[:, None], "head", split_axis=0, concat_axis=1, tiled=True
    ).reshape(row_count, 3 * model_width)
    grad_qkv = jnp.einsum("td,te->de", attn_in, grad_packed, preferred_element_type=jnp.float32)
    grad_split = jnp.sum(grad_packed.astype(jnp.float32), axis=0).reshape(HEADS, 3, HEAD_DIM)
    grad_query_bias = grad_split[:, 0].reshape(model_width)
    grad_value_bias = grad_split[:, 2].reshape(model_width)
    grad_hidden_one = grad_two + jnp.einsum(
        "te,de->td", grad_packed, full_qkv, preferred_element_type=jnp.float32
    )
    (grad_conv_pre,) = conv_act_back(grad_hidden_one)
    grad_conv_low = grad_conv_pre.astype(low_type)
    grad_conv_bias = jnp.sum(grad_conv_low.astype(jnp.float32), axis=0)
    grad_window = with_halo(grad_conv_low, (("head", 0),), half_kernel)
    grad_frames_conv, grad_conv = conv_backward(
        window, grad_window, seg_window, seg_mine, grad_conv_low, full_conv
    )
    frames_grad = grad_hidden_one + grad_frames_conv
    grad_vectors = jnp.stack(
        [
            grad_conv_bias,
            grad_query_bias,
            grad_value_bias,
            grad_proj_bias,
            grad_gain_one,
            grad_shift_one,
            grad_down_bias,
            grad_gain_two,
            grad_shift_two,
        ],
        axis=0,
    )
    sum_qkv, sum_proj, sum_up, sum_down, sum_conv, sum_vectors, sum_ffn_bias = (
        lax.psum_scatter(grad_qkv, ("seq", "head"), scatter_dimension=0, tiled=True),
        lax.psum_scatter(grad_proj, ("seq", "head"), scatter_dimension=0, tiled=True),
        lax.psum_scatter(grad_up, ("seq", "head"), scatter_dimension=0, tiled=True),
        lax.psum_scatter(grad_down, ("seq", "head"), scatter_dimension=0, tiled=True),
        lax.psum_scatter(grad_conv, ("seq", "head"), scatter_dimension=1, tiled=True),
        lax.psum_scatter(grad_vectors, ("seq", "head"), scatter_dimension=1, tiled=True),
        lax.psum_scatter(grad_ffn_bias, ("seq", "head"), scatter_dimension=0, tiled=True),
    )
    summed = (sum_qkv, sum_proj, sum_up, sum_down, sum_conv, sum_vectors, sum_ffn_bias)
    square_sum = jnp.zeros((), jnp.float32)
    for member in summed:
        square_sum = square_sum + jnp.sum(member * member)
    grad_norm = jnp.sqrt(lax.psum(square_sum, ("seq", "head")))
    factor = jnp.minimum(1.0, clip_bound / grad_norm)
    masters = (qkv_weight, proj_weight, up_weight, down_weight, conv_weight, bias_gains, ffn_bias)
    firsts = (
        qkv_first,
        proj_first,
        up_first,
        down_first,
        conv_first,
        bias_gains_first,
        ffn_bias_first,
    )
    seconds = (
        qkv_second,
        proj_second,
        up_second,
        down_second,
        conv_second,
        bias_gains_second,
        ffn_bias_second,
    )
    news, first_news, second_news = ([], [], [])
    for index in range(7):
        rate = weight_rates[index]
        decay = matrix_decay if index < 5 else 0.0
        new_weight, first_new, second_new = adam_update(
            masters[index], summed[index] * factor, firsts[index], seconds[index], rate, decay
        )
        news.append(new_weight)
        first_news.append(first_new)
        second_news.append(second_new)
    layer_out = layer_out_full.astype(low_type)
    return (
        layer_out,
        frames_grad,
        grad_norm,
        news[0],
        news[1],
        news[2],
        news[3],
        news[4],
        news[5],
        news[6],
        first_news[0],
        first_news[1],
        first_news[2],
        first_news[3],
        first_news[4],
        first_news[5],
        first_news[6],
        second_news[0],
        second_news[1],
        second_news[2],
        second_news[3],
        second_news[4],
        second_news[5],
        second_news[6],
    )


def solution(mesh):
    placed = (
        P(("seq", "head"), None),
        P(("seq", "head"), None),
        P("seq", None),
        P(("seq", "head"), None),
        P(("seq", "head"), None),
        P(("seq", "head"), None),
        P(("seq", "head"), None),
        P(None, ("seq", "head"), None),
        P(None, ("seq", "head")),
        P(("seq", "head")),
        P(("seq", "head"), None),
        P(("seq", "head"), None),
        P(("seq", "head"), None),
        P(("seq", "head"), None),
        P(None, ("seq", "head"), None),
        P(None, ("seq", "head")),
        P(("seq", "head")),
        P(("seq", "head"), None),
        P(("seq", "head"), None),
        P(("seq", "head"), None),
        P(("seq", "head"), None),
        P(None, ("seq", "head"), None),
        P(None, ("seq", "head")),
        P(("seq", "head")),
    )
    return jax.shard_map(
        shards,
        mesh=mesh,
        in_specs=placed,
        out_specs=(
            P(("seq", "head"), None),
            P(("seq", "head"), None),
            P(),
            P(("seq", "head"), None),
            P(("seq", "head"), None),
            P(("seq", "head"), None),
            P(("seq", "head"), None),
            P(None, ("seq", "head"), None),
            P(None, ("seq", "head")),
            P(("seq", "head")),
            P(("seq", "head"), None),
            P(("seq", "head"), None),
            P(("seq", "head"), None),
            P(("seq", "head"), None),
            P(None, ("seq", "head"), None),
            P(None, ("seq", "head")),
            P(("seq", "head")),
            P(("seq", "head"), None),
            P(("seq", "head"), None),
            P(("seq", "head"), None),
            P(("seq", "head"), None),
            P(None, ("seq", "head"), None),
            P(None, ("seq", "head")),
            P(("seq", "head")),
        ),
        check_vma=False,
    )
```

profile of v0, /device:TPU:0, one launch (start us, length us, event | category | flops | bytes accessed | tf_op | source)
XLA Modules:
  0.0 1570.5 jit_solution(5819900087158681230)
XLA Ops:
  18.4 45.9 %all-gather = bf16[32,24,9]{1,2,0:T(8,128)(2,1)S(1)} all-gather(bf16[1,24,9]{1,2,0:T(8,128)(2,1)S(1)} %convert_bitcast_fusion.2), channel_id=1, replica_groups=mesh['seq'=8,'head'=4] {'seq','head'}, dimensions={0}, use_global_device_ids=true | all-gather | bytes 14256 | tf_op jit(solution)/shard_map/all_gather | solution.py:263
  66.4 30.7 %all-gather.7.cloned.1.call-done = bf16[128,768,48]{0,2,1:T(8,128)(2,1)} async-done(((bf16[128,24,48]{0,2,1:T(8,128)(2,1)}), bf16[128,768,48]{0,2,1:T(8,128)(2,1)}) %all-gather.7.cloned.1.call-update) | async-done | bytes 9437200 | tf_op jit(solution)/shard_map/all_gather | solution.py:262
  97.0 14.6 copy.196
  111.6 207.7 %while.58 = (s32[]{:T(128)}, f32[512,16,48]{0,2,1:T(8,128)}, s32[16]{0:T(128)S(1)}, bf16[128,768,48]{1,2,0:T(8,128)(2,1)}, s32[640]{0:T(1024)S(1)}, /*index=5*/s...) while((s32[]{:T(128)}, f32[512,16,48]{0,2,1:T(8,128)}, ...), condition=%wide.region_1.2_spmd.clone, body=%wide.region_0.1_spmd.clone.sunk | while | flops 305926176 | bytes 50227964 | solution.py:82
  342.5 28.6 %all-to-all-done = bf16[512,4,3,192]{0,3,2,1:T(8,128)(2,1)S(1)} async-done(((bf16[512,4,3,192]{0,3,2,1:T(8,128)(2,1)}), bf16[512,4,3,192]{0,3,2,1:T(8,128)(2,1)S(1)}, u32[]{:S(2)}, u32[]{:S(2)}) %all-to-all-start) | async-done | bytes 2359328 | tf_op jit(solution)/shard_map/all_to_all | solution.py:293
  382.0 88.4 %while.57 = (s32[]{:T(128)}, bf16[4,512,3,64]{1,3,2,0:T(8,128)(2,1)}, f32[4,512,3]{1,2,0:T(4,128)S(1)}, s32[4]{0:T(128)S(1)}, s32[2048]{0:T(1024)S(1)}, /*index=...) while((s32[]{:T(128)}, ...), condition=%wide.region_5.6_spmd, body=%wide.region_2.5_spmd.sunk | while | flops 844200448 | bytes 43978956 | solution.py:164
  482.5 44.8 %all-reduce.1 = bf16[3072]{0:T(1024)(128)(2,1)S(1)} all-reduce(bf16[3072]{0:T(1024)(128)(2,1)S(1)} %dynamic-update-slice), channel_id=1, replica_groups=mesh['seq'=8,'head'=4] {'seq','head'}, use_global_device_ids=true, to_apply=%add.1 | all-reduce | flops 3072 | bytes 12288
  538.6 20.8 %multiply_convert_fusion.1 = (bf16[512,3072]{1,0:T(8,128)(2,1)}, f32[512,3072]{1,0:T(8,128)}, f32[512,3072]{1,0:T(8,128)}) fusion(f32[3072]{0:T(1024)S(1)} %convert_element_type.113, bf16[768,3072]{1,0:T(8,128)(2,1)} %all-gather.13.cloned.1.call-done, f32[512,768]{1,0:T(8,128)} %copy-done.19, f32[768]{0:T(1024)S(1)} %copy-done.69, f32[768]{0:T(1024)S(1)} %copy-done.59, ...), kind=kOutput, calls=%fused_computation.123 | convolution fusion | flops 2521694208 | bytes 22042624 | tf_op jit(solution)/shard_map/dot_general | solution.py:306
  570.2 9.3 convert_reduce_fusion
  608.4 126.4 %while.59 = (s32[]{:T(128)}, f32[2048,3,64]{0,2,1:T(8,128)}, f32[2048,3,64]{0,2,1:T(8,128)}, bf16[4,512,3,64]{1,3,2,0:T(8,128)(2,1)}, s32[4]{0:T(128)S(1)}, /*in...) while((s32[]{:T(128)}, f32[2048,3,64]{0,2,1:T(8,128)}, ...), condition=%wide.region_16.17_spmd.clone, body=%wide.region_14.16_spmd.clone.sunk | while | flops 2063563264 | bytes 156688880 | solution.py:214
  743.8 53.9 %all_to_all.60 = bf16[2048,1,3,192]{3,2,1,0:T(4,128)(2,1)} all-to-all(bf16[2048,1,3,192]{3,2,1,0:T(4,128)(2,1)} %copy.210), channel_id=1, replica_groups=mesh['seq'=8,'head'=4] {'head'}, dimensions={0} | all-to-all | bytes 4718592 | tf_op jit(solution)/shard_map/all_to_all | solution.py:341
  843.0 393.7 %while.60 = (s32[]{:T(128)}, f32[512,16,48]{0,2,1:T(8,128)}, f32[16,8,16,48,48]{3,2,4,1,0:T(8,128)}, s32[16]{0:T(128)S(1)}, bf16[128,768,48]{1,2,0:T(8,128)(2,1)...) while((s32[]{:T(128)}, f32[512,16,48]{0,2,1:T(8,128)}, ...), condition=%wide.region_18.19_spmd.clone, body=%wide.region_17.18_spmd.clone.sunk | while | flops 611065920 | bytes 93572480 | solution.py:120
  848.5 8.3 constant_dynamic-slice_fusion.33
  873.0 8.3 constant_dynamic-slice_fusion.33
  897.6 8.3 constant_dynamic-slice_fusion.33
  946.8 8.3 constant_dynamic-slice_fusion.33
  1045.2 8.3 constant_dynamic-slice_fusion.33
  1069.7 8.3 constant_dynamic-slice_fusion.33
  1217.7 8.3 constant_dynamic-slice_fusion.33
  1236.7 40.1 %reshape.820 = f32[128,768,48]{1,2,0:T(8,128)} reshape(f32[16,8,16,48,48]{3,2,4,1,0:T(8,128)} %get-tuple-element.457) | data formatting | bytes 37748736 | tf_op jit(solution)/shard_map/reshape | solution.py:125
  1276.8 19.2 %copy.218 = f32[128,768,48]{0,2,1:T(8,128)} copy(f32[128,768,48]{1,2,0:T(8,128)} %reshape.820) | data formatting | bytes 37748736 | tf_op jit(solution)/shard_map/reshape | solution.py:125
  1299.4 43.4 %all-reduce.4 = (f32[9,768]{1,0:T(8,128)S(1)}, f32[3072]{0:T(1024)S(1)}) all-reduce(f32[9,768]{1,0:T(8,128)S(1)} %stack.185, f32[3072]{0:T(1024)S(1)} %copy-done.61), channel_id=7, replica_groups=mesh['seq'=8,'head'=4] {'seq','head'}, use_global_device_ids=true, to_apply=%region_37.38.clone | all-reduce | flops 9984 | bytes 79872
  1355.4 149.4 %reduce-scatter.15.cloned.1.call-done = f32[128,24,48]{0,2,1:T(8,128)} async-done(((f32[128,768,48]{0,2,1:T(8,128)}), f32[128,24,48]{0,2,1:T(8,128)}) %reduce-scatter.15.cloned.1.call-update) | async-done | bytes 589840 | tf_op jit(solution)/shard_map/reduce_scatter | solution.py:378
  1510.0 39.1 %psum.7 = f32[]{:T(128)} all-reduce(f32[]{:T(128)S(6)} %add.799), channel_id=1, replica_groups=mesh['seq'=8,'head'=4] {'seq','head'}, use_global_device_ids=true, to_apply=%region_42.43 | all-reduce | flops 1 | bytes 8 | tf_op jit(solution)/shard_map/psum | solution.py:386
  (1310 shorter events, 916.4 us)
Async XLA Ops:
  7.2 89.8 %all-gather.7.cloned.1.call-start = ((), (), s32[]{:S(2)}) async-start(), calls=%async_computation.9 | async-start | bytes 9732096 | tf_op jit(solution)/shard_map/all_gather | solution.py:262
  9.2 318.4 %all-gather.9.cloned.1.call-start = ((), (), s32[]{:S(2)}) async-start(), calls=%async_computation.10 | async-start | bytes 3649536 | tf_op jit(solution)/shard_map/all_gather | solution.py:258
  10.8 523.3 %all-gather.11.cloned.1.call-start = ((), (), s32[]{:S(2)}) async-start(), calls=%async_computation.11 | async-start | bytes 1216512 | tf_op jit(solution)/shard_map/all_gather | solution.py:259
  12.4 526.1 %all-gather.13.cloned.1.call-start = ((), (), s32[]{:S(2)}) async-start(), calls=%async_computation.12 | async-start | bytes 4866048 | tf_op jit(solution)/shard_map/all_gather | solution.py:260
  14.0 51.8 %collective-permute-start = (bf16[64,768]{0,1:T(8,128)(2,1)S(1)}, bf16[64,768]{0,1:T(8,128)(2,1)S(1)}, u32[]{:S(2)}, u32[]{:S(2)}) collective-permute-start(bf16[64,768]{0,1:T(8,128)(2,1)S(1)} %get-tuple-element.900), channel_id=1, source_target_pairs={{0,1},{1,2},{2,3},{4,5},{5,6},{6,7},{8,9},{9,10},{10,11},{12,13},{... | collective-permute-start | bytes 294920 | tf_op jit(solution)/shard_map/ppermute | solution.py:28
  16.4 49.4 %collective-permute-start.1 = (bf16[64,768]{0,1:T(8,128)(2,1)S(1)}, bf16[64,768]{0,1:T(8,128)(2,1)S(1)}, u32[]{:S(2)}, u32[]{:S(2)}) collective-permute-start(bf16[64,768]{0,1:T(8,128)(2,1)S(1)} %get-tuple-element.901), channel_id=1, source_target_pairs={{1,0},{2,1},{3,2},{5,4},{6,5},{7,6},{9,8},{10,9},{11,10},{13,12},{... | collective-permute-start | bytes 294920 | tf_op jit(solution)/shard_map/ppermute | solution.py:30
  65.3 256.3 %copy-start.52 = (f32[768]{0:T(1024)}, f32[768]{0:T(1024)S(1)}, u32[]{:S(2)}) copy-start(f32[768]{0:T(1024)S(1)} %get-tuple-element.714) | copy-start | bytes 9220
  337.8 33.3 %all-to-all-start = ((bf16[512,4,3,192]{0,3,2,1:T(8,128)(2,1)}), bf16[512,4,3,192]{0,3,2,1:T(8,128)(2,1)S(1)}, u32[]{:S(2)}, u32[]{:S(2)}) async-start(bf16[512,4,3,192]{0,3,2,1:T(8,128)(2,1)} %bitcast.345), calls=%async_computation | async-start | bytes 4718592 | tf_op jit(solution)/shard_map/all_to_all | solution.py:293
  341.6 217.8 %all-gather.15.cloned.1.call-start = ((), (), s32[]{:S(2)}) async-start(), calls=%async_computation.13 | async-start | bytes 4866048 | tf_op jit(solution)/shard_map/all_gather | solution.py:261
  478.7 48.6 %all-to-all-start.1 = ((bf16[4,2,49152]{2,1,0:T(2,128)(2,1)}), bf16[4,2,49152]{2,1,0:T(2,128)(2,1)S(1)}, u32[]{:S(2)}, u32[]{:S(2)}) async-start(bf16[4,2,49152]{2,1,0:T(2,128)(2,1)} %reshape.850), calls=%async_computation.1 | async-start | bytes 1572864 | tf_op jit(solution)/shard_map/all_to_all | solution.py:298
  588.8 15.2 all-to-all-start.2
  592.4 753.9 %reduce-scatter.9.cloned.1.call-start = ((), (), s32[]{:S(2)}) async-start(), calls=%async_computation.15 | async-start | bytes 2433024 | tf_op jit(solution)/shard_map/reduce_scatter | solution.py:375
  596.1 751.7 %reduce-scatter.7.cloned.1.call-start = ((), (), s32[]{:S(2)}) async-start(), calls=%async_computation.14 | async-start | bytes 7299072 | tf_op jit(solution)/shard_map/reduce_scatter | solution.py:374
  812.4 538.3 %reduce-scatter.11.cloned.1.call-start = ((), (), s32[]{:S(2)}) async-start(), calls=%async_computation.16 | async-start | bytes 9732096 | tf_op jit(solution)/shard_map/reduce_scatter | solution.py:376
  821.0 532.1 %reduce-scatter.13.cloned.1.call-start = ((), (), s32[]{:S(2)}) async-start(), calls=%async_computation.17 | async-start | bytes 9732096 | tf_op jit(solution)/shard_map/reduce_scatter | solution.py:377
  831.0 9.1 collective-permute-start.2
  832.4 7.7 collective-permute-start.3
  838.9 665.9 %reduce-scatter.15.cloned.1.call-start = ((), (), s32[]{:S(2)}) async-start(), calls=%async_computation.18 | async-start | bytes 19464192 | tf_op jit(solution)/shard_map/reduce_scatter | solution.py:378
  1298.8 209.8 %copy-start.32 = (f32[512,768]{1,0:T(8,128)S(1)}, f32[512,768]{1,0:T(8,128)}, u32[]{:S(2)}) copy-start(f32[512,768]{1,0:T(8,128)} %get-tuple-element.908) | copy-start | bytes 4718596
  1346.2 203.7 %copy-start.49 = (f32[9,24]{1,0:T(8,128)S(1)}, f32[9,24]{1,0:T(8,128)}, u32[]{:S(2)}) copy-start(f32[9,24]{1,0:T(8,128)} %param.40) | copy-start | bytes 2596
  1346.2 205.1 %copy-start.77 = (f32[96]{0:T(128)S(1)}, f32[96]{0:T(128)}, u32[]{:S(2)}) copy-start(f32[96]{0:T(128)} %param.41) | copy-start | bytes 1156
  1346.2 205.1 %copy-start.78 = (f32[96]{0:T(128)S(1)}, f32[96]{0:T(128)}, u32[]{:S(2)}) copy-start(f32[96]{0:T(128)} %param.48) | copy-start | bytes 1156
  1346.2 205.1 %copy-start.79 = (f32[96]{0:T(128)S(1)}, f32[96]{0:T(128)}, u32[]{:S(2)}) copy-start(f32[96]{0:T(128)} %param.55) | copy-start | bytes 1156
  1346.2 206.4 %copy-start.44 = (f32[24,768]{1,0:T(8,128)S(1)}, f32[24,768]{1,0:T(8,128)}, u32[]{:S(2)}) copy-start(f32[24,768]{1,0:T(8,128)} %param.36) | copy-start | bytes 221188
  (194 other events, 1756.6 us)
Sparse Core Ops, SparseCore 0:
  11.5 85.4 all-gather.6
  100.5 58.7 all-gather.8
  162.8 52.8 all-gather.10
  219.1 62.5 all-gather.12
  345.6 63.7 all-gather.14
  598.1 99.4 reduce-scatter.8
  812.5 117.9 reduce-scatter.6
  936.5 134.7 reduce-scatter.10
  1078.2 134.6 reduce-scatter.12
  1296.2 208.6 reduce-scatter.14
where the time goes:
time: 1580 us; the launch traced here: 1570 us
  local copies, waits for them, and re-layouts  643 us (41%)
  matrix products  307 us (19%)
  blocking collectives  227 us (14%)
  waiting for transfers between devices  217 us (14%)
  other arithmetic  103 us (7%)
  loops' own time  34.3 us (2%)
  between operations  21.9 us (1%)
  starting transfers between devices  17.7 us (1%)
    dynamic_slice x64, local copies, waits for them, and re-layouts, tap_rows(): lax.dynamic_slice_in_dim(source, first_tap + direction * offset, row_coun...  200 us
    reduce_scatter x1, waiting for transfers between devices, shards(): lax.psum_scatter(grad_conv, ('seq', 'head'), scatter_dimension=1, tiled=T...  149 us
    while x592, local copies, waits for them, and re-layouts  101 us
    unnamed x2, blocking collectives  88.2 us
    reshape x32, local copies, waits for them, and re-layouts, advance(): lax.dynamic_slice_in_dim(conv_w, first_tap, tap_count, 0)  76.1 us
    reshape x2, local copies, waits for them, and re-layouts, conv_backward(): weight_parts.reshape(kernel_len, model_width, group_width)  59.3 us
    dynamic_update_slice x16, local copies, waits for them, and re-layouts, conv_backward(): lax.scan(advance, start, jnp.arange(kernel_len // tap_count, dtype=jnp.in...  56.1 us
    all_to_all x1, blocking collectives, shards(): lax.all_to_all(grad_packed_heads[:, None], 'head', split_axis=0, concat_a...  53.9 us
  transfers between devices with their start and end apart: 17, of which 4 were waited for; matrix products, arithmetic and copies ran while one was open for 58% of the time, Pallas kernels for 0%

commit v1 on v0

v1 whole, which is shorter than its diff:
```python
import functools

import jax
import jax.numpy as jnp
from jax import lax
from jax.experimental import pallas as pl
from jax.experimental.pallas import tpu as pltpu
from jax.sharding import PartitionSpec as P

HEADS = 12
HEAD_DIM = 64
STEP = 10


norm_eps = 1e-05
beta_first = 0.9
beta_second = 0.999
adam_eps = 1e-08
weight_rates = (0.02, 0.1, 0.02, 0.02, 0.02, 0.2, 0.2)
matrix_decay = 0.01
clip_bound = 1.0


def with_halo(cells, sides, width):
    for axis, dim in sides:
        count = lax.axis_size(axis)
        ends = count - 1
        head = lax.slice_in_dim(cells, 0, width, axis=dim)
        tail = lax.slice_in_dim(cells, cells.shape[dim] - width, cells.shape[dim], axis=dim)
        cells = jnp.concatenate(
            [
                lax.ppermute(tail, axis, [(i, (i + 1) % count) for i in range(ends)]),
                cells,
                lax.ppermute(head, axis, [((i + 1) % count, i) for i in range(ends)]),
            ],
            axis=dim,
        )
    return cells


def layer_norm(values, scale_gain, shift_row):
    center = values - jnp.mean(values, axis=-1, keepdims=True)
    spread = jnp.mean(center * center, axis=-1, keepdims=True)
    return center * lax.rsqrt(spread + norm_eps) * scale_gain + shift_row


def gelu_exact(values):
    return jax.nn.gelu(values, approximate=False)


def adam_update(weight, grad, first, second, rate, decay):
    first_new = beta_first * first + (1.0 - beta_first) * grad
    second_new = beta_second * second + (1.0 - beta_second) * grad * grad
    first_hat = first_new / (1.0 - beta_first**STEP)
    second_hat = second_new / (1.0 - beta_second**STEP)
    new_weight = weight - rate * (first_hat / (jnp.sqrt(second_hat) + adam_eps) + decay * weight)
    return (new_weight, first_new, second_new)


HALF = 64
OWN = 512
WIN = OWN + 2 * HALF
EXT = WIN + HALF
ZROWS = OWN + HALF + 8
CGW = 48

def up(v, n):
    return pltpu.roll(v, v.shape[0] - n, 0)

def down(v, n):
    return pltpu.roll(v, n, 0)

def left(v, n):
    return pltpu.roll(v, v.shape[1] - n, 1)

def right(v, n):
    return pltpu.roll(v, n, 1)

def place(g):
    tile = jnp.minimum(g * CGW // 128, 4)
    return pl.ds(pl.multiple_of(tile * 128, 128), 256), g * CGW - tile * 128

def take_group(ref, g):
    lanes, rem = place(g)
    wide = ref[:, lanes].astype(jnp.float32)
    return pltpu.roll(wide, 256 - rem, 1)[:, :128]

def gapped(xg, cut):
    row = lax.broadcasted_iota(jnp.int32, (EXT, 128), 0)
    zero = jnp.zeros((HALF, 128), jnp.float32)
    before = jnp.concatenate([xg, zero], axis=0)
    after = jnp.concatenate([zero, xg], axis=0)
    return jnp.where(row < cut, before, jnp.where(row < cut + HALF, 0.0, after))

def im2col(xg, rows):
    lane = lax.broadcasted_iota(jnp.int32, (rows, 128), 1)
    turned = {off: (right(xg, off) if off else xg) for off in range(0, 128, 16)}
    cols = []
    for v in range(6):
        acc = None
        for r in range(16):
            lo = CGW * r
            if lo + CGW <= 128 * v or lo >= 128 * (v + 1):
                continue
            piece = turned[lo % 128][8 * r : 8 * r + rows, :]
            acc = piece if acc is None else jnp.where(lane >= lo - 128 * v, piece, acc)
        cols.append(acc.astype(jnp.bfloat16))
    return jnp.concatenate(cols, axis=1)

def pad_weights(w_ref, wp_ref):
    for h in range(2):
        for a in range(8):
            wp_ref[pl.ds(h * 256 + a * 32, 24), :] = w_ref[0, h, a]

def fold_out(z):
    lane = lax.broadcasted_iota(jnp.int32, (ZROWS, 128), 1)
    u = []
    for h in range(2):
        t = z[:, h * 256 : h * 256 + 128] + up(z[:, h * 256 + 128 : h * 256 + 256], 4)
        u.append(t + left(up(t, 2), 64))
    v = jnp.where(lane < 64, u[0], right(u[1], 64))
    o = v + left(up(v, 1), 32)
    return jnp.where(lane < 24, o, left(o, 40))[: OWN + HALF]

def pick_own(o, cut):
    row = lax.broadcasted_iota(jnp.int32, (OWN, 128), 0) + HALF
    return jnp.where(row < cut, o[:OWN], o[HALF : OWN + HALF])

def put_group(out_ref, g, o):
    lanes, rem = place(g)
    lane = lax.broadcasted_iota(jnp.int32, (OWN, 128), 1)
    o = jnp.where(lane < CGW, o, 0.0)
    wide = jnp.concatenate([o, jnp.zeros((OWN, 128), jnp.float32)], axis=1)
    out_ref[:, lanes] += pltpu.roll(wide, rem, 1)

def conv_fwd_kernel(cut_ref, x_ref, w_ref, out_ref, wp_ref):
    g = pl.program_id(0)
    cut = cut_ref[0]
    @pl.when(g == 0)
    def _():
        wp_ref[...] = jnp.zeros_like(wp_ref)
        out_ref[...] = jnp.zeros_like(out_ref)
    pad_weights(w_ref, wp_ref)
    cols = im2col(gapped(take_group(x_ref, g), cut), ZROWS)
    z = lax.dot_general(cols, wp_ref[...], (((1,), (1,)), ((), ())), preferred_element_type=jnp.float32)
    put_group(out_ref, g, pick_own(fold_out(z), cut))

def conv_fwd(cut, xw, w):
    return pl.pallas_call(
        conv_fwd_kernel,
        grid_spec=pltpu.PrefetchScalarGridSpec(
            num_scalar_prefetch=1, grid=(16,),
            in_specs=[pl.BlockSpec((WIN, 768), lambda g, c: (0, 0)),
                      pl.BlockSpec((1, 2, 8, 24, 768), lambda g, c: (g, 0, 0, 0, 0))],
            out_specs=pl.BlockSpec((OWN, 768), lambda g, c: (0, 0)),
            scratch_shapes=[pltpu.VMEM((512, 768), jnp.bfloat16)]),
        out_shape=jax.ShapeDtypeStruct((OWN, 768), jnp.float32),
        compiler_params=pltpu.CompilerParams(vmem_limit_bytes=50 * 2**20),
        cost_estimate=pl.CostEstimate(flops=2 * 16 * 584 * 768 * 512, bytes_accessed=12_000_000, transcendentals=0),
    )(cut, xw, w)

def taps_of(gg):
    lane = lax.broadcasted_iota(jnp.int32, (EXT, 128), 1)
    low = jnp.where(lane < 24, gg, 0.0)
    high = jnp.where((lane >= 64) & (lane < 88), right(gg, 40), 0.0)
    s = low + high
    q = s + right(down(s, 1), 32)
    q2 = down(q, 2)
    parts = []
    for h in range(2):
        if h == 0:
            r = jnp.where(lane < 64, q, right(q2, 64))
        else:
            r = jnp.where(lane < 64, right(q, 64), q2)
        parts += [r, down(r, 4)]
    return jnp.concatenate([p.astype(jnp.bfloat16) for p in parts], axis=1)

def fold_back(z):
    n = OWN + HALF
    lane = lax.broadcasted_iota(jnp.int32, (n, 128), 1)
    a = [z[HALF:, 128 * i : 128 * i + 128] + z[: EXT - HALF, 384 + 128 * i : 512 + 128 * i] for i in range(3)]
    acc = None
    for r in range(8):
        lo = CGW * r
        first = HALF - 8 * r
        tile, off = lo // 128, lo % 128
        piece = a[tile][first : first + n]
        if off:
            piece = left(piece, off)
        if off + CGW > 128:
            piece = jnp.where(lane < 128 - off, piece, right(a[tile + 1][first : first + n], 128 - off))
        acc = piece if acc is None else acc + piece
    return acc

def conv_bwd_kernel(cut_ref, x_ref, g_ref, w_ref, dx_ref, dw_ref, wp_ref):
    g = pl.program_id(0)
    cut = cut_ref[0]
    @pl.when(g == 0)
    def _():
        wp_ref[...] = jnp.zeros_like(wp_ref)
        dx_ref[...] = jnp.zeros_like(dx_ref)
    pad_weights(w_ref, wp_ref)
    taps = taps_of(gapped(take_group(g_ref, g), cut))
    z = jnp.dot(taps, wp_ref[...], preferred_element_type=jnp.float32)
    put_group(dx_ref, g, pick_own(fold_back(z), cut))
    cols = im2col(gapped(take_group(x_ref, g), cut), ZROWS)
    row = lax.broadcasted_iota(jnp.int32, (ZROWS, 512), 0) + HALF
    begin = jnp.where(cut <= HALF, 2 * HALF, HALF)
    end = jnp.where(cut_ref[1] > 0, EXT, jnp.where(cut <= HALF + OWN, OWN + 2 * HALF, OWN + HALF))
    own = jnp.where((row >= begin) & (row < end), taps[HALF : HALF + ZROWS].astype(jnp.float32), 0.0).astype(jnp.bfloat16)
    dw = lax.dot_general(own, cols, (((0,), (0,)), ((), ())), preferred_element_type=jnp.float32)
    for h in range(2):
        for a in range(8):
            dw_ref[0, h, a] = dw[h * 256 + a * 32 : h * 256 + a * 32 + 24].astype(dw_ref.dtype)

def conv_bwd(cut, xw, gw, w, dtype=jnp.bfloat16):
    return pl.pallas_call(
        conv_bwd_kernel,
        grid_spec=pltpu.PrefetchScalarGridSpec(
            num_scalar_prefetch=1, grid=(16,),
            in_specs=[pl.BlockSpec((WIN, 768), lambda g, c: (0, 0)),
                      pl.BlockSpec((WIN, 768), lambda g, c: (0, 0)),
                      pl.BlockSpec((1, 2, 8, 24, 768), lambda g, c: (g, 0, 0, 0, 0))],
            out_specs=[pl.BlockSpec((OWN, 768), lambda g, c: (0, 0)),
                       pl.BlockSpec((1, 2, 8, 24, 768), lambda g, c: (g, 0, 0, 0, 0))],
            scratch_shapes=[pltpu.VMEM((512, 768), jnp.bfloat16)]),
        out_shape=[jax.ShapeDtypeStruct((OWN, 768), jnp.float32), jax.ShapeDtypeStruct((16, 2, 8, 24, 768), dtype)],
        compiler_params=pltpu.CompilerParams(vmem_limit_bytes=50 * 2**20),
        cost_estimate=pl.CostEstimate(flops=4 * 16 * 640 * 768 * 512, bytes_accessed=22_000_000, transcendentals=0),
    )(cut, xw, gw, w)


QT = 256
FAR = -1e30

def fill_keys(seg_ref, blocks, kq_ref, q_ref):
    n = seg_ref.shape[1]
    seg = seg_ref[...]
    row = lax.broadcasted_iota(jnp.int32, (64, n), 0)
    mark = jnp.where(row < 2, jnp.where(seg == row, 1.0, 0.0), 0.0)
    push = jnp.where(row < 2, jnp.where(seg == row, 0.0, FAR), 0.0)
    keys = jnp.concatenate([b[64:128, :] for b in blocks], axis=1).astype(jnp.float32)
    kq_ref[...] = jnp.transpose(jnp.concatenate([keys, mark], axis=0)).astype(jnp.bfloat16)
    queries = jnp.concatenate([b[0:64, :] for b in blocks], axis=1).astype(jnp.float32) * 0.125
    q_ref[...] = jnp.concatenate([queries, push], axis=0).astype(jnp.bfloat16)

def attn_fwd_kernel(seg_ref, b0, b1, b2, b3, c0, c1, c2, c3, lse_ref, o_ref, k_s, q_s, v_s):
    blocks = (b0, b1, b2, b3)
    n = seg_ref.shape[1]
    size = b0.shape[1]
    fill_keys(seg_ref, blocks, k_s, q_s)
    v_s[...] = jnp.concatenate([b[128:192, :] for b in blocks], axis=1)

    def tile(i, unused):
        at = pl.ds(pl.multiple_of(i * QT, QT), QT)
        s = jnp.dot(k_s[...], q_s[:, at], preferred_element_type=jnp.float32)
        peak = jnp.max(s, axis=0, keepdims=True)
        e = jnp.exp(s - peak)
        denom = jnp.sum(e, axis=0, keepdims=True)
        p = (e * (1.0 / denom)).astype(jnp.bfloat16)
        o_ref[0, :, at] = jnp.dot(v_s[...], p, preferred_element_type=jnp.float32)
        lse_ref[0, :, at] = peak + jnp.log(denom)
        return unused

    lax.fori_loop(0, n // QT, tile, 0)
    for j, c in enumerate((c0, c1, c2, c3)):
        c[...] = o_ref[0, :, j * size : (j + 1) * size].astype(jnp.bfloat16)

def attn_fwd(seg, blocks):
    size = blocks[0].shape[1]
    n = 4 * size
    heads = blocks[0].shape[0] // 192
    return pl.pallas_call(
        attn_fwd_kernel,
        grid=(heads,),
        in_specs=[pl.BlockSpec((1, n), lambda h: (0, 0))] + [pl.BlockSpec((192, size), lambda h: (h, 0))] * 4,
        out_specs=[pl.BlockSpec((64, size), lambda h: (h, 0))] * 4
        + [pl.BlockSpec((1, 1, n), lambda h: (h, 0, 0)), pl.BlockSpec((1, 64, n), lambda h: (h, 0, 0))],
        out_shape=[jax.ShapeDtypeStruct((heads * 64, size), jnp.bfloat16)] * 4
        + [jax.ShapeDtypeStruct((heads, 1, n), jnp.float32), jax.ShapeDtypeStruct((heads, 64, n), jnp.float32)],
        scratch_shapes=[pltpu.VMEM((n, 128), jnp.bfloat16), pltpu.VMEM((128, n), jnp.bfloat16), pltpu.VMEM((64, n), jnp.bfloat16)],
        compiler_params=pltpu.CompilerParams(vmem_limit_bytes=50 * 2**20),
        cost_estimate=pl.CostEstimate(flops=heads * n * n * 256, bytes_accessed=6_000_000, transcendentals=heads * n * n),
    )(seg, *blocks)

def attn_bwd_kernel(seg_ref, b0, b1, b2, b3, d0, d1, d2, d3, lse_ref, o_ref, g0, g1, g2, g3, k_s, q_s, v_s, kt_s, do_s, dk_s, dv_s, dq_s):
    blocks = (b0, b1, b2, b3)
    n = seg_ref.shape[1]
    size = b0.shape[1]
    fill_keys(seg_ref, blocks, k_s, q_s)
    v_s[...] = jnp.transpose(jnp.concatenate([b[128:192, :] for b in blocks], axis=1).astype(jnp.float32)).astype(jnp.bfloat16)
    kt_s[...] = jnp.concatenate([b[64:128, :] for b in blocks], axis=1)
    do_s[...] = jnp.concatenate([d[...] for d in (d0, d1, d2, d3)], axis=1)
    dk_s[...] = jnp.zeros_like(dk_s)
    dv_s[...] = jnp.zeros_like(dv_s)

    def tile(i, unused):
        at = pl.ds(pl.multiple_of(i * QT, QT), QT)
        q = q_s[:, at]
        do = do_s[:, at]
        delta = jnp.sum(do.astype(jnp.float32) * o_ref[0, :, at], axis=0, keepdims=True)
        s = jnp.dot(k_s[...], q, preferred_element_type=jnp.float32)
        p = jnp.exp(s - lse_ref[0, :, at])
        dp = jnp.dot(v_s[...], do, preferred_element_type=jnp.float32)
        ds = (p * (dp - delta)).astype(jnp.bfloat16)
        p = p.astype(jnp.bfloat16)
        nt = (((1,), (1,)), ((), ()))
        dv_s[...] += lax.dot_general(do, p, nt, preferred_element_type=jnp.float32)
        dk_s[...] += lax.dot_general(q[:64], ds, nt, preferred_element_type=jnp.float32)
        dq_s[:, at] = jnp.dot(kt_s[...], ds, preferred_element_type=jnp.float32) * 0.125
        return unused

    lax.fori_loop(0, n // QT, tile, 0)
    for j, g in enumerate((g0, g1, g2, g3)):
        span = slice(j * size, (j + 1) * size)
        g[0:64, :] = dq_s[:, span].astype(jnp.bfloat16)
        g[64:128, :] = dk_s[:, span].astype(jnp.bfloat16)
        g[128:192, :] = dv_s[:, span].astype(jnp.bfloat16)

def attn_bwd(seg, blocks, grads, lse, o):
    size = blocks[0].shape[1]
    n = 4 * size
    heads = blocks[0].shape[0] // 192
    return pl.pallas_call(
        attn_bwd_kernel,
        grid=(heads,),
        in_specs=[pl.BlockSpec((1, n), lambda h: (0, 0))] + [pl.BlockSpec((192, size), lambda h: (h, 0))] * 4
        + [pl.BlockSpec((64, size), lambda h: (h, 0))] * 4
        + [pl.BlockSpec((1, 1, n), lambda h: (h, 0, 0)), pl.BlockSpec((1, 64, n), lambda h: (h, 0, 0))],
        out_specs=[pl.BlockSpec((192, size), lambda h: (h, 0))] * 4,
        out_shape=[jax.ShapeDtypeStruct((heads * 192, size), jnp.bfloat16)] * 4,
        scratch_shapes=[pltpu.VMEM((n, 128), jnp.bfloat16), pltpu.VMEM((128, n), jnp.bfloat16), pltpu.VMEM((n, 64), jnp.bfloat16),
                        pltpu.VMEM((64, n), jnp.bfloat16), pltpu.VMEM((64, n), jnp.bfloat16),
                        pltpu.VMEM((64, n), jnp.float32), pltpu.VMEM((64, n), jnp.float32), pltpu.VMEM((64, n), jnp.float32)],
        compiler_params=pltpu.CompilerParams(vmem_limit_bytes=50 * 2**20),
        cost_estimate=pl.CostEstimate(flops=heads * n * n * 640, bytes_accessed=10_000_000, transcendentals=heads * n * n),
    )(seg, *blocks, *grads, lse, o)


MESH = pl.DeviceIdType.MESH

def spot():
    seq, head = lax.axis_index("seq"), lax.axis_index("head")
    return seq // 2, seq % 2, head // 2, head % 2

def device(z, x, y, c):
    return {"seq": z * 2 + x, "head": y * 2 + c}

def greet():
    z, x, y, c = spot()
    barrier = pltpu.get_barrier_semaphore()
    for where in (device(z, x, y, 1 - c), device(z, x, 1 - y, c), device(z, 1 - x, y, c)):
        pl.semaphore_signal(barrier, inc=1, device_id=where, device_id_type=MESH)

    @pl.when(z > 0)
    def _():
        pl.semaphore_signal(barrier, inc=1, device_id=device(z - 1, x, y, c), device_id_type=MESH)

    @pl.when(z < 3)
    def _():
        pl.semaphore_signal(barrier, inc=1, device_id=device(z + 1, x, y, c), device_id_type=MESH)

    pl.semaphore_wait(barrier, jnp.where((z == 0) | (z == 3), 4, 5))

class Spread:
    def __init__(self, own, whole, cut, x_first, send, recv):
        self.own, self.whole, self.cut, self.x_first, self.send, self.recv = own, whole, cut, x_first, send, recv

    def block(self, *lead):
        return self.whole.at[tuple(lead) + self.cut]

    def copy(self, src, dst, n, to):
        return pltpu.make_async_remote_copy(
            src_ref=src, dst_ref=dst, send_sem=self.send.at[n], recv_sem=self.recv.at[n], device_id=to, device_id_type=MESH
        )

    def up(self, k):
        z, x, y, c = spot()
        ref = self.block(z - (k - 1), x, y, c)
        src = self.own.at[self.cut] if k == 1 else ref
        return (z < 3) & (z >= k - 1), self.copy(src, ref, k - 1, device(z + 1, x, y, c))

    def up_landed(self, k):
        z, x, y, c = spot()
        ref = self.block(z - k, x, y, c)
        return z >= k, self.copy(ref, ref, k - 1, device(z, x, y, 1 - c))

    def down(self, k):
        z, x, y, c = spot()
        ref = self.block(z + (k - 1), x, y, c)
        src = self.own.at[self.cut] if k == 1 else ref
        return (z > 0) & (z + k - 1 <= 3), self.copy(src, ref, 2 + k, device(z - 1, x, y, c))

    def down_landed(self, k):
        z, x, y, c = spot()
        ref = self.block(z + k, x, y, c)
        return z + k <= 3, self.copy(ref, ref, 2 + k, device(z, x, y, 1 - c))

    def side(self, which):
        z, x, y, c = spot()
        if which == 2:
            return self.copy(self.block(slice(None), slice(None), slice(None), c), self.block(slice(None), slice(None), slice(None), c), 8, device(z, x, y, 1 - c)), None
        over_x = self.x_first == (which == 0)
        if which == 0:
            mine = self.block(slice(None), x, y, c)
        elif over_x:
            mine = self.block(slice(None), x, slice(None), c)
        else:
            mine = self.block(slice(None), slice(None), y, c)
        to = device(z, 1 - x, y, c) if over_x else device(z, x, 1 - y, c)
        return self.copy(mine, mine, 6 + which, to), None

    def stage(self, n):
        if n == 0:
            z, x, y, c = spot()
            self.local = pltpu.make_async_copy(self.own.at[self.cut], self.block(z, x, y, c), self.recv.at[9])
            self.local.start()
            for ok, copy in (self.up(1), self.down(1)):
                pl.when(ok)(copy.start)
        elif n in (1, 2):
            for landed, onward in ((self.up_landed, self.up), (self.down_landed, self.down)):
                ok, copy = landed(n)
                pl.when(ok)(copy.wait_recv)
                ok, copy = onward(n + 1)
                pl.when(ok)(copy.start)
        elif n == 3:
            for landed in (self.up_landed, self.down_landed):
                ok, copy = landed(3)
                pl.when(ok)(copy.wait_recv)
            self.local.wait()
            self.side(0)[0].start()
        elif n in (4, 5):
            self.side(n - 4)[0].wait_recv()
            self.side(n - 3)[0].start()
        elif n == 6:
            self.side(2)[0].wait_recv()

    def finish(self):
        for k in (1, 2, 3):
            for ok, copy in (self.up(k), self.down(k)):
                pl.when(ok)(copy.wait_send)
        for which in range(3):
            self.side(which)[0].wait_send()

def gather_kernel(plan, n_in, *refs):
    owns, wholes, send, recv = refs[:n_in], refs[n_in : 2 * n_in], refs[2 * n_in], refs[2 * n_in + 1]
    greet()
    units = [Spread(owns[i], wholes[i], cut, x_first, send.at[n], recv.at[n]) for n, (i, cut, x_first) in enumerate(plan)]
    pairs = [units[i : i + 2] for i in range(0, len(units), 2)]
    for t in range(len(pairs) + 6):
        for n in (3, 4, 5, 6, 2, 1, 0):
            if 0 <= t - n < len(pairs):
                for unit in pairs[t - n]:
                    unit.stage(n)
    for unit in units:
        unit.finish()

def gather_all(shards, plan, collective_id=1):
    n = len(shards)
    return pl.pallas_call(
        functools.partial(gather_kernel, plan, n),
        in_specs=[pl.BlockSpec(memory_space=pl.ANY)] * n,
        out_specs=[pl.BlockSpec(memory_space=pl.ANY)] * n,
        out_shape=[jax.ShapeDtypeStruct((4, 2, 2, 2) + s.shape, s.dtype) for s in shards],
        scratch_shapes=[pltpu.SemaphoreType.DMA((len(plan), 9)), pltpu.SemaphoreType.DMA((len(plan), 10))],
        compiler_params=pltpu.CompilerParams(collective_id=collective_id, has_side_effects=True),
    )(*shards)


def greet_plane():
    z, x, y, c = spot()
    barrier = pltpu.get_barrier_semaphore()
    for n in range(1, 8):
        pl.semaphore_signal(barrier, inc=1, device_id=device(z, x ^ (n >> 2), y ^ ((n >> 1) & 1), c ^ (n & 1)), device_id_type=MESH)
    for n in range(1, 4):
        pl.semaphore_signal(barrier, inc=1, device_id=device(z ^ n, x, y, c), device_id_type=MESH)
    pl.semaphore_wait(barrier, 10)


def add_into(dst, src, lead):
    def one(i, unused):
        for n in range(lead[1]):
            for m in range(lead[2]):
                d, s = dst(i, n, m), src(i, n, m)
                d[...] = (d[...].astype(jnp.float32) + s[...].astype(jnp.float32)).astype(d.dtype)
        return unused

    lax.fori_loop(0, lead[0], one, 0)


class Collect:
    def __init__(self, parts, out, cut, x_first, bufs, send, recv):
        self.parts, self.out, self.cut, self.x_first, self.send, self.recv = parts, out, cut, x_first, send, recv
        self.own, self.rc, self.r1, self.r2, self.rz = bufs

    def copy(self, src, dst, n, to):
        return pltpu.make_async_remote_copy(
            src_ref=src, dst_ref=dst, send_sem=self.send.at[n], recv_sem=self.recv.at[n], device_id=to, device_id_type=MESH
        )

    def load(self):
        z, x, y, c = spot()
        every = slice(None)
        return pltpu.make_async_copy(self.parts.at[(every, every, every, c) + self.cut], self.own, self.recv.at[9])

    def core(self):
        z, x, y, c = spot()
        every = slice(None)
        return self.copy(self.parts.at[(every, every, every, 1 - c) + self.cut], self.rc, 0, device(z, x, y, 1 - c))

    def first(self):
        z, x, y, c = spot()
        if self.x_first:
            return self.copy(self.own.at[:, 1 - x], self.r1, 1, device(z, 1 - x, y, c))
        return self.copy(self.own.at[:, :, 1 - y], self.r1, 1, device(z, x, 1 - y, c))

    def second(self):
        z, x, y, c = spot()
        if self.x_first:
            return self.copy(self.own.at[:, x, 1 - y], self.r2, 2, device(z, x, 1 - y, c))
        return self.copy(self.own.at[:, 1 - x, y], self.r2, 2, device(z, 1 - x, y, c))

    def down(self, k):
        z, x, y, c = spot()
        d = z - (4 - k)
        return d >= 0, self.copy(self.own.at[jnp.maximum(d, 0), x, y], self.rz.at[k - 1], 2 + k, device(z - 1, x, y, c))

    def down_landed(self, k):
        z, x, y, c = spot()
        d = z - (3 - k)
        ref = self.rz.at[k - 1]
        return (z < 3) & (d >= 0), d, ref, self.copy(ref, ref, 2 + k, device(z, x, y, 1 - c))

    def up(self, k):
        z, x, y, c = spot()
        d = z + (4 - k)
        return d <= 3, self.copy(self.own.at[jnp.minimum(d, 3), x, y], self.rz.at[2 + k], 5 + k, device(z + 1, x, y, c))

    def up_landed(self, k):
        z, x, y, c = spot()
        d = z + (3 - k)
        ref = self.rz.at[2 + k]
        return (z > 0) & (d <= 3), d, ref, self.copy(ref, ref, 5 + k, device(z, x, y, 1 - c))

    def stage(self, n):
        z, x, y, c = spot()
        if n == 0:
            self.core().start()
            self.load().start()
        elif n == 1:
            self.core().wait_recv()
            self.load().wait()
            add_into(lambda i, j, k: self.own.at[i, j, k], lambda i, j, k: self.rc.at[i, j, k], (4, 2, 2))
            self.first().start()
        elif n == 2:
            self.first().wait_recv()
            if self.x_first:
                add_into(lambda i, j, k: self.own.at[i, x, j], lambda i, j, k: self.r1.at[i, j], (4, 2, 1))
            else:
                add_into(lambda i, j, k: self.own.at[i, j, y], lambda i, j, k: self.r1.at[i, j], (4, 2, 1))
            self.second().start()
        elif n == 3:
            self.second().wait_recv()
            add_into(lambda i, j, k: self.own.at[i, x, y], lambda i, j, k: self.r2.at[i], (4, 1, 1))
            for ok, copy in (self.down(1), self.up(1)):
                pl.when(ok)(copy.start)
        elif n in (4, 5):
            for landed, onward in ((self.down_landed, self.down), (self.up_landed, self.up)):
                ok, d, ref, copy = landed(n - 3)

                @pl.when(ok)
                def _(d=d, ref=ref, copy=copy):
                    copy.wait_recv()
                    own = self.own.at[jnp.clip(d, 0, 3), x, y]
                    own[...] = (own[...].astype(jnp.float32) + ref[...].astype(jnp.float32)).astype(own.dtype)

                ok, copy = onward(n - 2)
                pl.when(ok)(copy.start)
        elif n == 6:
            out = self.out.at[self.cut] if self.cut else self.out
            out[...] = self.own[z, x, y].astype(jnp.float32)
            for landed in (self.down_landed, self.up_landed):
                ok, d, ref, copy = landed(3)

                @pl.when(ok)
                def _(ref=ref, copy=copy):
                    copy.wait_recv()
                    out[...] += ref[...].astype(jnp.float32)

    def finish(self):
        for copy in (self.core(), self.first(), self.second()):
            copy.wait_send()
        for k in (1, 2, 3):
            for ok, copy in (self.down(k), self.up(k)):
                pl.when(ok)(copy.wait_send)


def square_sum(refs, tile):
    tile[...] = jnp.zeros_like(tile)
    for ref in refs:
        v = ref[...]
        v = (v * v).reshape(-1, v.shape[-1])
        v = jnp.sum(v.reshape(-1, 8, v.shape[-1]), axis=0)
        for i in range(0, v.shape[-1], 128):
            tile[...] += v[:, i : i + 128]


def total_square(outs, norm, tiles, send, recv):
    z, x, y, c = spot()
    mine = x * 4 + y * 2 + c
    square_sum(outs, tiles.at[mine])
    copies = []
    for n in range(1, 8):
        to = device(z, x ^ (n >> 2), y ^ ((n >> 1) & 1), c ^ (n & 1))
        copies.append(pltpu.make_async_remote_copy(
            src_ref=tiles.at[mine], dst_ref=tiles.at[mine], send_sem=send.at[n], recv_sem=recv.at[n], device_id=to, device_id_type=MESH))
        copies[-1].start()
    for n in range(1, 8):
        ref = tiles.at[mine ^ n]
        pltpu.make_async_remote_copy(src_ref=ref, dst_ref=ref, send_sem=send.at[n], recv_sem=recv.at[n], device_id=device(z, x, y, 1 - c), device_id_type=MESH).wait_recv()
    total = tiles[0]
    for n in range(1, 8):
        total = total + tiles[n]
    tiles[8 + z] = total
    for n in range(1, 4):
        copies.append(pltpu.make_async_remote_copy(
            src_ref=tiles.at[8 + z], dst_ref=tiles.at[8 + z], send_sem=send.at[7 + n], recv_sem=recv.at[7 + n], device_id=device(z ^ n, x, y, c), device_id_type=MESH))
        copies[-1].start()
    for n in range(1, 4):
        ref = tiles.at[8 + (z ^ n)]
        pltpu.make_async_remote_copy(src_ref=ref, dst_ref=ref, send_sem=send.at[7 + n], recv_sem=recv.at[7 + n], device_id=device(z, x, y, 1 - c), device_id_type=MESH).wait_recv()
    norm[...] = (tiles[8] + tiles[9]) + (tiles[10] + tiles[11])
    for copy in copies:
        copy.wait_send()


def unit_shape(shape, cut):
    cut = tuple(cut) + (slice(None),) * (len(shape) - len(cut))
    return tuple(len(range(*s.indices(d))) for s, d in zip(cut, shape))


def collect_kernel(plan, n_in, *refs):
    parts, outs, norm = refs[:n_in], refs[n_in : 2 * n_in], refs[2 * n_in]
    send, recv, tiles, nsend, nrecv = refs[2 * n_in + 1 : 2 * n_in + 6]
    bufs = refs[2 * n_in + 6 :]
    greet_plane()
    units = [
        Collect(parts[i], outs[i], cut, x_first, bufs[5 * n : 5 * n + 5], send.at[n], recv.at[n])
        for n, (i, cut, x_first) in enumerate(plan)
    ]
    pairs = [units[i : i + 2] for i in range(0, len(units), 2)]
    for t in range(len(pairs) + 6):
        for n in range(7):
            if 0 <= t - n < len(pairs):
                for unit in pairs[t - n]:
                    unit.stage(n)
    for unit in units:
        unit.finish()
    total_square(outs, norm, tiles, nsend, nrecv)


def collect_scratch(plan, shapes, dtype):
    scratch = []
    for i, cut, x_first in plan:
        m = unit_shape(shapes[i], cut)
        scratch += [pltpu.VMEM(lead + m, dtype) for lead in ((4, 2, 2), (4, 2, 2), (4, 2), (4,), (6,))]
    return scratch


def collect_all(parts, plan, collective_id=2):
    n = len(parts)
    shapes = [p.shape[4:] for p in parts]
    return pl.pallas_call(
        functools.partial(collect_kernel, plan, n),
        in_specs=[pl.BlockSpec(memory_space=pl.ANY)] * n,
        out_specs=[pl.BlockSpec(memory_space=pltpu.VMEM)] * (n + 1),
        out_shape=[jax.ShapeDtypeStruct(s, jnp.float32) for s in shapes] + [jax.ShapeDtypeStruct((8, 128), jnp.float32)],
        scratch_shapes=[pltpu.SemaphoreType.DMA((len(plan), 9)), pltpu.SemaphoreType.DMA((len(plan), 10)),
                        pltpu.VMEM((12, 8, 128), jnp.float32), pltpu.SemaphoreType.DMA((11,)), pltpu.SemaphoreType.DMA((11,))]
        + collect_scratch(plan, shapes, parts[0].dtype),
        compiler_params=pltpu.CompilerParams(collective_id=collective_id, has_side_effects=True, vmem_limit_bytes=60 * 2**20),
    )(*parts)


S = slice


def gather_plan():
    plan = []
    for a in range(0, 8, 2):
        plan += [(0, (S(a, a + 1),), False), (0, (S(a + 1, a + 2),), True)]
    plan += [(1, (S(None), S(0, 1152)), False), (1, (S(None), S(1152, 2304)), True)]
    plan += [(2, (S(None), S(0, 384)), False), (2, (S(None), S(384, 768)), True)]
    for i in range(0, 3072, 1536):
        plan += [(3, (S(None), S(i, i + 768)), False), (3, (S(None), S(i + 768, i + 1536)), True)]
    plan += [(4, (S(0, 32),), False), (4, (S(32, 64),), True), (4, (S(64, 96),), False), (5, (), True)]
    return plan


def collect_plan():
    plan = [(4, (S(0, 32),), False), (4, (S(32, 64),), True), (4, (S(64, 96),), False)]
    for i in range(4):
        plan.append((3, (S(None), S(768 * i, 768 * i + 768)), i % 2 == 0))
    plan.append((2, (), True))
    for i in range(3):
        plan.append((1, (S(None), S(768 * i, 768 * i + 768)), i % 2 == 0))
    for a in range(0, 8, 2):
        plan += [(0, (S(a, a + 1),), True), (0, (S(a + 1, a + 2),), False)]
    plan.append((5, (), False))
    return plan


def by_chips():
    return lax.axis_size("seq") == 8 and lax.axis_size("head") == 4


def gather_weights(parts):
    if by_chips():
        return [w.reshape((32,) + w.shape[4:]) for w in gather_all(parts, gather_plan())]
    return [lax.all_gather(p, ("seq", "head"), axis=0) for p in parts]


def collect_grads(parts):
    if by_chips():
        outs = collect_all([p.reshape((4, 2, 2, 2) + p.shape[1:]) for p in parts], collect_plan())
        return outs[:-1], jnp.sum(outs[-1])
    outs = [lax.psum_scatter(p.astype(jnp.float32), ("seq", "head"), scatter_dimension=0, tiled=False) for p in parts]
    square = jnp.zeros((), jnp.float32)
    for out in outs:
        square = square + jnp.sum(out * out)
    return outs, lax.psum(square, ("seq", "head"))


def trade(pieces):
    count = lax.axis_size("head")
    return [pieces[0]] + [lax.ppermute(pieces[d], "head", [(i, i ^ d) for i in range(count)]) for d in range(1, count)]


def by_partner(stacked):
    me = lax.axis_index("head")
    return [lax.dynamic_index_in_dim(stacked, me ^ d, 0, keepdims=False) for d in range(stacked.shape[0])]


def from_partner(pieces):
    me = lax.axis_index("head")
    stacked = jnp.stack(pieces)
    return jnp.concatenate([lax.dynamic_index_in_dim(stacked, me ^ j, 0, keepdims=False) for j in range(len(pieces))], axis=0)


def shards(
    frames, output_grad, segment_ids, qkv_weight, proj_weight, up_weight, down_weight, conv_weight, bias_gains, ffn_bias,
    qkv_first, proj_first, up_first, down_first, conv_first, bias_gains_first, ffn_bias_first,
    qkv_second, proj_second, up_second, down_second, conv_second, bias_gains_second, ffn_bias_second,
):
    low_type = jnp.bfloat16
    f32 = jnp.float32
    count = lax.axis_size("seq") * lax.axis_size("head")
    row_count, model_width = frames.shape
    head_groups = lax.axis_size("head")
    head_index = lax.axis_index("head")
    kernel_len, conv_rows, group_width = conv_weight.shape
    vec_rows, vec_cols = bias_gains.shape
    ffn_cols = ffn_bias.shape[0]
    conv_low = conv_weight.astype(low_type).reshape(16, 8, conv_rows, group_width).transpose(1, 2, 0, 3).reshape(8, conv_rows, 768)
    small = jnp.concatenate([bias_gains.astype(low_type).reshape(-1), ffn_bias.astype(low_type)])
    small = jnp.pad(small, (0, 2048 - small.shape[0])).reshape(16, 128)
    all_conv, all_qkv, all_proj, all_up, all_down, all_small = gather_weights(
        [conv_low, qkv_weight.astype(low_type), proj_weight.astype(low_type), up_weight.astype(low_type), down_weight.astype(low_type), small]
    )
    full_qkv = all_qkv.reshape(model_width, -1)
    full_proj = all_proj.reshape(model_width, -1)
    full_up = all_up.reshape(model_width, -1)
    full_down = all_down.reshape(-1, model_width)
    full_conv = all_conv.reshape(16, 2, 24 // conv_rows, 8, conv_rows, 768).transpose(0, 1, 3, 2, 4, 5).reshape(16, 2, 8, 24, 768)
    all_small = all_small.reshape(count, 2048).astype(f32)
    vectors = all_small[:, : vec_rows * vec_cols].reshape(count, vec_rows, vec_cols).transpose(1, 0, 2).reshape(vec_rows, model_width)
    full_ffn = all_small[:, vec_rows * vec_cols : vec_rows * vec_cols + ffn_cols].reshape(-1)

    seg_group = segment_ids[0]
    half_kernel = kernel_len // 2
    boundary = jnp.sum((seg_group == 0).astype(jnp.int32))
    cut = jnp.clip(boundary - head_index * row_count + half_kernel, 0, row_count + kernel_len)
    cut = jnp.stack([cut, (head_index == head_groups - 1).astype(jnp.int32)]).astype(jnp.int32)
    seg_rows = jnp.concatenate(by_partner(seg_group.reshape(head_groups, 1, row_count)), axis=1)

    window = with_halo(frames, (("head", 0),), half_kernel)
    conv_pre = conv_fwd(cut, window, full_conv) + vectors[0]
    conv_act, conv_act_back = jax.vjp(gelu_exact, conv_pre)
    hidden_one = frames.astype(f32) + conv_act
    attn_in = hidden_one.astype(low_type)
    zero_part = jnp.zeros((HEADS, HEAD_DIM), f32)
    qkv_bias = jnp.stack(
        [vectors[1].reshape(HEADS, HEAD_DIM), zero_part, vectors[2].reshape(HEADS, HEAD_DIM)], axis=1
    ).reshape(3 * model_width)
    packed = (
        lax.dot_general(full_qkv, attn_in, (((0,), (1,)), ((), ())), preferred_element_type=f32) + qkv_bias[:, None]
    ).astype(low_type)
    blocks = trade(by_partner(packed.reshape(head_groups, -1, row_count)))
    fwd = attn_fwd(seg_rows, blocks)
    context = from_partner(trade(fwd[:4]))
    attn_out = lax.dot_general(context, full_proj, (((0,), (0,)), ((), ())), preferred_element_type=f32) + vectors[3]
    normed_one, norm_one_back = jax.vjp(layer_norm, hidden_one + attn_out, vectors[4], vectors[5])
    ffn_in = normed_one.astype(low_type)
    up_act, up_back = jax.vjp(gelu_exact, jnp.dot(ffn_in, full_up, preferred_element_type=f32) + full_ffn)
    hidden_mid = up_act.astype(low_type)
    hidden_three = normed_one + jnp.dot(hidden_mid, full_down, preferred_element_type=f32) + vectors[6]
    layer_out_full, norm_two_back = jax.vjp(layer_norm, hidden_three, vectors[7], vectors[8])
    grad_three, grad_gain_two, grad_shift_two = norm_two_back(output_grad.astype(f32))
    grad_ffn = grad_three.astype(low_type)
    grad_down = jnp.einsum("tf,td->fd", hidden_mid, grad_ffn, preferred_element_type=f32).astype(low_type)
    grad_down_bias = jnp.sum(grad_ffn.astype(f32), axis=0)
    (grad_up_pre,) = up_back(jnp.einsum("td,fd->tf", grad_ffn, full_down, preferred_element_type=f32))
    grad_up_low = grad_up_pre.astype(low_type)
    grad_up = jnp.einsum("td,tf->df", ffn_in, grad_up_low, preferred_element_type=f32).astype(low_type)
    grad_ffn_bias = jnp.sum(grad_up_low.astype(f32), axis=0)
    grad_normed = grad_three + jnp.einsum("tf,df->td", grad_up_low, full_up, preferred_element_type=f32)
    grad_two, grad_gain_one, grad_shift_one = norm_one_back(grad_normed)
    grad_attn = grad_two.astype(low_type)
    grad_proj = jnp.dot(context, grad_attn, preferred_element_type=f32).astype(low_type)
    grad_proj_bias = jnp.sum(grad_attn.astype(f32), axis=0)
    grad_context = lax.dot_general(full_proj, grad_attn, (((1,), (1,)), ((), ())), preferred_element_type=f32).astype(low_type)
    grad_blocks = trade(by_partner(grad_context.reshape(head_groups, -1, row_count)))
    grad_packed = from_partner(trade(attn_bwd(seg_rows, blocks, grad_blocks, fwd[4], fwd[5])))
    grad_qkv = lax.dot_general(attn_in, grad_packed, (((0,), (1,)), ((), ())), preferred_element_type=f32).astype(low_type)
    grad_split = jnp.sum(grad_packed.astype(f32), axis=1).reshape(HEADS, 3, HEAD_DIM)
    grad_query_bias = grad_split[:, 0].reshape(model_width)
    grad_value_bias = grad_split[:, 2].reshape(model_width)
    grad_hidden_one = grad_two + lax.dot_general(grad_packed, full_qkv, (((0,), (1,)), ((), ())), preferred_element_type=f32)
    (grad_conv_pre,) = conv_act_back(grad_hidden_one)
    grad_conv_low = grad_conv_pre.astype(low_type)
    grad_conv_bias = jnp.sum(grad_conv_low.astype(f32), axis=0)
    grad_window = with_halo(grad_conv_low, (("head", 0),), half_kernel)
    grad_frames_conv, grad_conv = conv_bwd(cut, window, grad_window, full_conv)
    frames_grad = grad_hidden_one + grad_frames_conv
    grad_conv = grad_conv.reshape(16, 2, 8, 24 // conv_rows, conv_rows, 768).transpose(0, 1, 3, 2, 4, 5).reshape(count, 8, conv_rows, 768)
    grad_vectors = jnp.stack(
        [
            grad_conv_bias, grad_query_bias, grad_value_bias, grad_proj_bias, grad_gain_one, grad_shift_one,
            grad_down_bias, grad_gain_two, grad_shift_two,
        ],
        axis=0,
    )
    grad_small = jnp.concatenate(
        [grad_vectors.reshape(vec_rows, count, vec_cols).transpose(1, 0, 2).reshape(count, -1), grad_ffn_bias.reshape(count, ffn_cols)], axis=1
    )
    grad_small = jnp.pad(grad_small, ((0, 0), (0, 2048 - grad_small.shape[1]))).astype(low_type).reshape(count, 16, 128)
    (sum_conv, sum_qkv, sum_proj, sum_up, sum_down, sum_small), square_sum = collect_grads(
        [
            grad_conv,
            grad_qkv.reshape((count,) + qkv_weight.shape),
            grad_proj.reshape((count,) + proj_weight.shape),
            grad_up.reshape((count,) + up_weight.shape),
            grad_down.reshape((count,) + down_weight.shape),
            grad_small,
        ]
    )
    sum_conv = sum_conv.reshape(8, conv_rows, 16, group_width).transpose(2, 0, 1, 3).reshape(conv_weight.shape)
    sum_small = sum_small.reshape(-1)
    sum_vectors = sum_small[: vec_rows * vec_cols].reshape(vec_rows, vec_cols)
    sum_ffn_bias = sum_small[vec_rows * vec_cols : vec_rows * vec_cols + ffn_cols]
    summed = (sum_qkv, sum_proj, sum_up, sum_down, sum_conv, sum_vectors, sum_ffn_bias)
    grad_norm = jnp.sqrt(square_sum)
    factor = jnp.minimum(1.0, clip_bound / grad_norm)
    masters = (qkv_weight, proj_weight, up_weight, down_weight, conv_weight, bias_gains, ffn_bias)
    firsts = (qkv_first, proj_first, up_first, down_first, conv_first, bias_gains_first, ffn_bias_first)
    seconds = (qkv_second, proj_second, up_second, down_second, conv_second, bias_gains_second, ffn_bias_second)
    news, first_news, second_news = [], [], []
    for index in range(7):
        decay = matrix_decay if index < 5 else 0.0
        new_weight, first_new, second_new = adam_update(
            masters[index], summed[index] * factor, firsts[index], seconds[index], weight_rates[index], decay
        )
        news.append(new_weight)
        first_news.append(first_new)
        second_news.append(second_new)
    return (layer_out_full.astype(low_type), frames_grad, grad_norm, *news, *first_news, *second_news)


def solution(mesh):
    rows, both = P(("seq", "head"), None), ("seq", "head")
    weights = (rows, rows, rows, rows, P(None, both, None), P(None, both), P(both))
    return jax.shard_map(
        shards,
        mesh=mesh,
        in_specs=(rows, rows, P("seq", None)) + weights * 3,
        out_specs=(rows, rows, P()) + weights * 3,
        check_vma=False,
    )
```

time: 1580 us -> 628 us (0.40)
  local copies, waits for them, and re-layouts: 643 us -> 50.4 us
  Pallas kernels: 0 us -> 409 us
  matrix products: 307 us -> 62.1 us
  blocking collectives: 227 us -> 0 us
  waiting for transfers between devices: 217 us -> 46.8 us
  other arithmetic: 103 us -> 32.7 us
  loops' own time: 34.3 us -> 0 us
  between operations: 21.9 us -> 4.57 us
    pallas_call x0 -> x6, Pallas kernels: none -> 409 us  [the longest x1 130 us: collect_all(): pl.pallas_call(functools.partial(collect_kernel, plan, n), in_specs=[pl.B...]
    dynamic_slice x146 -> x0, local copies, waits for them, and re-layouts: 260 us -> none  [the longest x64 200 us: tap_rows(): lax.dynamic_slice_in_dim(source, first_tap + direction * offset, row_coun...]
    dot_general x88 -> x12, matrix products: 307 us -> 62.1 us  [the longest x1 18.5 us: shards(): jnp.dot(ffn_in, full_up, preferred_element_type=f32) + full_ffn]
    reduce_scatter x5 -> x0, waiting for transfers between devices: 149 us -> none  [the longest x1 149 us: shards(): lax.psum_scatter(grad_conv, ('seq', 'head'), scatter_dimension=1, tiled=T...]
    reshape x41 -> x4, local copies, waits for them, and re-layouts: 140 us -> 3.01 us  [the longest x1 1.48 us: shards(): conv_weight.astype(low_type).reshape(16, 8, conv_rows, group_width)]
    while x592 -> x0, local copies, waits for them, and re-layouts: 101 us -> none
    unnamed x2 -> x0, blocking collectives: 88.2 us -> none
    dynamic_update_slice x16 -> x0, local copies, waits for them, and re-layouts: 56.1 us -> none  [conv_backward(): lax.scan(advance, start, jnp.arange(kernel_len // tap_count, dtype=jnp.in...]
  transfers between devices with their start and end apart: 17 -> 16, of which waited for: 4 -> 5; matrix products, arithmetic and copies ran while one was open for 58% -> 8% of each run, Pallas kernels for 0% -> 20%
where the time goes in v1:
time: 628 us; the launch traced here: 622 us
  Pallas kernels  409 us (65%)
  matrix products  62.1 us (10%)
  local copies, waits for them, and re-layouts  50.4 us (8%)
  waiting for transfers between devices  46.8 us (7%)
  other arithmetic  32.7 us (5%)
  starting transfers between devices  16.8 us (3%)
    pallas_call x1, Pallas kernels, collect_all(): pl.pallas_call(functools.partial(collect_kernel, plan, n), in_specs=[pl.B...  130 us
    pallas_call x1, Pallas kernels, gather_all(): pl.pallas_call(functools.partial(gather_kernel, plan, n), in_specs=[pl.Bl...  122 us
    pallas_call x1, Pallas kernels, conv_bwd(): pl.pallas_call(conv_bwd_kernel, grid_spec=pltpu.PrefetchScalarGridSpec(nu...  54.5 us
    ppermute x12, waiting for transfers between devices, trade(): lax.ppermute(pieces[d], 'head', [(i, i ^ d) for i in range(count)])  46.8 us
    pallas_call x1, Pallas kernels, attn_bwd(): pl.pallas_call(attn_bwd_kernel, grid=(heads,), in_specs=[pl.BlockSpec((1,...  37.3 us
    pallas_call x1, Pallas kernels, attn_fwd(): pl.pallas_call(attn_fwd_kernel, grid=(heads,), in_specs=[pl.BlockSpec((1,...  36.7 us
    pallas_call x1, Pallas kernels, conv_fwd(): pl.pallas_call(conv_fwd_kernel, grid_spec=pltpu.PrefetchScalarGridSpec(nu...  28.2 us
    dot_general x1, matrix products, shards(): jnp.dot(ffn_in, full_up, preferred_element_type=f32) + full_ffn  18.5 us
  transfers between devices with their start and end apart: 16, of which 5 were waited for; matrix products, arithmetic and copies ran while one was open for 8% of the time, Pallas kernels for 20%

profile of v1, /device:TPU:0, one launch (start us, length us, event | category | flops | bytes accessed | tf_op | source)
XLA Modules:
  0.0 622.2 jit_solution(4658711687847905252)
XLA Ops:
  2.3 2.3 collective-permute-start
  13.1 121.8 %shard_map.415 = (bf16[4,2,2,2,8,24,768]{6,5,4,3,2,1,0:T(8,128)(2,1)}, bf16[4,2,2,2,24,2304]{5,4,3,2,1,0:T(8,128)(2,1)}, bf16[4,2,2,2,24,768]{5,4,3,2,1,0:T(8,12...) custom-call(bf16[8,24,768]{2,1,0:T(8,128)(2,1)} %reshape.207.refs_0_, ...), custom_call_target="tpu_custom_call" | custom-call | tf_op jit(solution)/shard_map/pallas_call | solution.py:460
  141.2 28.2 %shard_map.416 = f32[512,768]{1,0:T(8,128)S(1)} custom-call(s32[2]{0:T(128)S(1)} %pad_add_fusion.1.cut_ref, bf16[640,768]{1,0:T(8,128)(2,1)S(1)} %constant_dynamic-update-slice_fusion.x_ref, bf16[16,2,8,24,768]{4,3,2,1,0:T(8,128)(2,1)} %bitcast.128), custom_call_target="tpu_custom_call" | custom-call | flops 7348420608 | bytes 12000000 | tf_op jit(solution)/shard_map/pallas_call | solution.py:149
  169.4 4.4 multiply_add_fusion.1
  173.8 2.4 fusion.6
  180.0 14.5 %collective-permute-done.3.b2 = bf16[576,512]{1,0:T(8,128)(2,1)} collective-permute-done((bf16[576,512]{1,0:T(8,128)(2,1)}, bf16[576,512]{1,0:T(8,128)(2,1)}, u32[]{:S(2)}, u32[]{:S(2)}) %collective-permute-start.3) | collective-permute-done | bytes 589856 | tf_op jit(solution)/shard_map/ppermute | solution.py:736
  194.5 10.7 %collective-permute-done.4.b3 = bf16[576,512]{1,0:T(8,128)(2,1)} collective-permute-done((bf16[576,512]{1,0:T(8,128)(2,1)}, bf16[576,512]{1,0:T(8,128)(2,1)}, u32[]{:S(2)}, u32[]{:S(2)}) %collective-permute-start.4) | collective-permute-done | bytes 589856 | tf_op jit(solution)/shard_map/ppermute | solution.py:736
  205.3 36.7 %shard_map.417 = (bf16[192,512]{1,0:T(8,128)(2,1)S(1)}, bf16[192,512]{1,0:T(8,128)(2,1)S(1)}, bf16[192,512]{1,0:T(8,128)(2,1)}, bf16[192,512]{1,0:T(8,128)(2,1)}...) custom-call(s32[1,2048]{1,0:T(1,128)S(1)} %pad_add_fusion.seg_ref, bf16[576,512]{1,0:T(8,128)(2,1)S(1)} %get-tuple-element.199.b0, ...), custom_call_target="tpu_custom_call" | custom-call | flops 3221225472 | bytes 6000000 | tf_op jit(solution)/shard_map/pallas_call | solution.py:273
  270.5 2.1 slice-done
  272.7 18.5 %multiply_convert_fusion = (bf16[512,3072]{1,0:T(8,128)(2,1)S(1)}, f32[512,3072]{1,0:T(8,128)}, f32[512,3072]{1,0:T(8,128)}) fusion(f32[3072]{0:T(1024)S(1)} %copy-done.57, bf16[768,3072]{1,0:T(8,128)(2,1)S(1)} %bitcast.132, f32[512,768]{1,0:T(8,128)S(1)} %get-tuple-element.227, f32[768]{0:T(1024)S(1)} %copy-done.67, f32[768]{0:T(1024)S(1)} %copy-done.55, ...), kind=kOutput, calls=%fused_computation.3 | convolution fusion | flops 2521694208 | bytes 22042624 | tf_op jit(solution)/shard_map/dot_general | solution.py:804
  291.2 2.8 fusion.68
  298.9 4.4 convolution_convert_fusion
  303.3 9.7 %fusion.59 = (bf16[3072]{0:T(1024)(128)(2,1)}, bf16[512,3072]{1,0:T(8,128)(2,1)}) fusion(f32[512,3072]{1,0:T(8,128)} %get-tuple-element.189, f32[512,3072]{1,0:T(8,128)} %get-tuple-element.228, f32[3072]{0:T(1024)S(1)} %copy-done.57, bf16[512,768]{1,0:T(8,128)(2,1)S(1)} %get-tuple-element.177, bf16[3072,768]{1,0:T(8,128)(2,1)S(1)} %bitcast.137), kind=kOutput, calls=%fused_computation.172 | convolution fusion | flops 2441081856 | bytes 21252096 | tf_op jit(solution)/shard_map/td,fd->tf/dot_general | solution.py:812
  312.9 5.7 multiply_reduce_fusion
  331.7 3.3 convolution_convert_fusion.3
  335.1 37.3 %shard_map.418 = (bf16[576,512]{1,0:T(8,128)(2,1)S(1)}, bf16[576,512]{1,0:T(8,128)(2,1)S(1)}, bf16[576,512]{1,0:T(8,128)(2,1)S(1)}, bf16[576,512]{1,0:T(8,128)(2,1)S(1)}) custom-call(s32[1,2048]{1,0:T(1,128)S(1)} %pad_add_fusion.seg_ref, bf16[576,512]{1,0:T(8,128)(2,1)S(1)} %get-tuple-element.199.b0, bf16[576,512]{1,0:T(8,128)(2,1)} %collective-permute-done.2.b1, ...), custom_call_target="tpu_custom_call" | custom-call | flops 8053063680 | bytes 10000000 | tf_op jit(solution)/shard_map/pallas_call | solution.py:324
  374.8 4.8 convolution_convert_fusion.1
  379.6 8.3 %collective-permute-done.13 = bf16[576,512]{1,0:T(8,128)(2,1)S(1)} collective-permute-done((bf16[576,512]{1,0:T(8,128)(2,1)S(1)}, bf16[576,512]{1,0:T(8,128)(2,1)S(1)}, u32[]{:S(2)}, u32[]{:S(2)}) %collective-permute-start.13) | collective-permute-done | bytes 589856 | tf_op jit(solution)/shard_map/ppermute | solution.py:736
  388.0 12.8 %collective-permute-done.12 = bf16[576,512]{1,0:T(8,128)(2,1)S(1)} collective-permute-done((bf16[576,512]{1,0:T(8,128)(2,1)S(1)}, bf16[576,512]{1,0:T(8,128)(2,1)S(1)}, u32[]{:S(2)}, u32[]{:S(2)}) %collective-permute-start.12) | collective-permute-done | bytes 589856 | tf_op jit(solution)/shard_map/ppermute | solution.py:736
  403.3 2.1 add_add_fusion.4
  405.4 6.7 %convolution_convert_fusion.2 = bf16[768,2304]{1,0:T(8,128)(2,1)} fusion(f32[512,768]{1,0:T(8,128)S(1)} %copy-done.14, bf16[576,512]{1,0:T(8,128)(2,1)S(1)} %get-tuple-element.193, bf16[576,512]{1,0:T(8,128)(2,1)S(1)} %get-tuple-element.194, bf16[576,512]{1,0:T(8,128)(2,1)S(1)} %get-tuple-element.195, bf16[576,512]{1,0:T(8,128)(2,1)S(1)} %get-tuple-element.192), kind=kOutput, calls=%fused_computation.19 | convolution fusion | flops 1823539200 | bytes 7471104 | tf_op jit(solution)/shard_map/dot_general | solution.py:824
  415.7 3.0 collective-permute-start.14
  420.4 54.5 %shard_map.419 = (f32[512,768]{1,0:T(8,128)S(1)}, bf16[16,2,8,24,768]{4,3,2,1,0:T(8,128)(2,1)}) custom-call(s32[2]{0:T(128)S(1)} %pad_add_fusion.1.cut_ref, bf16[640,768]{1,0:T(8,128)(2,1)S(1)} %constant_dynamic-update-slice_fusion.x_ref, bf16[640,768]{1,0:T(8,128)(2,1)S(1)} %pad_maximum_fusion.2.g_ref, bf16[16,2,8,24,768]{4,3,2,1,0:T(8,128)(2,1)} %bitcast.129), custom_call_target="tpu_custom_call" | custom-call | flops 16106127360 | bytes 22000000 | tf_op jit(solution)/shard_map/pallas_call | solution.py:217
  476.2 130.3 %shard_map.420 = (f32[8,24,768]{2,1,0:T(8,128)}, f32[24,2304]{1,0:T(8,128)}, f32[24,768]{1,0:T(8,128)}, f32[24,3072]{1,0:T(8,128)}, f32[96,768]{1,0:T(8,128)}, /*index=5*/f32[16,128]{1,0:T(8,128)}, f32[8,128]{1,0:T(8,128)}) custom-call(bf16[4,2,2,2,8,24,768]{6,5,4,3,2,1,0:T(8,128)(2,1)} %bitcast.107, bf16[4,2,2,2,24,2304]{5,4,3,2,1,0:T(8,128)(2,1)} %bitcast.111, ...), custom_call_target="tpu_custom_call" | custom-call | tf_op jit(solution)/shard_map/pallas_call | solution.py:673
  (310 shorter events, 90.1 us)
Async XLA Ops:
  2.3 138.9 %collective-permute-start = (bf16[64,768]{1,0:T(8,128)(2,1)}, bf16[64,768]{1,0:T(8,128)(2,1)S(1)}, u32[]{:S(2)}, u32[]{:S(2)}) collective-permute-start(bf16[64,768]{1,0:T(8,128)(2,1)} %get-tuple-element.212), channel_id=1, source_target_pairs={{0,1},{1,2},{2,3},{4,5},{5,6},{6,7},{8,9},{9,10},{10,11},{12,13},{... | collective-permute-start | bytes 294920 | tf_op jit(solution)/shard_map/ppermute | solution.py:32
  4.6 136.6 %collective-permute-start.1 = (bf16[64,768]{1,0:T(8,128)(2,1)S(1)}, bf16[64,768]{1,0:T(8,128)(2,1)S(1)}, u32[]{:S(2)}, u32[]{:S(2)}) collective-permute-start(bf16[64,768]{1,0:T(8,128)(2,1)S(1)} %get-tuple-element.211), channel_id=1, source_target_pairs={{1,0},{2,1},{3,2},{5,4},{6,5},{7,6},{9,8},{10,9},{11,10},{13,12},{... | collective-permute-start | bytes 294920 | tf_op jit(solution)/shard_map/ppermute | solution.py:34
  9.6 128.1 %copy-start.66 = (s32[1,2048]{1,0:T(1,128)S(1)}, s32[1,2048]{1,0:T(1,128)}, u32[]{:S(2)}) copy-start(s32[1,2048]{1,0:T(1,128)} %param.26) | copy-start | bytes 24580
  10.3 130.8 %copy-start.10 = (bf16[512,768]{1,0:T(8,128)(2,1)S(1)}, bf16[512,768]{1,0:T(8,128)(2,1)}, u32[]{:S(2)}) copy-start(bf16[512,768]{1,0:T(8,128)(2,1)} %param.24) | copy-start | bytes 2359300
  177.5 2.5 collective-permute-start.2
  178.0 16.5 %collective-permute-start.3 = (bf16[576,512]{1,0:T(8,128)(2,1)}, bf16[576,512]{1,0:T(8,128)(2,1)}, u32[]{:S(2)}, u32[]{:S(2)}) collective-permute-start(bf16[576,512]{1,0:T(8,128)(2,1)} %get-tuple-element.197), channel_id=1, source_target_pairs={{0,2},{1,3},{2,0},{3,1},{4,6},{5,7},{6,4},{7,5},{8,10},{9,11},{10,... | collective-permute-start | bytes 1769480 | tf_op jit(solution)/shard_map/ppermute | solution.py:736
  179.6 25.7 %collective-permute-start.4 = (bf16[576,512]{1,0:T(8,128)(2,1)}, bf16[576,512]{1,0:T(8,128)(2,1)}, u32[]{:S(2)}, u32[]{:S(2)}) collective-permute-start(bf16[576,512]{1,0:T(8,128)(2,1)} %get-tuple-element.196), channel_id=1, source_target_pairs={{0,3},{1,2},{2,1},{3,0},{4,7},{5,6},{6,5},{7,4},{8,11},{9,10},{10,... | collective-permute-start | bytes 1769480 | tf_op jit(solution)/shard_map/ppermute | solution.py:736
  242.6 24.6 %collective-permute-start.7 = (bf16[192,512]{1,0:T(8,128)(2,1)}, bf16[192,512]{1,0:T(8,128)(2,1)}, u32[]{:S(2)}, u32[]{:S(2)}) collective-permute-start(bf16[192,512]{1,0:T(8,128)(2,1)} %get-tuple-element.55), channel_id=1, source_target_pairs={{0,3},{1,2},{2,1},{3,0},{4,7},{5,6},{6,5},{7,4},{8,11},{9,10},{10,... | collective-permute-start | bytes 589832 | tf_op jit(solution)/shard_map/ppermute | solution.py:736
  244.5 22.6 %collective-permute-start.6 = (bf16[192,512]{1,0:T(8,128)(2,1)}, bf16[192,512]{1,0:T(8,128)(2,1)}, u32[]{:S(2)}, u32[]{:S(2)}) collective-permute-start(bf16[192,512]{1,0:T(8,128)(2,1)} %get-tuple-element.54), channel_id=1, source_target_pairs={{0,2},{1,3},{2,0},{3,1},{4,6},{5,7},{6,4},{7,5},{8,10},{9,11},{10,... | collective-permute-start | bytes 589832 | tf_op jit(solution)/shard_map/ppermute | solution.py:736
  245.0 22.2 %collective-permute-start.5 = (bf16[192,512]{1,0:T(8,128)(2,1)S(1)}, bf16[192,512]{1,0:T(8,128)(2,1)}, u32[]{:S(2)}, u32[]{:S(2)}) collective-permute-start(bf16[192,512]{1,0:T(8,128)(2,1)S(1)} %get-tuple-element.53), channel_id=1, source_target_pairs={{0,1},{1,0},{2,3},{3,2},{4,5},{5,4},{6,7},{7,6},{8,9},{9,8},{10,11... | collective-permute-start | bytes 589832 | tf_op jit(solution)/shard_map/ppermute | solution.py:736
  270.1 48.5 %copy-start.3 = (f32[512,768]{1,0:T(8,128)}, f32[512,768]{1,0:T(8,128)S(1)}, u32[]{:S(2)}) copy-start(f32[512,768]{1,0:T(8,128)S(1)} %get-tuple-element.227) | copy-start | bytes 4718596
  270.2 48.5 %copy-start.52 = (f32[512]{0:T(512)}, f32[512]{0:T(512)S(1)}, u32[]{:S(2)}) copy-start(f32[512]{0:T(512)S(1)} %broadcast_multiply_fusion.2) | copy-start | bytes 6148
  270.5 48.2 %copy-start.60 = (f32[512]{0:T(512)}, f32[512]{0:T(512)S(1)}, u32[]{:S(2)}) copy-start(f32[512]{0:T(512)S(1)} %fusion.39) | copy-start | bytes 6148
  322.0 13.0 %collective-permute-start.8 = (bf16[192,512]{1,0:T(8,128)(2,1)}, bf16[192,512]{1,0:T(8,128)(2,1)S(1)}, u32[]{:S(2)}, u32[]{:S(2)}) collective-permute-start(bf16[192,512]{1,0:T(8,128)(2,1)} %get-tuple-element.205), channel_id=1, source_target_pairs={{0,1},{1,0},{2,3},{3,2},{4,5},{5,4},{6,7},{7,6},{8,9},{9,8},{10,11... | collective-permute-start | bytes 589832 | tf_op jit(solution)/shard_map/ppermute | solution.py:736
  322.6 12.5 %collective-permute-start.9 = (bf16[192,512]{1,0:T(8,128)(2,1)}, bf16[192,512]{1,0:T(8,128)(2,1)}, u32[]{:S(2)}, u32[]{:S(2)}) collective-permute-start(bf16[192,512]{1,0:T(8,128)(2,1)} %get-tuple-element.204), channel_id=1, source_target_pairs={{0,2},{1,3},{2,0},{3,1},{4,6},{5,7},{6,4},{7,5},{8,10},{9,11},{10,... | collective-permute-start | bytes 589832 | tf_op jit(solution)/shard_map/ppermute | solution.py:736
  324.1 10.9 %collective-permute-start.10 = (bf16[192,512]{1,0:T(8,128)(2,1)}, bf16[192,512]{1,0:T(8,128)(2,1)}, u32[]{:S(2)}, u32[]{:S(2)}) collective-permute-start(bf16[192,512]{1,0:T(8,128)(2,1)} %get-tuple-element.203), channel_id=1, source_target_pairs={{0,3},{1,2},{2,1},{3,0},{4,7},{5,6},{6,5},{7,4},{8,11},{9,10},{10,... | collective-permute-start | bytes 589832 | tf_op jit(solution)/shard_map/ppermute | solution.py:736
  335.0 39.7 %copy-start.4 = (f32[512,768]{1,0:T(8,128)S(1)}, f32[512,768]{1,0:T(8,128)}, u32[]{:S(2)}) copy-start(f32[512,768]{1,0:T(8,128)} %copy-done.3) | copy-start | bytes 4718596
  335.1 39.7 %copy-start.53 = (f32[512]{0:T(512)S(1)}, f32[512]{0:T(512)}, u32[]{:S(2)}) copy-start(f32[512]{0:T(512)} %copy-done.52) | copy-start | bytes 6148
  372.5 15.5 %collective-permute-start.13 = (bf16[576,512]{1,0:T(8,128)(2,1)S(1)}, bf16[576,512]{1,0:T(8,128)(2,1)S(1)}, u32[]{:S(2)}, u32[]{:S(2)}) collective-permute-start(bf16[576,512]{1,0:T(8,128)(2,1)S(1)} %get-tuple-element.64), channel_id=1, source_target_pairs={{0,3},{1,2},{2,1},{3,0},{4,7},{5,6},{6,5},{7,4},{8,11},{9,10},{10,... | collective-permute-start | bytes 1769480 | tf_op jit(solution)/shard_map/ppermute | solution.py:736
  374.3 26.5 %collective-permute-start.12 = (bf16[576,512]{1,0:T(8,128)(2,1)S(1)}, bf16[576,512]{1,0:T(8,128)(2,1)S(1)}, u32[]{:S(2)}, u32[]{:S(2)}) collective-permute-start(bf16[576,512]{1,0:T(8,128)(2,1)S(1)} %get-tuple-element.63), channel_id=1, source_target_pairs={{0,2},{1,3},{2,0},{3,1},{4,6},{5,7},{6,4},{7,5},{8,10},{9,11},{10,... | collective-permute-start | bytes 1769480 | tf_op jit(solution)/shard_map/ppermute | solution.py:736
  374.7 26.0 %collective-permute-start.11 = (bf16[576,512]{1,0:T(8,128)(2,1)S(1)}, bf16[576,512]{1,0:T(8,128)(2,1)S(1)}, u32[]{:S(2)}, u32[]{:S(2)}) collective-permute-start(bf16[576,512]{1,0:T(8,128)(2,1)S(1)} %get-tuple-element.62), channel_id=1, source_target_pairs={{0,1},{1,0},{2,3},{3,2},{4,5},{5,4},{6,7},{7,6},{8,9},{9,8},{10,11... | collective-permute-start | bytes 1769480 | tf_op jit(solution)/shard_map/ppermute | solution.py:736
  414.4 5.9 collective-permute-start.15
  415.7 4.6 collective-permute-start.14
  420.4 54.5 %copy-start.9 = (f32[512,768]{1,0:T(8,128)S(1)}, f32[512,768]{1,0:T(8,128)}, u32[]{:S(2)}) copy-start(f32[512,768]{1,0:T(8,128)} %copy-done.8) | copy-start | bytes 4718596
  (75 other events, 454.8 us)

commit v2 on v1

--- a/solution.py
+++ b/solution.py
@@ -231,7 +231,15 @@
 
 
 QT = 256
+QF = 512
 FAR = -1e30
+
+def fold_rows(v, op):
+    while v.shape[0] > 8:
+        n = v.shape[0] // 2
+        v = op(v[:n], v[n:])
+    return v
+
 
 def fill_keys(seg_ref, blocks, kq_ref, q_ref):
     n = seg_ref.shape[1]
@@ -254,11 +262,11 @@
     def tile(i, unused):
         at = pl.ds(pl.multiple_of(i * QT, QT), QT)
         s = jnp.dot(k_s[...], q_s[:, at], preferred_element_type=jnp.float32)
-        peak = jnp.max(s, axis=0, keepdims=True)
+        peak = jnp.max(fold_rows(s, jnp.maximum), axis=0, keepdims=True)
         e = jnp.exp(s - peak)
-        denom = jnp.sum(e, axis=0, keepdims=True)
-        p = (e * (1.0 / denom)).astype(jnp.bfloat16)
-        o_ref[0, :, at] = jnp.dot(v_s[...], p, preferred_element_type=jnp.float32)
+        denom = jnp.sum(fold_rows(e, jnp.add), axis=0, keepdims=True)
+        o = jnp.dot(v_s[...], e.astype(jnp.bfloat16), preferred_element_type=jnp.float32)
+        o_ref[0, :, at] = o * (1.0 / denom)
         lse_ref[0, :, at] = peak + jnp.log(denom)
         return unused
 
@@ -338,261 +346,312 @@
 
 
 MESH = pl.DeviceIdType.MESH
+EVERY = slice(None)
+
 
 def spot():
     seq, head = lax.axis_index("seq"), lax.axis_index("head")
     return seq // 2, seq % 2, head // 2, head % 2
 
+
 def device(z, x, y, c):
     return {"seq": z * 2 + x, "head": y * 2 + c}
 
-def greet():
+
+def hail(where):
+    pl.semaphore_signal(pltpu.get_barrier_semaphore(), inc=1, device_id=where, device_id_type=MESH)
+
+
+def greet(plane=False, group=False, halo=False):
     z, x, y, c = spot()
-    barrier = pltpu.get_barrier_semaphore()
-    for where in (device(z, x, y, 1 - c), device(z, x, 1 - y, c), device(z, 1 - x, y, c)):
-        pl.semaphore_signal(barrier, inc=1, device_id=where, device_id_type=MESH)
-
-    @pl.when(z > 0)
-    def _():
-        pl.semaphore_signal(barrier, inc=1, device_id=device(z - 1, x, y, c), device_id_type=MESH)
-
-    @pl.when(z < 3)
-    def _():
-        pl.semaphore_signal(barrier, inc=1, device_id=device(z + 1, x, y, c), device_id_type=MESH)
-
-    pl.semaphore_wait(barrier, jnp.where((z == 0) | (z == 3), 4, 5))
-
-class Spread:
-    def __init__(self, own, whole, cut, x_first, send, recv):
-        self.own, self.whole, self.cut, self.x_first, self.send, self.recv = own, whole, cut, x_first, send, recv
-
-    def block(self, *lead):
-        return self.whole.at[tuple(lead) + self.cut]
-
-    def copy(self, src, dst, n, to):
+    if plane:
+        for n in range(1, 8):
+            hail(device(z, x ^ (n >> 2), y ^ ((n >> 1) & 1), c ^ (n & 1)))
+        for n in range(1, 4):
+            hail(device(z ^ n, x, y, c))
+        pl.semaphore_wait(pltpu.get_barrier_semaphore(), 10)
+        return
+    count = jnp.where((z == 0) | (z == 3), 4, 5)
+    hail(device(z, x, y, 1 - c))
+    hail(device(z, x, 1 - y, c))
+    hail(device(z, 1 - x, y, c))
+    pl.when(z > 0)(lambda: hail(device(z - 1, x, y, c)))
+    pl.when(z < 3)(lambda: hail(device(z + 1, x, y, c)))
+    if group:
+        hail(device(z, x, 1 - y, 1 - c))
+        count = count + 1
+    elif halo:
+        far = y != c
+        pl.when(far)(lambda: hail(device(z, x, 1 - y, 1 - c)))
+        count = count + jnp.where(far, 1, 0)
+    pl.semaphore_wait(pltpu.get_barrier_semaphore(), count)
+
+
+class Unit:
+    def remote(self, src, dst, n, to):
         return pltpu.make_async_remote_copy(
             src_ref=src, dst_ref=dst, send_sem=self.send.at[n], recv_sem=self.recv.at[n], device_id=to, device_id_type=MESH
         )
 
+    def landed(self, ref, n):
+        z, x, y, c = spot()
+        return self.remote(ref, ref, n, device(z, x, y, 1 - c))
+
+
+class Spread(Unit):
+    def __init__(self, own, whole, cut, order, send, recv):
+        self.own, self.whole, self.cut, self.order, self.send, self.recv = own, whole, cut, order, send, recv
+        self.steps = []
+        for at, axis in enumerate(order):
+            self.steps += [("z", 1), ("z", 2), ("z", 3)] if axis == "z" else [(axis, at)]
+        self.steps.append(("c", 3))
+
+    def block(self, at, **given):
+        z, x, y, c = spot()
+        here = {"z": z, "x": x, "y": y, "c": c}
+        done = self.order[:at]
+        lead = tuple(given[a] if a in given else (EVERY if a in done else here[a]) for a in "zxyc")
+        return self.whole.at[lead + self.cut]
+
+    def source(self, at, ref):
+        return self.own.at[self.cut] if at == 0 and self.cut else (self.own if at == 0 else ref)
+
     def up(self, k):
         z, x, y, c = spot()
-        ref = self.block(z - (k - 1), x, y, c)
-        src = self.own.at[self.cut] if k == 1 else ref
-        return (z < 3) & (z >= k - 1), self.copy(src, ref, k - 1, device(z + 1, x, y, c))
-
-    def up_landed(self, k):
-        z, x, y, c = spot()
-        ref = self.block(z - k, x, y, c)
-        return z >= k, self.copy(ref, ref, k - 1, device(z, x, y, 1 - c))
+        at = self.order.index("z")
+        ref = self.block(at, z=z - (k - 1))
+        src = self.source(at, ref) if k == 1 else ref
+        return (z < 3) & (z >= k - 1), self.remote(src, ref, k - 1, device(z + 1, x, y, c))
 
     def down(self, k):
         z, x, y, c = spot()
-        ref = self.block(z + (k - 1), x, y, c)
-        src = self.own.at[self.cut] if k == 1 else ref
-        return (z > 0) & (z + k - 1 <= 3), self.copy(src, ref, 2 + k, device(z - 1, x, y, c))
-
-    def down_landed(self, k):
+        at = self.order.index("z")
+        ref = self.block(at, z=z + (k - 1))
+        src = self.source(at, ref) if k == 1 else ref
+        return (z > 0) & (z + k - 1 <= 3), self.remote(src, ref, 2 + k, device(z - 1, x, y, c))
+
+    def came_up(self, k):
         z, x, y, c = spot()
-        ref = self.block(z + k, x, y, c)
-        return z + k <= 3, self.copy(ref, ref, 2 + k, device(z, x, y, 1 - c))
-
-    def side(self, which):
+        ref = self.block(self.order.index("z"), z=z - k)
+        return z >= k, self.landed(ref, k - 1)
+
+    def came_down(self, k):
         z, x, y, c = spot()
-        if which == 2:
-            return self.copy(self.block(slice(None), slice(None), slice(None), c), self.block(slice(None), slice(None), slice(None), c), 8, device(z, x, y, 1 - c)), None
-        over_x = self.x_first == (which == 0)
-        if which == 0:
-            mine = self.block(slice(None), x, y, c)
-        elif over_x:
-            mine = self.block(slice(None), x, slice(None), c)
+        ref = self.block(self.order.index("z"), z=z + k)
+        return z + k <= 3, self.landed(ref, 2 + k)
+
+    def swap(self, axis, at):
+        z, x, y, c = spot()
+        ref = self.block(at)
+        to = {"x": device(z, 1 - x, y, c), "y": device(z, x, 1 - y, c), "c": device(z, x, y, 1 - c)}[axis]
+        return self.remote(self.source(at, ref), ref, 6 + "xyc".index(axis), to)
+
+    def came_over(self, axis, at):
+        z, x, y, c = spot()
+        other = {"x": 1 - x, "y": 1 - y, "c": 1 - c}[axis]
+        return self.landed(self.block(at, **{axis: other}), 6 + "xyc".index(axis))
+
+    def start(self, step):
+        axis, k = step
+        if axis == "z":
+            for ok, copy in (self.up(k), self.down(k)):
+                pl.when(ok)(copy.start)
         else:
-            mine = self.block(slice(None), slice(None), y, c)
-        to = device(z, 1 - x, y, c) if over_x else device(z, x, 1 - y, c)
-        return self.copy(mine, mine, 6 + which, to), None
+            self.swap(axis, k).start()
+
+    def end(self, step):
+        axis, k = step
+        if axis == "z":
+            for ok, copy in (self.came_up(k), self.came_down(k)):
+                pl.when(ok)(copy.wait_recv)
+        else:
+            self.came_over(axis, k).wait_recv()
 
     def stage(self, n):
-        if n == 0:
+        z, x, y, c = spot()
+        if n < 2:
+            local = pltpu.make_async_copy(self.source(0, None), self.block(0), self.recv.at[9])
+            local.start() if n == 0 else local.wait()
+        if n > 0:
+            self.end(self.steps[n - 1])
+        if n < len(self.steps):
+            self.start(self.steps[n])
+
+    stages = 7
+
+    def finish(self):
+        for axis, k in self.steps:
+            if axis == "z":
+                for ok, copy in (self.up(k), self.down(k)):
+                    pl.when(ok)(copy.wait_send)
+            else:
+                self.swap(axis, k).wait_send()
+
+
+def add_rows(dst, src):
+    dst[...] = (dst[...].astype(jnp.float32) + src[...].astype(jnp.float32)).astype(dst.dtype)
+
+
+class Collect(Unit):
+    def __init__(self, parts, out, cut, order, own, rc, r1, r2, rz, send, recv):
+        self.parts, self.out, self.cut, self.order, self.send, self.recv = parts, out, cut, order, send, recv
+        self.own, self.rc, self.r1, self.r2, self.rz = own, rc, r1, r2, rz
+        self.steps = [("c", 0)]
+        for at, axis in enumerate(order):
+            self.steps += [("z", 1), ("z", 2), ("z", 3)] if axis == "z" else [(axis, at)]
+
+    def block(self, *lead):
+        if self.own is None:
             z, x, y, c = spot()
-            self.local = pltpu.make_async_copy(self.own.at[self.cut], self.block(z, x, y, c), self.recv.at[9])
-            self.local.start()
-            for ok, copy in (self.up(1), self.down(1)):
-                pl.when(ok)(copy.start)
-        elif n in (1, 2):
-            for landed, onward in ((self.up_landed, self.up), (self.down_landed, self.down)):
-                ok, copy = landed(n)
-                pl.when(ok)(copy.wait_recv)
-                ok, copy = onward(n + 1)
-                pl.when(ok)(copy.start)
-        elif n == 3:
-            for landed in (self.up_landed, self.down_landed):
-                ok, copy = landed(3)
-                pl.when(ok)(copy.wait_recv)
-            self.local.wait()
-            self.side(0)[0].start()
-        elif n in (4, 5):
-            self.side(n - 4)[0].wait_recv()
-            self.side(n - 3)[0].start()
-        elif n == 6:
-            self.side(2)[0].wait_recv()
-
-    def finish(self):
-        for k in (1, 2, 3):
-            for ok, copy in (self.up(k), self.down(k)):
-                pl.when(ok)(copy.wait_send)
-        for which in range(3):
-            self.side(which)[0].wait_send()
-
-def gather_kernel(plan, n_in, *refs):
-    owns, wholes, send, recv = refs[:n_in], refs[n_in : 2 * n_in], refs[2 * n_in], refs[2 * n_in + 1]
-    greet()
-    units = [Spread(owns[i], wholes[i], cut, x_first, send.at[n], recv.at[n]) for n, (i, cut, x_first) in enumerate(plan)]
-    pairs = [units[i : i + 2] for i in range(0, len(units), 2)]
-    for t in range(len(pairs) + 6):
-        for n in (3, 4, 5, 6, 2, 1, 0):
-            if 0 <= t - n < len(pairs):
-                for unit in pairs[t - n]:
-                    unit.stage(n)
-    for unit in units:
-        unit.finish()
-
-def gather_all(shards, plan, collective_id=1):
-    n = len(shards)
-    return pl.pallas_call(
-        functools.partial(gather_kernel, plan, n),
-        in_specs=[pl.BlockSpec(memory_space=pl.ANY)] * n,
-        out_specs=[pl.BlockSpec(memory_space=pl.ANY)] * n,
-        out_shape=[jax.ShapeDtypeStruct((4, 2, 2, 2) + s.shape, s.dtype) for s in shards],
-        scratch_shapes=[pltpu.SemaphoreType.DMA((len(plan), 9)), pltpu.SemaphoreType.DMA((len(plan), 10))],
-        compiler_params=pltpu.CompilerParams(collective_id=collective_id, has_side_effects=True),
-    )(*shards)
-
-
-def greet_plane():
-    z, x, y, c = spot()
-    barrier = pltpu.get_barrier_semaphore()
-    for n in range(1, 8):
-        pl.semaphore_signal(barrier, inc=1, device_id=device(z, x ^ (n >> 2), y ^ ((n >> 1) & 1), c ^ (n & 1)), device_id_type=MESH)
-    for n in range(1, 4):
-        pl.semaphore_signal(barrier, inc=1, device_id=device(z ^ n, x, y, c), device_id_type=MESH)
-    pl.semaphore_wait(barrier, 10)
-
-
-def add_into(dst, src, lead):
-    def one(i, unused):
-        for n in range(lead[1]):
-            for m in range(lead[2]):
-                d, s = dst(i, n, m), src(i, n, m)
-                d[...] = (d[...].astype(jnp.float32) + s[...].astype(jnp.float32)).astype(d.dtype)
-        return unused
-
-    lax.fori_loop(0, lead[0], one, 0)
-
-
-class Collect:
-    def __init__(self, parts, out, cut, x_first, bufs, send, recv):
-        self.parts, self.out, self.cut, self.x_first, self.send, self.recv = parts, out, cut, x_first, send, recv
-        self.own, self.rc, self.r1, self.r2, self.rz = bufs
-
-    def copy(self, src, dst, n, to):
-        return pltpu.make_async_remote_copy(
-            src_ref=src, dst_ref=dst, send_sem=self.send.at[n], recv_sem=self.recv.at[n], device_id=to, device_id_type=MESH
-        )
+            return self.parts.at[tuple(lead) + (c,) + self.cut]
+        return self.own.at[tuple(lead)]
+
+    def lead(self, at, **given):
+        z, x, y, c = spot()
+        here = {"z": z, "x": x, "y": y}
+        done = self.order[:at]
+        return tuple(given[a] if a in given else (here[a] if a in done else EVERY) for a in "zxy")
+
+    def swap(self, axis, at):
+        z, x, y, c = spot()
+        if axis == "c":
+            return self.remote(self.parts.at[(EVERY, EVERY, EVERY, 1 - c) + self.cut], self.rc, 0, device(z, x, y, 1 - c))
+        other = {"x": 1 - x, "y": 1 - y}[axis]
+        to = {"x": device(z, 1 - x, y, c), "y": device(z, x, 1 - y, c)}[axis]
+        return self.remote(self.block(*self.lead(at, **{axis: other})), self.r1 if at == 0 else self.r2, 1 + min(at, 1), to)
 
     def load(self):
         z, x, y, c = spot()
-        every = slice(None)
-        return pltpu.make_async_copy(self.parts.at[(every, every, every, c) + self.cut], self.own, self.recv.at[9])
-
-    def core(self):
+        return pltpu.make_async_copy(self.parts.at[(EVERY, EVERY, EVERY, c) + self.cut], self.own, self.recv.at[9])
+
+    def hop(self, k, rising):
         z, x, y, c = spot()
-        every = slice(None)
-        return self.copy(self.parts.at[(every, every, every, 1 - c) + self.cut], self.rc, 0, device(z, x, y, 1 - c))
-
-    def first(self):
+        at = self.order.index("z")
+        d = z + (4 - k) if rising else z - (4 - k)
+        ok = d <= 3 if rising else d >= 0
+        slot = 2 + k if rising else k - 1
+        to = device(z + 1, x, y, c) if rising else device(z - 1, x, y, c)
+        return ok, self.remote(self.block(*self.lead(at, z=jnp.clip(d, 0, 3))), self.rz.at[slot], 3 + slot, to)
+
+    def hopped(self, k, rising):
         z, x, y, c = spot()
-        if self.x_first:
-            return self.copy(self.own.at[:, 1 - x], self.r1, 1, device(z, 1 - x, y, c))
-        return self.copy(self.own.at[:, :, 1 - y], self.r1, 1, device(z, x, 1 - y, c))
-
-    def second(self):
+        d = z + (3 - k) if rising else z - (3 - k)
+        ok = (z > 0) & (d <= 3) if rising else (z < 3) & (d >= 0)
+        slot = 2 + k if rising else k - 1
+        return ok, jnp.clip(d, 0, 3), self.rz.at[slot], self.landed(self.rz.at[slot], 3 + slot)
+
+    def start(self, step):
+        axis, k = step
+        if axis == "z":
+            for rising in (False, True):
+                ok, copy = self.hop(k, rising)
+                pl.when(ok)(copy.start)
+        else:
+            self.swap(axis, k).start()
+            if axis == "c" and self.own is not None:
+                self.load().start()
+
+    def end(self, step, last):
         z, x, y, c = spot()
-        if self.x_first:
-            return self.copy(self.own.at[:, x, 1 - y], self.r2, 2, device(z, x, 1 - y, c))
-        return self.copy(self.own.at[:, 1 - x, y], self.r2, 2, device(z, 1 - x, y, c))
-
-    def down(self, k):
-        z, x, y, c = spot()
-        d = z - (4 - k)
-        return d >= 0, self.copy(self.own.at[jnp.maximum(d, 0), x, y], self.rz.at[k - 1], 2 + k, device(z - 1, x, y, c))
-
-    def down_landed(self, k):
-        z, x, y, c = spot()
-        d = z - (3 - k)
-        ref = self.rz.at[k - 1]
-        return (z < 3) & (d >= 0), d, ref, self.copy(ref, ref, 2 + k, device(z, x, y, 1 - c))
-
-    def up(self, k):
-        z, x, y, c = spot()
-        d = z + (4 - k)
-        return d <= 3, self.copy(self.own.at[jnp.minimum(d, 3), x, y], self.rz.at[2 + k], 5 + k, device(z + 1, x, y, c))
-
-    def up_landed(self, k):
-        z, x, y, c = spot()
-        d = z + (3 - k)
-        ref = self.rz.at[2 + k]
-        return (z > 0) & (d <= 3), d, ref, self.copy(ref, ref, 5 + k, device(z, x, y, 1 - c))
-
-    def stage(self, n):
-        z, x, y, c = spot()
-        if n == 0:
-            self.core().start()
-            self.load().start()
-        elif n == 1:
-            self.core().wait_recv()
-            self.load().wait()
-            add_into(lambda i, j, k: self.own.at[i, j, k], lambda i, j, k: self.rc.at[i, j, k], (4, 2, 2))
-            self.first().start()
-        elif n == 2:
-            self.first().wait_recv()
-            if self.x_first:
-                add_into(lambda i, j, k: self.own.at[i, x, j], lambda i, j, k: self.r1.at[i, j], (4, 2, 1))
-            else:
-                add_into(lambda i, j, k: self.own.at[i, j, y], lambda i, j, k: self.r1.at[i, j], (4, 2, 1))
-            self.second().start()
-        elif n == 3:
-            self.second().wait_recv()
-            add_into(lambda i, j, k: self.own.at[i, x, y], lambda i, j, k: self.r2.at[i], (4, 1, 1))
-            for ok, copy in (self.down(1), self.up(1)):
-                pl.when(ok)(copy.start)
-        elif n in (4, 5):
-            for landed, onward in ((self.down_landed, self.down), (self.up_landed, self.up)):
-                ok, d, ref, copy = landed(n - 3)
+        axis, k = step
+        if axis == "z":
+            at = self.order.index("z")
+            pair = "x" if "x" not in self.order[:at] else ("y" if "y" not in self.order[:at] else None)
+            for rising in (False, True):
+                ok, d, ref, copy = self.hopped(k, rising)
 
                 @pl.when(ok)
                 def _(d=d, ref=ref, copy=copy):
                     copy.wait_recv()
-                    own = self.own.at[jnp.clip(d, 0, 3), x, y]
-                    own[...] = (own[...].astype(jnp.float32) + ref[...].astype(jnp.float32)).astype(own.dtype)
-
-                ok, copy = onward(n - 2)
-                pl.when(ok)(copy.start)
-        elif n == 6:
+                    for n in range(2 if pair else 1):
+                        given = {"z": d, pair: n} if pair else {"z": d}
+                        add_rows(self.block(*self.lead(at, **given)), ref.at[n] if pair else ref)
+        elif axis == "c":
+            self.landed(self.rc, 0).wait_recv()
+            if self.own is not None:
+                self.load().wait()
+
+            def one(i, unused):
+                for n in range(2):
+                    for m in range(2):
+                        add_rows(self.block(i, n, m), self.rc.at[i, n, m])
+                return unused
+
+            lax.fori_loop(0, 4, one, 0)
+        else:
+            ref = self.r1 if k == 0 else self.r2
+            self.landed(ref, 1 + min(k, 1)).wait_recv()
+            here = {"x": x, "y": y}[axis]
+            rest = [a for a in "zxy" if a not in self.order[: k + 1]]
+            if not rest:
+                add_rows(self.block(z, x, y), ref)
+            else:
+
+                def one(i, unused):
+                    for n in range(2 if len(rest) == 2 else 1):
+                        given = {"z": i, axis: here}
+                        if len(rest) == 2:
+                            given[rest[1]] = n
+                        add_rows(self.block(*self.lead(k, **given)), ref.at[i, n] if len(rest) == 2 else ref.at[i])
+                    return unused
+
+                lax.fori_loop(0, 4, one, 0)
+        if last:
             out = self.out.at[self.cut] if self.cut else self.out
-            out[...] = self.own[z, x, y].astype(jnp.float32)
-            for landed in (self.down_landed, self.up_landed):
-                ok, d, ref, copy = landed(3)
-
-                @pl.when(ok)
-                def _(ref=ref, copy=copy):
-                    copy.wait_recv()
-                    out[...] += ref[...].astype(jnp.float32)
+            out[...] = self.block(z, x, y)[...].astype(jnp.float32)
+
+    stages = 7
+
+    def stage(self, n):
+        if n > 0:
+            self.end(self.steps[n - 1], n == len(self.steps))
+        if n < len(self.steps):
+            self.start(self.steps[n])
 
     def finish(self):
-        for copy in (self.core(), self.first(), self.second()):
-            copy.wait_send()
-        for k in (1, 2, 3):
-            for ok, copy in (self.down(k), self.up(k)):
-                pl.when(ok)(copy.wait_send)
+        for axis, k in self.steps:
+            if axis == "z":
+                for rising in (False, True):
+                    ok, copy = self.hop(k, rising)
+                    pl.when(ok)(copy.wait_send)
+            else:
+                self.swap(axis, k).wait_send()
+
+
+def unit_shape(shape, cut):
+    cut = tuple(cut) + (slice(None),) * (len(shape) - len(cut))
+    return tuple(len(range(*s.indices(d))) for s, d in zip(cut, shape))
+
+
+def collect_scratch(plan, shapes, dtype, inside):
+    scratch = []
+    for i, cut, order in plan:
+        m = unit_shape(shapes[i], cut)
+        leads = [] if i in inside else [(4, 2, 2)]
+        leads += [(4, 2, 2), (4, 2), () if order[1] == "z" else (4,), (6, 2) if order[1] == "z" else (6,)]
+        scratch += [pltpu.VMEM(lead + m, dtype) for lead in leads]
+    return scratch
+
+
+def collect_units(plan, parts, outs, bufs, inside, send, recv):
+    units, bufs = [], list(bufs)
+    for n, (i, cut, order) in enumerate(plan):
+        own = None if i in inside else bufs.pop(0)
+        units.append(Collect(parts[i], outs[i], cut, order, own, bufs.pop(0), bufs.pop(0), bufs.pop(0), bufs.pop(0), send.at[n], recv.at[n]))
+    return units
+
+
+def waves(units, width=2):
+    rows = [units[i : i + width] for i in range(0, len(units), width)]
+    steps = []
+    for t in range(len(rows) + 6):
+        steps.append([(unit, n) for n in (3, 4, 5, 6, 2, 1, 0) if 0 <= t - n < len(rows) for unit in rows[t - n]])
+    return steps
+
+
+def go(step):
+    for unit, n in step:
+        unit.stage(n)
 
 
 def square_sum(refs, tile):
@@ -605,109 +664,572 @@
             tile[...] += v[:, i : i + 128]
 
 
-def total_square(outs, norm, tiles, send, recv):
+def total_square(norm, tiles, send, recv):
     z, x, y, c = spot()
     mine = x * 4 + y * 2 + c
-    square_sum(outs, tiles.at[mine])
     copies = []
+
+    def push(slot, n, to):
+        copies.append(pltpu.make_async_remote_copy(
+            src_ref=tiles.at[slot], dst_ref=tiles.at[slot], send_sem=send.at[n], recv_sem=recv.at[n], device_id=to, device_id_type=MESH))
+        copies[-1].start()
+
+    def pull(slot, n):
+        ref = tiles.at[slot]
+        pltpu.make_async_remote_copy(
+            src_ref=ref, dst_ref=ref, send_sem=send.at[n], recv_sem=recv.at[n], device_id=device(z, x, y, 1 - c), device_id_type=MESH).wait_recv()
+
     for n in range(1, 8):
-        to = device(z, x ^ (n >> 2), y ^ ((n >> 1) & 1), c ^ (n & 1))
-        copies.append(pltpu.make_async_remote_copy(
-            src_ref=tiles.at[mine], dst_ref=tiles.at[mine], send_sem=send.at[n], recv_sem=recv.at[n], device_id=to, device_id_type=MESH))
-        copies[-1].start()
+        push(mine, n, device(z, x ^ (n >> 2), y ^ ((n >> 1) & 1), c ^ (n & 1)))
     for n in range(1, 8):
-        ref = tiles.at[mine ^ n]
-        pltpu.make_async_remote_copy(src_ref=ref, dst_ref=ref, send_sem=send.at[n], recv_sem=recv.at[n], device_id=device(z, x, y, 1 - c), device_id_type=MESH).wait_recv()
+        pull(mine ^ n, n)
     total = tiles[0]
     for n in range(1, 8):
         total = total + tiles[n]
     tiles[8 + z] = total
     for n in range(1, 4):
-        copies.append(pltpu.make_async_remote_copy(
-            src_ref=tiles.at[8 + z], dst_ref=tiles.at[8 + z], send_sem=send.at[7 + n], recv_sem=recv.at[7 + n], device_id=device(z ^ n, x, y, c), device_id_type=MESH))
-        copies[-1].start()
+        push(8 + z, 7 + n, device(z ^ n, x, y, c))
     for n in range(1, 4):
-        ref = tiles.at[8 + (z ^ n)]
-        pltpu.make_async_remote_copy(src_ref=ref, dst_ref=ref, send_sem=send.at[7 + n], recv_sem=recv.at[7 + n], device_id=device(z, x, y, 1 - c), device_id_type=MESH).wait_recv()
+        pull(8 + (z ^ n), 7 + n)
     norm[...] = (tiles[8] + tiles[9]) + (tiles[10] + tiles[11])
     for copy in copies:
         copy.wait_send()
 
 
-def unit_shape(shape, cut):
-    cut = tuple(cut) + (slice(None),) * (len(shape) - len(cut))
-    return tuple(len(range(*s.indices(d))) for s, d in zip(cut, shape))
-
-
-def collect_kernel(plan, n_in, *refs):
-    parts, outs, norm = refs[:n_in], refs[n_in : 2 * n_in], refs[2 * n_in]
-    send, recv, tiles, nsend, nrecv = refs[2 * n_in + 1 : 2 * n_in + 6]
-    bufs = refs[2 * n_in + 6 :]
-    greet_plane()
-    units = [
-        Collect(parts[i], outs[i], cut, x_first, bufs[5 * n : 5 * n + 5], send.at[n], recv.at[n])
-        for n, (i, cut, x_first) in enumerate(plan)
-    ]
-    pairs = [units[i : i + 2] for i in range(0, len(units), 2)]
-    for t in range(len(pairs) + 6):
-        for n in range(7):
-            if 0 <= t - n < len(pairs):
-                for unit in pairs[t - n]:
-                    unit.stage(n)
+def take_rows(win_ref, g, cut):
+    return gapped(take_group(win_ref, g), cut)
+
+
+def halo_copies(edges_ref, win_ref, send, recv):
+    z, x, y, c = spot()
+    h = y * 2 + c
+    n = edges_ref.shape[0]
+
+    def to(other):
+        return {"seq": z * 2 + x, "head": other}
+
+    def copy(src, dst, k, other):
+        return pltpu.make_async_remote_copy(
+            src_ref=src, dst_ref=dst, send_sem=send.at[k], recv_sem=recv.at[k], device_id=to(other), device_id_type=MESH)
+
+    after = copy(edges_ref.at[n - HALF : n], win_ref.at[0:HALF], 0, h + 1)
+    before = copy(edges_ref.at[0:HALF], win_ref.at[n + HALF : n + 2 * HALF], 1, h - 1)
+    from_before = copy(win_ref.at[0:HALF], win_ref.at[0:HALF], 0, h ^ 1)
+    from_after = copy(win_ref.at[n + HALF : n + 2 * HALF], win_ref.at[n + HALF : n + 2 * HALF], 1, h ^ 1)
+    return (h < 3, after), (h > 0, before), (h > 0, from_before), (h < 3, from_after)
+
+
+def halo_start(edges_ref, win_ref, send, recv):
+    for ok, copy in halo_copies(edges_ref, win_ref, send, recv)[:2]:
+        pl.when(ok)(copy.start)
+
+
+def halo_end(edges_ref, win_ref, send, recv):
+    n = edges_ref.shape[0]
+    after, before, from_before, from_after = halo_copies(edges_ref, win_ref, send, recv)
+    for (ok, copy), rows in ((from_before, slice(0, HALF)), (from_after, slice(n + HALF, n + 2 * HALF))):
+        pl.when(ok)(copy.wait_recv)
+
+        @pl.when(jnp.logical_not(ok))
+        def _(rows=rows):
+            win_ref[rows, :] = jnp.zeros((HALF, win_ref.shape[1]), win_ref.dtype)
+
+    for ok, copy in (after, before):
+        pl.when(ok)(copy.wait_send)
+
+
+def open_kernel(plan, n_in, early, *refs):
+    cut_ref, frames_ref = refs[:2]
+    owns = refs[2 : 2 + n_in]
+    out_ref, win_ref = refs[2 + n_in : 4 + n_in]
+    wholes = refs[4 + n_in : 4 + 2 * n_in]
+    cols_s, low_s, w_s, wp_s, send, recv, hsend, hrecv, wsem = refs[4 + 2 * n_in :]
+    cut = cut_ref[0]
+    greet(halo=True)
+    halo_start(frames_ref, win_ref, hsend, hrecv)
+    units = [Spread(owns[i], wholes[i], where, order, send.at[n], recv.at[n]) for n, (i, where, order) in enumerate(plan)]
+    steps = waves(units)
+    go(steps[0])
+    win_ref[HALF : HALF + OWN, :] = frames_ref[...]
+    out_ref[...] = jnp.zeros_like(out_ref)
+    wp_s[...] = jnp.zeros_like(wp_s)
+    go(steps[1])
+    halo_end(frames_ref, win_ref, hsend, hrecv)
+
+    def columns(g, unused):
+        cols_s[g] = im2col(take_rows(win_ref, g, cut), ZROWS)
+        return unused
+
+    def load(half, z):
+        return pltpu.make_async_copy(wholes[0].at[z, :, :, :, 4 * half : 4 * half + 4], w_s.at[z], wsem.at[z])
+
+    def product(g):
+        z, x, y = g // 4, (g // 2) % 2, g % 2
+        for h in range(2):
+            for a in range(4):
+                wp_s[h * 128 + a * 32 : h * 128 + a * 32 + 24, :] = w_s[z, x, y, h, a]
+        return lax.dot_general(cols_s[g], wp_s[...], (((1,), (1,)), ((), ())), preferred_element_type=jnp.float32)
+
+    def low(g, unused):
+        low_s[g] = product(g)
+        return unused
+
+    def high(g, unused):
+        z = jnp.concatenate([low_s[g], product(g)], axis=1)
+        z = jnp.concatenate([z[:, 0:128], z[:, 256:384], z[:, 128:256], z[:, 384:512]], axis=1)
+        put_group(out_ref, g, pick_own(fold_out(z), cut))
+        return unused
+
+    t = 2
+    for chunk in range(4):
+        lax.fori_loop(4 * chunk, 4 * chunk + 4, columns, 0)
+        go(steps[t])
+        t += 1
+    done = 0
+    while t < len(steps) or done < 2:
+        if done < 2 and t - 1 - 6 >= early[done]:
+            for z in range(4):
+                load(done, z).start()
+            for z in range(4):
+                load(done, z).wait()
+                lax.fori_loop(4 * z, 4 * z + 4, (low, high)[done], 0)
+                if t < len(steps) and z % 2 == 1:
+                    go(steps[t])
+                    t += 1
+            done += 1
+        elif t < len(steps):
+            go(steps[t])
+            t += 1
     for unit in units:
         unit.finish()
-    total_square(outs, norm, tiles, nsend, nrecv)
-
-
-def collect_scratch(plan, shapes, dtype):
-    scratch = []
-    for i, cut, x_first in plan:
-        m = unit_shape(shapes[i], cut)
-        scratch += [pltpu.VMEM(lead + m, dtype) for lead in ((4, 2, 2), (4, 2, 2), (4, 2), (4,), (6,))]
-    return scratch
-
-
-def collect_all(parts, plan, collective_id=2):
+
+
+def open_step(cut, frames, shards, plan, early, collective_id=1):
+    n = len(shards)
+    vmem = pl.BlockSpec(memory_space=pltpu.VMEM)
+    anywhere = pl.BlockSpec(memory_space=pl.ANY)
+    return pl.pallas_call(
+        functools.partial(open_kernel, plan, n, early),
+        in_specs=[pl.BlockSpec(memory_space=pltpu.SMEM), vmem] + [anywhere] * n,
+        out_specs=[vmem, vmem] + [anywhere] * n,
+        out_shape=[jax.ShapeDtypeStruct((OWN, 768), jnp.float32), jax.ShapeDtypeStruct((WIN, 768), jnp.bfloat16)]
+        + [jax.ShapeDtypeStruct((4, 2, 2, 2) + s.shape, s.dtype) for s in shards],
+        scratch_shapes=[
+            pltpu.VMEM((16, ZROWS, 768), jnp.bfloat16),
+            pltpu.VMEM((16, ZROWS, 256), jnp.float32),
+            pltpu.VMEM((4, 2, 2, 2, 4, 24, 768), jnp.bfloat16),
+            pltpu.VMEM((256, 768), jnp.bfloat16),
+            pltpu.SemaphoreType.DMA((len(plan), 9)),
+            pltpu.SemaphoreType.DMA((len(plan), 10)),
+            pltpu.SemaphoreType.DMA((2,)),
+            pltpu.SemaphoreType.DMA((2,)),
+            pltpu.SemaphoreType.DMA((4,)),
+        ],
+        compiler_params=pltpu.CompilerParams(collective_id=collective_id, has_side_effects=True, vmem_limit_bytes=56 * 2**20),
+    )(cut, frames, *shards)
+
+
+HEADS_HERE = 3
+ROWS_HERE = 192 * HEADS_HERE
+
+
+def group_copy(src, dst, send, recv, other):
+    return pltpu.make_async_remote_copy(
+        src_ref=src, dst_ref=dst, send_sem=send, recv_sem=recv, device_id={"head": other}, device_id_type=MESH
+    )
+
+
+def spaced(steps, slots):
+    out = [[] for _ in range(slots)]
+    for t, step in enumerate(steps):
+        out[min(t * slots // max(len(steps), 1), slots - 1)].append(step)
+    return out
+
+
+def go_at(slot, by_slot):
+    for t, steps in enumerate(by_slot):
+        if steps:
+
+            @pl.when(slot == t)
+            def _(steps=steps):
+                for step in steps:
+                    go(step)
+
+
+def fill_heads(seg_ref, qkv_ref, h, k_s, q_s):
+    n = seg_ref.shape[1]
+    seg = seg_ref[...]
+    row = lax.broadcasted_iota(jnp.int32, (64, n), 0)
+    mark = jnp.where(row < 2, jnp.where(seg == row, 1.0, 0.0), 0.0)
+    push = jnp.where(row < 2, jnp.where(seg == row, 0.0, FAR), 0.0)
+    at = pl.multiple_of(h * 192, 64)
+    keys = qkv_ref[pl.ds(at + 64, 64), :].astype(jnp.float32)
+    k_s[...] = jnp.transpose(jnp.concatenate([keys, mark], axis=0)).astype(jnp.bfloat16)
+    queries = qkv_ref[pl.ds(at, 64), :].astype(jnp.float32) * 0.125
+    q_s[...] = jnp.concatenate([queries, push], axis=0).astype(jnp.bfloat16)
+
+
+def attend_kernel(plan, n_in, *refs):
+    seg_ref, packed_ref = refs[:2]
+    owns = refs[2 : 2 + n_in]
+    qkv_ref, ctx_ref, lse_ref, o_ref = refs[2 + n_in : 6 + n_in]
+    wholes = refs[6 + n_in : 6 + 2 * n_in]
+    k_s, q_s, ctx_s, asend, arecv, csend, crecv, osem, send, recv = refs[6 + 2 * n_in :]
+    z, x, y, c = spot()
+    me = y * 2 + c
+    size = packed_ref.shape[1]
+    greet(group=True)
+
+    def bring(h, d):
+        return group_copy(
+            packed_ref.at[pl.ds((me ^ d) * ROWS_HERE + h * 192, 192)],
+            qkv_ref.at[pl.ds(h * 192, 192), d * size : d * size + size],
+            asend.at[h, d - 1], arecv.at[h, d - 1], me ^ d,
+        )
+
+    def give(h, d):
+        return group_copy(
+            ctx_s.at[pl.ds(h * 64, 64), d * size : d * size + size],
+            ctx_ref.at[pl.ds(me * 64 * HEADS_HERE + h * 64, 64)],
+            csend.at[h, d - 1], crecv.at[h, d - 1], me ^ d,
+        )
+
+    def given(h, d):
+        ref = ctx_ref.at[pl.ds((me ^ d) * 64 * HEADS_HERE + h * 64, 64)]
+        return group_copy(ref, ref, csend.at[h, d - 1], crecv.at[h, d - 1], me ^ d)
+
+    own = pltpu.make_async_copy(packed_ref.at[pl.ds(me * ROWS_HERE, ROWS_HERE)], qkv_ref.at[:, 0:size], osem)
+    own.start()
+    for h in range(HEADS_HERE):
+        for d in (2, 3, 1):
+            bring(h, d).start()
+    units = [Spread(owns[i], wholes[i], where, order, send.at[n], recv.at[n]) for n, (i, where, order) in enumerate(plan)]
+    steps = waves(units)
+    go(steps[0])
+    tiles = 4 * size // QF
+    by_slot = spaced(steps[1:], HEADS_HERE * tiles)
+    own.wait()
+
+    def head(h, unused):
+        for d in (1, 2, 3):
+            bring(h, d).wait_recv()
+        fill_heads(seg_ref, qkv_ref, h, k_s, q_s)
+
+        def tile(i, unused):
+            at = pl.ds(pl.multiple_of(i * QF, QF), QF)
+            s = jnp.dot(k_s[...], q_s[:, at], preferred_element_type=jnp.float32)
+            peak = jnp.max(fold_rows(s, jnp.maximum), axis=0, keepdims=True)
+            e = jnp.exp(s - peak)
+            denom = jnp.sum(fold_rows(e, jnp.add), axis=0, keepdims=True)
+            values = qkv_ref[pl.ds(pl.multiple_of(h * 192 + 128, 64), 64), :]
+            o = jnp.dot(values, e.astype(jnp.bfloat16), preferred_element_type=jnp.float32) * (1.0 / denom)
+            rows = pl.ds(pl.multiple_of(h * 64, 64), 64)
+            o_ref[rows, at] = o
+            ctx_s[rows, at] = o.astype(jnp.bfloat16)
+            lse_ref[h, :, at] = peak + jnp.log(denom)
+            go_at(h * tiles + i, by_slot)
+            return unused
+
+        lax.fori_loop(0, tiles, tile, 0)
+        for d in (2, 3, 1):
+            give(h, d).start()
+        ctx_ref[pl.ds(pl.multiple_of(me * 64 * HEADS_HERE + h * 64, 64), 64), :] = ctx_s[pl.ds(pl.multiple_of(h * 64, 64), 64), 0:size]
+        return unused
+
+    lax.fori_loop(0, HEADS_HERE, head, 0)
+    for h in range(HEADS_HERE):
+        for d in (1, 2, 3):
+            given(h, d).wait_recv()
+            give(h, d).wait_send()
+            bring(h, d).wait_send()
+    for unit in units:
+        unit.finish()
+
+
+def attend(seg, packed, shards, plan, collective_id=3):
+    n = len(shards)
+    size = packed.shape[1]
+    vmem = pl.BlockSpec(memory_space=pltpu.VMEM)
+    anywhere = pl.BlockSpec(memory_space=pl.ANY)
+    sem = pltpu.SemaphoreType.DMA
+    return pl.pallas_call(
+        functools.partial(attend_kernel, plan, n),
+        in_specs=[vmem, anywhere] + [anywhere] * n,
+        out_specs=[vmem] * 4 + [anywhere] * n,
+        out_shape=[
+            jax.ShapeDtypeStruct((ROWS_HERE, 4 * size), jnp.bfloat16),
+            jax.ShapeDtypeStruct((768, size), jnp.bfloat16),
+            jax.ShapeDtypeStruct((HEADS_HERE, 1, 4 * size), jnp.float32),
+            jax.ShapeDtypeStruct((64 * HEADS_HERE, 4 * size), jnp.float32),
+        ]
+        + [jax.ShapeDtypeStruct((4, 2, 2, 2) + s.shape, s.dtype) for s in shards],
+        scratch_shapes=[
+            pltpu.VMEM((4 * size, 128), jnp.bfloat16),
+            pltpu.VMEM((128, 4 * size), jnp.bfloat16),
+            pltpu.VMEM((64 * HEADS_HERE, 4 * size), jnp.bfloat16),
+            sem((3, 3)), sem((3, 3)), sem((3, 3)), sem((3, 3)), sem,
+            sem((max(len(plan), 1), 9)), sem((max(len(plan), 1), 10)),
+        ],
+        compiler_params=pltpu.CompilerParams(collective_id=collective_id, has_side_effects=True, vmem_limit_bytes=50 * 2**20),
+    )(seg, packed, *shards)
+
+
+def attend_back_kernel(plan, n_in, *refs):
+    seg_ref, qkv_ref, lse_ref, o_ref, gc_ref = refs[:5]
+    parts = refs[5 : 5 + n_in]
+    gp_ref, norm_ref = refs[5 + n_in : 7 + n_in]
+    outs = refs[7 + n_in : 7 + 2 * n_in]
+    k_s, q_s, v_s, do_s, dk_s, dv_s, dq_s, gp_s, asend, arecv, csend, crecv, osem, send, recv = refs[7 + 2 * n_in : 22 + 2 * n_in]
+    bufs = refs[22 + 2 * n_in :]
+    z, x, y, c = spot()
+    me = y * 2 + c
+    size = gc_ref.shape[1]
+    greet(group=True)
+
+    def bring(h, d):
+        return group_copy(
+            gc_ref.at[pl.ds((me ^ d) * 64 * HEADS_HERE + h * 64, 64)],
+            do_s.at[pl.ds(h * 64, 64), d * size : d * size + size],
+            asend.at[h, d - 1], arecv.at[h, d - 1], me ^ d,
+        )
+
+    def give(h, d):
+        return group_copy(
+            gp_s.at[pl.ds(h * 192, 192), d * size : d * size + size],
+            gp_ref.at[pl.ds(me * ROWS_HERE + h * 192, 192)],
+            csend.at[h, d - 1], crecv.at[h, d - 1], me ^ d,
+        )
+
+    def given(h, d):
+        ref = gp_ref.at[pl.ds((me ^ d) * ROWS_HERE + h * 192, 192)]
+        return group_copy(ref, ref, csend.at[h, d - 1], crecv.at[h, d - 1], me ^ d)
+
+    own = pltpu.make_async_copy(gc_ref.at[pl.ds(me * 64 * HEADS_HERE, 64 * HEADS_HERE)], do_s.at[:, 0:size], osem)
+    own.start()
+    for h in range(HEADS_HERE):
+        for d in (2, 3, 1):
+            bring(h, d).start()
+    units = collect_units(plan, parts, outs, bufs, (), send, recv)
+    steps = waves(units)
+    go(steps[0])
+    tiles = 4 * size // QT
+    by_slot = spaced(steps[1:], HEADS_HERE * tiles)
+    own.wait()
+
+    def head(h, unused):
+        for d in (1, 2, 3):
+            bring(h, d).wait_recv()
+        fill_heads(seg_ref, qkv_ref, h, k_s, q_s)
+        first = pl.multiple_of(h * 192, 64)
+        v_s[...] = jnp.transpose(qkv_ref[pl.ds(first + 128, 64), :].astype(jnp.float32)).astype(jnp.bfloat16)
+        dk_s[...] = jnp.zeros_like(dk_s)
+        dv_s[...] = jnp.zeros_like(dv_s)
+        rows = pl.ds(pl.multiple_of(h * 64, 64), 64)
+
+        def tile(i, unused):
+            at = pl.ds(pl.multiple_of(i * QT, QT), QT)
+            q = q_s[:, at]
+            do = do_s[rows, at]
+            delta = jnp.sum(do.astype(jnp.float32) * o_ref[rows, at], axis=0, keepdims=True)
+            s = jnp.dot(k_s[...], q, preferred_element_type=jnp.float32)
+            p = jnp.exp(s - lse_ref[h, :, at])
+            dp = jnp.dot(v_s[...], do, preferred_element_type=jnp.float32)
+            ds = (p * (dp - delta)).astype(jnp.bfloat16)
+            p = p.astype(jnp.bfloat16)
+            nt = (((1,), (1,)), ((), ()))
+            dv_s[...] += lax.dot_general(do, p, nt, preferred_element_type=jnp.float32)
+            dk_s[...] += lax.dot_general(q[:64], ds, nt, preferred_element_type=jnp.float32)
+            dq_s[:, at] = jnp.dot(qkv_ref[pl.ds(first + 64, 64), :], ds, preferred_element_type=jnp.float32) * 0.125
+            go_at(h * tiles + i, by_slot)
+            return unused
+
+        lax.fori_loop(0, tiles, tile, 0)
+        gp_s[pl.ds(first, 64), :] = dq_s[...].astype(jnp.bfloat16)
+        gp_s[pl.ds(first + 64, 64), :] = dk_s[...].astype(jnp.bfloat16)
+        gp_s[pl.ds(first + 128, 64), :] = dv_s[...].astype(jnp.bfloat16)
+        for d in (2, 3, 1):
+            give(h, d).start()
+        gp_ref[pl.ds(pl.multiple_of(me * ROWS_HERE + h * 192, 64), 192), :] = gp_s[pl.ds(first, 192), 0:size]
+        return unused
+
+    lax.fori_loop(0, HEADS_HERE, head, 0)
+    for h in range(HEADS_HERE):
+        for d in (1, 2, 3):
+            given(h, d).wait_recv()
+            give(h, d).wait_send()
+            bring(h, d).wait_send()
+    for unit in units:
+        unit.finish()
+    square_sum(outs, norm_ref)
+
+
+def attend_back(seg, qkv, lse, o, gc, parts, plan, collective_id=4):
+    n = len(parts)
+    size = gc.shape[1]
+    shapes = [p.shape[4:] for p in parts]
+    vmem = pl.BlockSpec(memory_space=pltpu.VMEM)
+    anywhere = pl.BlockSpec(memory_space=pl.ANY)
+    sem = pltpu.SemaphoreType.DMA
+    return pl.pallas_call(
+        functools.partial(attend_back_kernel, plan, n),
+        in_specs=[vmem] * 4 + [anywhere] + [anywhere] * n,
+        out_specs=[vmem] * 2 + [vmem] * n,
+        out_shape=[jax.ShapeDtypeStruct((4 * ROWS_HERE, size), jnp.bfloat16), jax.ShapeDtypeStruct((8, 128), jnp.float32)]
+        + [jax.ShapeDtypeStruct(s, jnp.float32) for s in shapes],
+        scratch_shapes=[
+            pltpu.VMEM((4 * size, 128), jnp.bfloat16),
+            pltpu.VMEM((128, 4 * size), jnp.bfloat16),
+            pltpu.VMEM((4 * size, 64), jnp.bfloat16),
+            pltpu.VMEM((64 * HEADS_HERE, 4 * size), jnp.bfloat16),
+            pltpu.VMEM((64, 4 * size), jnp.float32),
+            pltpu.VMEM((64, 4 * size), jnp.float32),
+            pltpu.VMEM((64, 4 * size), jnp.float32),
+            pltpu.VMEM((ROWS_HERE, 4 * size), jnp.bfloat16),
+            sem((3, 3)), sem((3, 3)), sem((3, 3)), sem((3, 3)), sem,
+            sem((len(plan), 9)), sem((len(plan), 10)),
+        ]
+        + collect_scratch(plan, shapes, jnp.bfloat16, ()),
+        compiler_params=pltpu.CompilerParams(collective_id=collective_id, has_side_effects=True, vmem_limit_bytes=58 * 2**20),
+    )(seg, qkv, lse, o, gc, *parts)
+
+
+def close_kernel(side_plan, main_plan, n_in, *refs):
+    cut_ref, win_ref, grad_ref, conv_ref, tile_ref = refs[:5]
+    parts = refs[5 : 5 + n_in]
+    dx_ref, norm_ref, conv_out = refs[5 + n_in : 8 + n_in]
+    outs = refs[8 + n_in : 8 + 2 * n_in]
+    (gwin_s, taps_s, dw_s, w_s, wp_s, tiles, send, recv, msend, mrecv, hsend, hrecv, nsend, nrecv, wsem) = refs[8 + 2 * n_in : 23 + 2 * n_in]
+    bufs = refs[23 + 2 * n_in :]
+    cut, last = cut_ref[0], cut_ref[1]
+    greet(plane=True)
+    halo_start(grad_ref, gwin_s, hsend, hrecv)
+    count = len(collect_scratch(side_plan, [o.shape for o in outs], jnp.bfloat16, ()))
+    side = collect_units(side_plan, parts, outs, bufs[:count], (), send, recv)
+    main = collect_units(main_plan, [dw_s], [conv_out], bufs[count:], (0,), msend, mrecv)
+    side_steps, main_steps = waves(side), waves(main)
+    go(side_steps[0])
+    gwin_s[HALF : HALF + OWN, :] = grad_ref[...]
+    dx_ref[...] = jnp.zeros_like(dx_ref)
+    wp_s[...] = jnp.zeros_like(wp_s)
+    halo_end(grad_ref, gwin_s, hsend, hrecv)
+
+    def load(z):
+        return pltpu.make_async_copy(conv_ref.at[z], w_s.at[z % 2], wsem.at[z % 2])
+
+    load(0).start()
+    load(1).start()
+    begin = jnp.where(cut <= HALF, 2 * HALF, HALF)
+    end = jnp.where(last > 0, EXT, jnp.where(cut <= HALF + OWN, OWN + 2 * HALF, OWN + HALF))
+
+    def weights(g, unused):
+        taps = taps_of(take_rows(gwin_s, g, cut))
+        taps_s[g] = taps
+        row = lax.broadcasted_iota(jnp.int32, (ZROWS, 512), 0) + HALF
+        own = jnp.where((row >= begin) & (row < end), taps[HALF : HALF + ZROWS].astype(jnp.float32), 0.0).astype(jnp.bfloat16)
+        cols = im2col(take_rows(win_ref, g, cut), ZROWS)
+        dw = lax.dot_general(own, cols, (((0,), (0,)), ((), ())), preferred_element_type=jnp.float32).astype(jnp.bfloat16)
+        for h in range(2):
+            for a in range(8):
+                dw_s[g // 4, (g // 2) % 2, g % 2, h, a] = dw[h * 256 + a * 32 : h * 256 + a * 32 + 24]
+        return unused
+
+    def inputs(g, unused):
+        z, x, y = g // 4, (g // 2) % 2, g % 2
+        for h in range(2):
+            for a in range(8):
+                wp_s[h * 256 + a * 32 : h * 256 + a * 32 + 24, :] = w_s[z % 2, x, y, h, a]
+        out = jnp.dot(taps_s[g], wp_s[...], preferred_element_type=jnp.float32)
+        put_group(dx_ref, g, pick_own(fold_back(out), cut))
+        return unused
+
+    by_slot = spaced(side_steps[1:], 8)
+    for k in range(8):
+        lax.fori_loop(2 * k, 2 * k + 2, weights, 0)
+        for step in by_slot[k]:
+            go(step)
+    by_slot = spaced(main_steps, 8)
+    for k in range(8):
+        for step in by_slot[k]:
+            go(step)
+        if k % 2 == 0:
+            load(k // 2).wait()
+        lax.fori_loop(2 * k, 2 * k + 2, inputs, 0)
+        if k % 2 == 1 and k < 4:
+            load(k // 2 + 2).start()
+    for unit in side + main:
+        unit.finish()
+    z, x, y, c = spot()
+    mine = tiles.at[x * 4 + y * 2 + c]
+    square_sum([conv_out] + list(outs), mine)
+    mine[...] += tile_ref[...]
+    total_square(norm_ref, tiles, nsend, nrecv)
+
+
+def close_step(cut, window, grad, conv, tile, parts, side_plan, main_plan, collective_id=2):
     n = len(parts)
     shapes = [p.shape[4:] for p in parts]
+    vmem = pl.BlockSpec(memory_space=pltpu.VMEM)
+    anywhere = pl.BlockSpec(memory_space=pl.ANY)
+    sem = pltpu.SemaphoreType.DMA
+    low = jnp.bfloat16
     return pl.pallas_call(
-        functools.partial(collect_kernel, plan, n),
-        in_specs=[pl.BlockSpec(memory_space=pl.ANY)] * n,
-        out_specs=[pl.BlockSpec(memory_space=pltpu.VMEM)] * (n + 1),
-        out_shape=[jax.ShapeDtypeStruct(s, jnp.float32) for s in shapes] + [jax.ShapeDtypeStruct((8, 128), jnp.float32)],
-        scratch_shapes=[pltpu.SemaphoreType.DMA((len(plan), 9)), pltpu.SemaphoreType.DMA((len(plan), 10)),
-                        pltpu.VMEM((12, 8, 128), jnp.float32), pltpu.SemaphoreType.DMA((11,)), pltpu.SemaphoreType.DMA((11,))]
-        + collect_scratch(plan, shapes, parts[0].dtype),
+        functools.partial(close_kernel, side_plan, main_plan, n),
+        in_specs=[pl.BlockSpec(memory_space=pltpu.SMEM), vmem, vmem, anywhere, vmem] + [anywhere] * n,
+        out_specs=[vmem] * (3 + n),
+        out_shape=[
+            jax.ShapeDtypeStruct((OWN, 768), jnp.float32),
+            jax.ShapeDtypeStruct((8, 128), jnp.float32),
+            jax.ShapeDtypeStruct(conv.shape[4:], jnp.float32),
+        ]
+        + [jax.ShapeDtypeStruct(s, jnp.float32) for s in shapes],
+        scratch_shapes=[
+            pltpu.VMEM((WIN, 768), low),
+            pltpu.VMEM((16, EXT, 512), low),
+            pltpu.VMEM(conv.shape, low),
+            pltpu.VMEM((2,) + conv.shape[1:], low),
+            pltpu.VMEM((512, 768), low),
+            pltpu.VMEM((12, 8, 128), jnp.float32),
+            sem((len(side_plan), 9)), sem((len(side_plan), 10)), sem((len(main_plan), 9)), sem((len(main_plan), 10)),
+            sem((2,)), sem((2,)), sem((11,)), sem((11,)), sem((2,)),
+        ]
+        + collect_scratch(side_plan, shapes, low, ())
+        + collect_scratch(main_plan, [conv.shape[4:]], low, (0,)),
         compiler_params=pltpu.CompilerParams(collective_id=collective_id, has_side_effects=True, vmem_limit_bytes=60 * 2**20),
-    )(*parts)
+    )(cut, window, grad, conv, tile, *parts)
 
 
 S = slice
 
 
-def gather_plan():
-    plan = []
-    for a in range(0, 8, 2):
-        plan += [(0, (S(a, a + 1),), False), (0, (S(a + 1, a + 2),), True)]
-    plan += [(1, (S(None), S(0, 1152)), False), (1, (S(None), S(1152, 2304)), True)]
-    plan += [(2, (S(None), S(0, 384)), False), (2, (S(None), S(384, 768)), True)]
-    for i in range(0, 3072, 1536):
-        plan += [(3, (S(None), S(i, i + 768)), False), (3, (S(None), S(i + 768, i + 1536)), True)]
-    plan += [(4, (S(0, 32),), False), (4, (S(32, 64),), True), (4, (S(64, 96),), False), (5, (), True)]
-    return plan
-
-
-def collect_plan():
-    plan = [(4, (S(0, 32),), False), (4, (S(32, 64),), True), (4, (S(64, 96),), False)]
-    for i in range(4):
-        plan.append((3, (S(None), S(768 * i, 768 * i + 768)), i % 2 == 0))
-    plan.append((2, (), True))
-    for i in range(3):
-        plan.append((1, (S(None), S(768 * i, 768 * i + 768)), i % 2 == 0))
-    for a in range(0, 8, 2):
-        plan += [(0, (S(a, a + 1),), True), (0, (S(a + 1, a + 2),), False)]
-    plan.append((5, (), False))
-    return plan
+def sliced(index, axis, size, count, orders, first=0):
+    step = size // count
+    return [
+        (index, (S(None),) * axis + (S(step * i, step * i + step),), orders[(first + i) % len(orders)]) for i in range(count)
+    ]
+
+
+GATHER = ("zxy", "zyx", "xzy", "yzx")
+REDUCE = ("yxz", "xyz", "yzx", "xzy")
+
+
+def open_plan():
+    return sliced(0, 0, 8, 8, GATHER) + sliced(1, 1, 2304, 2, GATHER) + [(3, (), "zxy"), (2, (), "yzx")]
+
+
+def attend_plan():
+    return sliced(0, 1, 3072, 4, GATHER) + sliced(1, 0, 96, 3, GATHER[1:])
+
+
+def attend_back_plan():
+    return sliced(2, 0, 96, 3, REDUCE) + sliced(1, 1, 3072, 4, REDUCE, 3) + [(0, (), "yxz")]
+
+
+def side_plan():
+    return sliced(0, 1, 2304, 3, REDUCE) + [(1, (), "xyz")]
+
+
+def main_plan():
+    return sliced(0, 0, 8, 8, REDUCE)
 
 
 def by_chips():
@@ -715,20 +1237,19 @@
 
 
 def gather_weights(parts):
-    if by_chips():
-        return [w.reshape((32,) + w.shape[4:]) for w in gather_all(parts, gather_plan())]
     return [lax.all_gather(p, ("seq", "head"), axis=0) for p in parts]
 
 
 def collect_grads(parts):
-    if by_chips():
-        outs = collect_all([p.reshape((4, 2, 2, 2) + p.shape[1:]) for p in parts], collect_plan())
-        return outs[:-1], jnp.sum(outs[-1])
     outs = [lax.psum_scatter(p.astype(jnp.float32), ("seq", "head"), scatter_dimension=0, tiled=False) for p in parts]
     square = jnp.zeros((), jnp.float32)
     for out in outs:
         square = square + jnp.sum(out * out)
     return outs, lax.psum(square, ("seq", "head"))
+
+
+def by_owner(part):
+    return part.reshape((4, 2, 2, 2) + part.shape[1:])
 
 
 def trade(pieces):
@@ -764,27 +1285,34 @@
     conv_low = conv_weight.astype(low_type).reshape(16, 8, conv_rows, group_width).transpose(1, 2, 0, 3).reshape(8, conv_rows, 768)
     small = jnp.concatenate([bias_gains.astype(low_type).reshape(-1), ffn_bias.astype(low_type)])
     small = jnp.pad(small, (0, 2048 - small.shape[0])).reshape(16, 128)
-    all_conv, all_qkv, all_proj, all_up, all_down, all_small = gather_weights(
-        [conv_low, qkv_weight.astype(low_type), proj_weight.astype(low_type), up_weight.astype(low_type), down_weight.astype(low_type), small]
-    )
-    full_qkv = all_qkv.reshape(model_width, -1)
-    full_proj = all_proj.reshape(model_width, -1)
-    full_up = all_up.reshape(model_width, -1)
-    full_down = all_down.reshape(-1, model_width)
-    full_conv = all_conv.reshape(16, 2, 24 // conv_rows, 8, conv_rows, 768).transpose(0, 1, 3, 2, 4, 5).reshape(16, 2, 8, 24, 768)
-    all_small = all_small.reshape(count, 2048).astype(f32)
-    vectors = all_small[:, : vec_rows * vec_cols].reshape(count, vec_rows, vec_cols).transpose(1, 0, 2).reshape(vec_rows, model_width)
-    full_ffn = all_small[:, vec_rows * vec_cols : vec_rows * vec_cols + ffn_cols].reshape(-1)
-
+    own_parts = [
+        conv_low, qkv_weight.astype(low_type), proj_weight.astype(low_type), up_weight.astype(low_type), down_weight.astype(low_type), small
+    ]
     seg_group = segment_ids[0]
     half_kernel = kernel_len // 2
     boundary = jnp.sum((seg_group == 0).astype(jnp.int32))
     cut = jnp.clip(boundary - head_index * row_count + half_kernel, 0, row_count + kernel_len)
     cut = jnp.stack([cut, (head_index == head_groups - 1).astype(jnp.int32)]).astype(jnp.int32)
+    if by_chips():
+        early = own_parts[:3] + own_parts[5:]
+        conv_pre, window, *parts = open_step(cut, frames, early, open_plan(), (1, 3))
+        all_conv, all_qkv, all_proj, all_small = [w.reshape((32,) + w.shape[4:]) for w in parts]
+        whole_conv = parts[0]
+    else:
+        all_conv, all_qkv, all_proj, all_up, all_down, all_small = gather_weights(own_parts)
+    full_qkv = all_qkv.reshape(model_width, -1)
+    full_proj = all_proj.reshape(model_width, -1)
+    full_conv = all_conv.reshape(16, 2, 24 // conv_rows, 8, conv_rows, 768).transpose(0, 1, 3, 2, 4, 5).reshape(16, 2, 8, 24, 768)
+    all_small = all_small.reshape(count, 2048).astype(f32)
+    vectors = all_small[:, : vec_rows * vec_cols].reshape(count, vec_rows, vec_cols).transpose(1, 0, 2).reshape(vec_rows, model_width)
+    full_ffn = all_small[:, vec_rows * vec_cols : vec_rows * vec_cols + ffn_cols].reshape(-1)
+
     seg_rows = jnp.concatenate(by_partner(seg_group.reshape(head_groups, 1, row_count)), axis=1)
 
-    window = with_halo(frames, (("head", 0),), half_kernel)
-    conv_pre = conv_fwd(cut, window, full_conv) + vectors[0]
+    if not by_chips():
+        window = with_halo(frames, (("head", 0),), half_kernel)
+        conv_pre = conv_fwd(cut, window, full_conv)
+    conv_pre = conv_pre + vectors[0]
     conv_act, conv_act_back = jax.vjp(gelu_exact, conv_pre)
     hidden_one = frames.astype(f32) + conv_act
     attn_in = hidden_one.astype(low_type)
@@ -795,9 +1323,14 @@
     packed = (
         lax.dot_general(full_qkv, attn_in, (((0,), (1,)), ((), ())), preferred_element_type=f32) + qkv_bias[:, None]
     ).astype(low_type)
-    blocks = trade(by_partner(packed.reshape(head_groups, -1, row_count)))
-    fwd = attn_fwd(seg_rows, blocks)
-    context = from_partner(trade(fwd[:4]))
+    if by_chips():
+        heads_qkv, context, log_sums, context_wide, all_up, all_down = attend(seg_rows, packed, own_parts[3:5], attend_plan())
+    else:
+        blocks = trade(by_partner(packed.reshape(head_groups, -1, row_count)))
+        fwd = attn_fwd(seg_rows, blocks)
+        context = from_partner(trade(fwd[:4]))
+    full_up = all_up.reshape(model_width, -1)
+    full_down = all_down.reshape(-1, model_width)
     attn_out = lax.dot_general(context, full_proj, (((0,), (0,)), ((), ())), preferred_element_type=f32) + vectors[3]
     normed_one, norm_one_back = jax.vjp(layer_norm, hidden_one + attn_out, vectors[4], vectors[5])
     ffn_in = normed_one.astype(low_type)
@@ -819,8 +1352,16 @@
     grad_proj = jnp.dot(context, grad_attn, preferred_element_type=f32).astype(low_type)
     grad_proj_bias = jnp.sum(grad_attn.astype(f32), axis=0)
     grad_context = lax.dot_general(full_proj, grad_attn, (((1,), (1,)), ((), ())), preferred_element_type=f32).astype(low_type)
-    grad_blocks = trade(by_partner(grad_context.reshape(head_groups, -1, row_count)))
-    grad_packed = from_partner(trade(attn_bwd(seg_rows, blocks, grad_blocks, fwd[4], fwd[5])))
+    grad_proj, grad_up, grad_down = [
+        g.reshape((count,) + w.shape) for g, w in ((grad_proj, proj_weight), (grad_up, up_weight), (grad_down, down_weight))
+    ]
+    if by_chips():
+        grad_packed, square_tile, sum_proj, sum_up, sum_down = attend_back(
+            seg_rows, heads_qkv, log_sums, context_wide, grad_context, [by_owner(g) for g in (grad_proj, grad_up, grad_down)], attend_back_plan()
+        )
+    else:
+        grad_blocks = trade(by_partner(grad_context.reshape(head_groups, -1, row_count)))
+        grad_packed = from_partner(trade(attn_bwd(seg_rows, blocks, grad_blocks, fwd[4], fwd[5])))
     grad_qkv = lax.dot_general(attn_in, grad_packed, (((0,), (1,)), ((), ())), preferred_element_type=f32).astype(low_type)
     grad_split = jnp.sum(grad_packed.astype(f32), axis=1).reshape(HEADS, 3, HEAD_DIM)
     grad_query_bias = grad_split[:, 0].reshape(model_width)
@@ -829,10 +1370,6 @@
     (grad_conv_pre,) = conv_act_back(grad_hidden_one)
     grad_conv_low = grad_conv_pre.astype(low_type)
     grad_conv_bias = jnp.sum(grad_conv_low.astype(f32), axis=0)
-    grad_window = with_halo(grad_conv_low, (("head", 0),), half_kernel)
-    grad_frames_conv, grad_conv = conv_bwd(cut, window, grad_window, full_conv)
-    frames_grad = grad_hidden_one + grad_frames_conv
-    grad_conv = grad_conv.reshape(16, 2, 8, 24 // conv_rows, conv_rows, 768).transpose(0, 1, 3, 2, 4, 5).reshape(count, 8, conv_rows, 768)
     grad_vectors = jnp.stack(
         [
             grad_conv_bias, grad_query_bias, grad_value_bias, grad_proj_bias, grad_gain_one, grad_shift_one,
@@ -844,22 +1381,26 @@
         [grad_vectors.reshape(vec_rows, count, vec_cols).transpose(1, 0, 2).reshape(count, -1), grad_ffn_bias.reshape(count, ffn_cols)], axis=1
     )
     grad_small = jnp.pad(grad_small, ((0, 0), (0, 2048 - grad_small.shape[1]))).astype(low_type).reshape(count, 16, 128)
-    (sum_conv, sum_qkv, sum_proj, sum_up, sum_down, sum_small), square_sum = collect_grads(
-        [
-            grad_conv,
-            grad_qkv.reshape((count,) + qkv_weight.shape),
-            grad_proj.reshape((count,) + proj_weight.shape),
-            grad_up.reshape((count,) + up_weight.shape),
-            grad_down.reshape((count,) + down_weight.shape),
-            grad_small,
-        ]
-    )
+    grad_qkv = grad_qkv.reshape((count,) + qkv_weight.shape)
+    if by_chips():
+        grad_frames_conv, norm_tile, sum_conv, sum_qkv, sum_small = close_step(
+            cut, window, grad_conv_low, whole_conv, square_tile, [by_owner(grad_qkv), by_owner(grad_small)], side_plan(), main_plan()
+        )
+        square_total = jnp.sum(norm_tile)
+    else:
+        grad_window = with_halo(grad_conv_low, (("head", 0),), half_kernel)
+        grad_frames_conv, grad_conv = conv_bwd(cut, window, grad_window, full_conv)
+        grad_conv = grad_conv.reshape(16, 2, 8, 24 // conv_rows, conv_rows, 768).transpose(0, 1, 3, 2, 4, 5).reshape(count, 8, conv_rows, 768)
+        (sum_conv, sum_qkv, sum_proj, sum_up, sum_down, sum_small), square_total = collect_grads(
+            [grad_conv, grad_qkv, grad_proj, grad_up, grad_down, grad_small]
+        )
+    frames_grad = grad_hidden_one + grad_frames_conv
     sum_conv = sum_conv.reshape(8, conv_rows, 16, group_width).transpose(2, 0, 1, 3).reshape(conv_weight.shape)
     sum_small = sum_small.reshape(-1)
     sum_vectors = sum_small[: vec_rows * vec_cols].reshape(vec_rows, vec_cols)
     sum_ffn_bias = sum_small[vec_rows * vec_cols : vec_rows * vec_cols + ffn_cols]
     summed = (sum_qkv, sum_proj, sum_up, sum_down, sum_conv, sum_vectors, sum_ffn_bias)
-    grad_norm = jnp.sqrt(square_sum)
+    grad_norm = jnp.sqrt(square_total)
     factor = jnp.minimum(1.0, clip_bound / grad_norm)
     masters = (qkv_weight, proj_weight, up_weight, down_weight, conv_weight, bias_gains, ffn_bias)
     firsts = (qkv_first, proj_first, up_first, down_first, conv_first, bias_gains_first, ffn_bias_first)

time: 628 us -> 535 us (0.85)
  waiting for transfers between devices: 46.8 us -> 0 us
  local copies, waits for them, and re-layouts: 50.4 us -> 24.5 us
  starting transfers between devices: 16.8 us -> 0 us
  matrix products: 62.1 us -> 71.9 us
  Pallas kernels: 409 us -> 400 us
    ppermute x16 -> x0, waiting for transfers between devices: 46.8 us -> none  [the longest x12 46.8 us: trade(): lax.ppermute(pieces[d], 'head', [(i, i ^ d) for i in range(count)])]
    ppermute x16 -> x0, starting transfers between devices: 16.8 us -> none  [the longest x12 8.84 us: trade(): lax.ppermute(pieces[d], 'head', [(i, i ^ d) for i in range(count)])]
    pallas_call x6 -> x4, Pallas kernels: 409 us -> 400 us  [the longest x1 126 us: close_step(): pl.pallas_call(functools.partial(close_kernel, side_plan, main_plan, n),...]
    dot_general x1, matrix products: 2.06 us -> 8.47 us  [shards(): lax.dot_general(grad_packed, full_qkv, (((0,), (1,)), ((), ())), preferre...]
    unnamed x181 -> x149, local copies, waits for them, and re-layouts: 12.2 us -> 13.1 us
  transfers between devices with their start and end apart: 16 -> 0, of which waited for: 5 -> 0; matrix products, arithmetic and copies ran while one was open for 8% -> 0% of each run, Pallas kernels for 20% -> 0%
where the time goes in v2:
time: 535 us; the launch traced here: 532 us
  Pallas kernels  400 us (75%)
  matrix products  71.9 us (13%)
  other arithmetic  30.8 us (6%)
  local copies, waits for them, and re-layouts  24.5 us (5%)
    pallas_call x1, Pallas kernels, close_step(): pl.pallas_call(functools.partial(close_kernel, side_plan, main_plan, n),...  126 us
    pallas_call x1, Pallas kernels, attend_back(): pl.pallas_call(functools.partial(attend_back_kernel, plan, n), in_specs=[...  99.5 us
    pallas_call x1, Pallas kernels, open_step(): pl.pallas_call(functools.partial(open_kernel, plan, n, early), in_specs=[...  91.6 us
    pallas_call x1, Pallas kernels, attend(): pl.pallas_call(functools.partial(attend_kernel, plan, n), in_specs=[vmem,...  83 us
    dot_general x1, matrix products, shards(): jnp.dot(ffn_in, full_up, preferred_element_type=f32) + full_ffn  19.8 us
    unnamed x149, local copies, waits for them, and re-layouts  13.1 us

profile of v2, /device:TPU:0, one launch (start us, length us, event | category | flops | bytes accessed | tf_op | source)
XLA Modules:
  0.0 531.6 jit_solution(6716056360639318588)
XLA Ops:
  1.2 2.0 fusion.30
  4.4 1.6 copy.120
  6.6 1.5 reshape.207.refs_2_
  10.2 91.6 %shard_map.415 = (f32[512,768]{1,0:T(8,128)}, bf16[640,768]{1,0:T(8,128)(2,1)}, bf16[4,2,2,2,8,24,768]{6,5,4,3,2,1,0:T(8,128)(2,1)}, bf16[4,2,2,2,24,2304]{5,4,3...) custom-call(s32[2]{0:T(128)} %pad_add_fusion.1.refs_0_, ...), custom_call_target="tpu_custom_call" | custom-call | tf_op jit(solution)/shard_map/pallas_call | solution.py:811
  105.8 5.8 %multiply_add_fusion.1 = (f32[512,768]{1,0:T(8,128)S(1)}, f32[512,768]{1,0:T(8,128)}) fusion(bf16[512,768]{1,0:T(8,128)(2,1)S(1)} %copy-done.6, f32[512,768]{1,0:T(8,128)} %get-tuple-element.46, f32[768]{0:T(1024)S(1)} %add.234), kind=kLoop, calls=%fused_computation.41 | loop fusion | flops 26345472 | bytes 5508096 | tf_op jit(solution)/shard_map/add | solution.py:1317
  111.7 3.8 fusion.6.refs_1_
  115.6 83.0 %shard_map.416 = (bf16[576,2048]{1,0:T(8,128)(2,1)}, bf16[768,512]{1,0:T(8,128)(2,1)S(1)}, f32[3,1,2048]{2,1,0:T(1,128)S(1)}, f32[192,2048]{1,0:T(8,128)S(1)}, b...) custom-call(s32[1,2048]{1,0:T(1,128)S(1)} %pad_add_fusion.refs_0_, ...), custom_call_target="tpu_custom_call" | custom-call | tf_op jit(solution)/shard_map/pallas_call | solution.py:955
  200.5 2.7 fusion.57
  203.9 19.8 %multiply_convert_fusion = (bf16[512,3072]{1,0:T(8,128)(2,1)S(1)}, f32[512,3072]{1,0:T(8,128)}, f32[512,3072]{1,0:T(8,128)}) fusion(f32[3072]{0:T(1024)S(1)} %copy-done.48, bf16[768,3072]{1,0:T(8,128)(2,1)} %bitcast.80, f32[512,768]{1,0:T(8,128)S(1)} %get-tuple-element.201, f32[768]{0:T(1024)S(1)} %add.250, f32[768]{0:T(1024)S(1)} %mul.501, ...), kind=kOutput, calls=%fused_computation.3 | convolution fusion | flops 2521694208 | bytes 22042624 | tf_op jit(solution)/shard_map/dot_general | solution.py:1337
  223.8 6.7 %fusion.58 = (f32[512]{0:T(512)S(1)}, f32[512,768]{1,0:T(8,128)S(1)}) fusion(f32[768]{0:T(1024)S(1)} %copy-done.55, bf16[512,3072]{1,0:T(8,128)(2,1)S(1)} %get-tuple-element.182, bf16[3072,768]{1,0:T(8,128)(2,1)} %bitcast.82, f32[768]{0:T(1024)S(1)} %add.250, f32[768]{0:T(1024)S(1)} %mul.501, f32[512]{0:T(512)S(1)} %fusion.35, f32[512,768]{1,0:T(8,128)} %copy-done.4, ...), kind=kOutput, calls=%fused_computation.145 | convolution fusion | flops 2418671104 | bytes 11025408 | tf_op jit(solution)/shard_map/dot_general | solution.py:1339
  231.6 2.0 fusion.10
  234.4 2.4 fusion.53
  237.6 7.7 %fusion.51 = (bf16[3072]{0:T(1024)(128)(2,1)S(1)}, bf16[512,3072]{1,0:T(8,128)(2,1)S(1)}) fusion(f32[512,3072]{1,0:T(8,128)} %get-tuple-element.183, f32[512,3072]{1,0:T(8,128)} %get-tuple-element.202, f32[3072]{0:T(1024)S(1)} %copy-done.49, bf16[512,768]{1,0:T(8,128)(2,1)S(1)} %get-tuple-element.171, bf16[3072,768]{1,0:T(8,128)(2,1)S(1)} %bitcast.83), kind=kOutput, calls=%fused_computation.140 | convolution fusion | flops 2441081856 | bytes 21252096 | tf_op jit(solution)/shard_map/td,fd->tf/dot_general | solution.py:1345
  245.3 6.1 %multiply_reduce_fusion = (bf16[768]{0:T(1024)(128)(2,1)}, f32[512]{0:T(512)S(1)}, bf16[768]{0:T(1024)(128)(2,1)S(1)}, f32[512,768]{1,0:T(8,128)S(1)}) fusion(f32[512,768]{1,0:T(8,128)S(1)} %copy-done.5, f32[512]{0:T(512)S(1)} %copy-done.52, f32[512]{0:T(512)S(1)} %copy-done.38, f32[768]{0:T(1024)S(1)} %copy-done.47, ...), kind=kOutput, calls=%fused_computation.32 | convolution fusion | flops 2419849216 | bytes 12597248 | tf_op jit(solution)/shard_map/tf,df->td/dot_general | solution.py:1349
  253.4 1.7 convolution_convert_fusion.4.refs_4_
  255.1 1.8 convolution_convert_fusion.3
  256.9 4.8 convolution_convert_fusion.2
  261.8 4.3 convolution_convert_fusion.1
  266.1 99.5 %shard_map.417 = (bf16[2304,512]{1,0:T(8,128)(2,1)}, f32[8,128]{1,0:T(8,128)}, f32[24,768]{1,0:T(8,128)}, f32[24,3072]{1,0:T(8,128)}, f32[96,768]{1,0:T(8,128)}) custom-call(s32[1,2048]{1,0:T(1,128)} %copy-done.1, bf16[576,2048]{1,0:T(8,128)(2,1)} %get-tuple-element.53.refs_1_, f32[3,1,2048]{2,1,0:T(1,128)} %copy-done.2, f32[192,2048]{1,0:T(8,128)} %copy-done, ...), custom_call_target="tpu_custom_call" | custom-call | tf_op jit(solution)/shard_map/pallas_call | solution.py:1073
  365.6 8.5 %fusion.50 = (bf16[768]{0:T(1024)(128)(2,1)}, bf16[512,768]{1,0:T(8,128)(2,1)}, f32[512,768]{1,0:T(8,128)}) fusion(f32[512,768]{1,0:T(8,128)} %get-tuple-element.185, f32[512,768]{1,0:T(8,128)} %get-tuple-element.46, f32[768]{0:T(1024)S(1)} %copy-done.45, bf16[2304,512]{1,0:T(8,128)(2,1)} %get-tuple-element.56, bf16[768,2304]{1,0:T(8,128)(2,1)} %bitcast.84, ...), kind=kOutput, calls=%fused_computation.139 | convolution fusion | flops 1819016448 | bytes 12982784 | tf_op jit(solution)/shard_map/dot_general | solution.py:1369
  374.1 3.9 convolution_convert_fusion
  388.3 125.9 %shard_map.418 = (f32[512,768]{1,0:T(8,128)}, f32[8,128]{1,0:T(8,128)}, f32[8,24,768]{2,1,0:T(8,128)}, f32[24,2304]{1,0:T(8,128)}, f32[16,128]{1,0:T(8,128)}) custom-call(s32[2]{0:T(128)} %pad_add_fusion.1.refs_0_, bf16[640,768]{1,0:T(8,128)(2,1)} %get-tuple-element.57.refs_1_, bf16[512,768]{1,0:T(8,128)(2,1)} %get-tuple-element.175.refs_2_, ...), custom_call_target="tpu_custom_call" | custom-call | tf_op jit(solution)/shard_map/pallas_call | solution.py:1175
  514.3 2.8 add.266
  525.0 2.6 multiply_subtract_fusion
  (231 shorter events, 34.6 us)
Async XLA Ops:
  8.1 97.6 %copy-start.6 = (bf16[512,768]{1,0:T(8,128)(2,1)S(1)}, bf16[512,768]{1,0:T(8,128)(2,1)}, u32[]{:S(2)}) copy-start(bf16[512,768]{1,0:T(8,128)(2,1)} %refs_1_.1) | copy-start | bytes 2359300
  105.0 10.6 %copy-start.1 = (s32[1,2048]{1,0:T(1,128)}, s32[1,2048]{1,0:T(1,128)S(1)}, u32[]{:S(2)}) copy-start(s32[1,2048]{1,0:T(1,128)S(1)} %pad_add_fusion.refs_0_) | copy-start | bytes 24580
  105.8 5.9 %copy-start.44 = (f32[768]{0:T(1024)}, f32[768]{0:T(1024)S(1)}, u32[]{:S(2)}) copy-start(f32[768]{0:T(1024)S(1)} %add.234) | copy-start | bytes 9220
  105.8 5.9 %copy-start.64 = (bf16[4,2,2,2,24,2304]{5,4,3,2,1,0:T(8,128)(2,1)S(1)}, bf16[4,2,2,2,24,2304]{5,4,3,2,1,0:T(8,128)(2,1)}, u32[]{:S(2)}) copy-start(bf16[4,2,2,2,24,2304]{5,4,3,2,1,0:T(8,128)(2,1)} %get-tuple-element.48) | copy-start | bytes 10616836
  203.2 20.6 %copy-start.4 = (f32[512,768]{1,0:T(8,128)}, f32[512,768]{1,0:T(8,128)S(1)}, u32[]{:S(2)}) copy-start(f32[512,768]{1,0:T(8,128)S(1)} %get-tuple-element.201) | copy-start | bytes 4718596
  203.4 20.4 %copy-start.56 = (f32[768]{0:T(1024)}, f32[768]{0:T(1024)S(1)}, u32[]{:S(2)}) copy-start(f32[768]{0:T(1024)S(1)} %add.250) | copy-start | bytes 9220
  203.6 20.2 %copy-start.46 = (f32[768]{0:T(1024)}, f32[768]{0:T(1024)S(1)}, u32[]{:S(2)}) copy-start(f32[768]{0:T(1024)S(1)} %mul.501) | copy-start | bytes 9220
  203.6 20.2 %copy-start.37 = (f32[512]{0:T(512)}, f32[512]{0:T(512)S(1)}, u32[]{:S(2)}) copy-start(f32[512]{0:T(512)S(1)} %broadcast_multiply_fusion.2) | copy-start | bytes 6148
  203.9 19.9 %copy-start.40 = (f32[512]{0:T(512)}, f32[512]{0:T(512)S(1)}, u32[]{:S(2)}) copy-start(f32[512]{0:T(512)S(1)} %multiply_reduce_fusion.3) | copy-start | bytes 6148
  203.9 19.9 %copy-start.51 = (f32[512]{0:T(512)}, f32[512]{0:T(512)S(1)}, u32[]{:S(2)}) copy-start(f32[512]{0:T(512)S(1)} %fusion.35) | copy-start | bytes 6148
  203.9 19.9 %copy-start.55 = (f32[768]{0:T(1024)S(1)}, f32[768]{0:T(1024)}, u32[]{:S(2)}) copy-start(f32[768]{0:T(1024)} %add.257) | copy-start | bytes 9220
  223.8 6.7 %copy-start.66 = (bf16[512,3072]{1,0:T(8,128)(2,1)}, bf16[512,3072]{1,0:T(8,128)(2,1)S(1)}, u32[]{:S(2)}) copy-start(bf16[512,3072]{1,0:T(8,128)(2,1)S(1)} %get-tuple-element.182) | copy-start | bytes 9437188
  237.5 7.7 %copy-start.5 = (f32[512,768]{1,0:T(8,128)S(1)}, f32[512,768]{1,0:T(8,128)}, u32[]{:S(2)}) copy-start(f32[512,768]{1,0:T(8,128)} %copy-done.4) | copy-start | bytes 4718596
  237.6 7.7 %copy-start.38 = (f32[512]{0:T(512)S(1)}, f32[512]{0:T(512)}, u32[]{:S(2)}) copy-start(f32[512]{0:T(512)} %copy-done.37) | copy-start | bytes 6148
  237.6 7.7 %copy-start.47 = (f32[768]{0:T(1024)S(1)}, f32[768]{0:T(1024)}, u32[]{:S(2)}) copy-start(f32[768]{0:T(1024)} %copy-done.46) | copy-start | bytes 9220
  237.6 7.8 %copy-start.52 = (f32[512]{0:T(512)S(1)}, f32[512]{0:T(512)}, u32[]{:S(2)}) copy-start(f32[512]{0:T(512)} %copy-done.51) | copy-start | bytes 6148
  245.3 6.1 %copy-start.41 = (f32[512]{0:T(512)S(1)}, f32[512]{0:T(512)}, u32[]{:S(2)}) copy-start(f32[512]{0:T(512)} %copy-done.40) | copy-start | bytes 6148
  256.9 4.9 copy-start.67
  266.1 99.5 %copy-start.45 = (f32[768]{0:T(1024)S(1)}, f32[768]{0:T(1024)}, u32[]{:S(2)}) copy-start(f32[768]{0:T(1024)} %copy-done.44) | copy-start | bytes 9220
  365.6 8.5 %copy-start.7 = (bf16[2304,512]{1,0:T(8,128)(2,1)S(1)}, bf16[2304,512]{1,0:T(8,128)(2,1)}, u32[]{:S(2)}) copy-start(bf16[2304,512]{1,0:T(8,128)(2,1)} %get-tuple-element.56) | copy-start | bytes 7077892
  365.6 8.5 %copy-start.10 = (f32[512,768]{1,0:T(8,128)S(1)}, f32[512,768]{1,0:T(8,128)}, u32[]{:S(2)}) copy-start(f32[512,768]{1,0:T(8,128)} %copy-done.9) | copy-start | bytes 4718596
  378.0 6.9 %copy-start.50 = (bf16[768]{0:T(1024)(128)(2,1)S(1)}, bf16[768]{0:T(1024)(128)(2,1)}, u32[]{:S(2)}) copy-start(bf16[768]{0:T(1024)(128)(2,1)} %get-tuple-element.142) | copy-start | bytes 4612
  388.3 125.9 %copy-start.11 = (f32[512,768]{1,0:T(8,128)S(1)}, f32[512,768]{1,0:T(8,128)}, u32[]{:S(2)}) copy-start(f32[512,768]{1,0:T(8,128)} %get-tuple-element.206) | copy-start | bytes 4718596
  514.2 4.2 copy-start.16
  (44 other events, 111.2 us)

commit v3 on v2

--- a/solution.py
+++ b/solution.py
@@ -364,19 +364,17 @@
 
 def greet(plane=False, group=False, halo=False):
     z, x, y, c = spot()
+    for n in range(1, 4):
+        hail(device(z ^ n, x, y, c))
     if plane:
         for n in range(1, 8):
             hail(device(z, x ^ (n >> 2), y ^ ((n >> 1) & 1), c ^ (n & 1)))
-        for n in range(1, 4):
-            hail(device(z ^ n, x, y, c))
         pl.semaphore_wait(pltpu.get_barrier_semaphore(), 10)
         return
-    count = jnp.where((z == 0) | (z == 3), 4, 5)
+    count = 6
     hail(device(z, x, y, 1 - c))
     hail(device(z, x, 1 - y, c))
     hail(device(z, 1 - x, y, c))
-    pl.when(z > 0)(lambda: hail(device(z - 1, x, y, c)))
-    pl.when(z < 3)(lambda: hail(device(z + 1, x, y, c)))
     if group:
         hail(device(z, x, 1 - y, 1 - c))
         count = count + 1
@@ -399,93 +397,56 @@
 
 
 class Spread(Unit):
+    heavy = (2, 1, 0, 3, 4)
+
     def __init__(self, own, whole, cut, order, send, recv):
         self.own, self.whole, self.cut, self.order, self.send, self.recv = own, whole, cut, order, send, recv
-        self.steps = []
-        for at, axis in enumerate(order):
-            self.steps += [("z", 1), ("z", 2), ("z", 3)] if axis == "z" else [(axis, at)]
-        self.steps.append(("c", 3))
-
-    def block(self, at, **given):
+
+    def block(self, done, **given):
         z, x, y, c = spot()
         here = {"z": z, "x": x, "y": y, "c": c}
-        done = self.order[:at]
         lead = tuple(given[a] if a in given else (EVERY if a in done else here[a]) for a in "zxyc")
         return self.whole.at[lead + self.cut]
 
-    def source(self, at, ref):
-        return self.own.at[self.cut] if at == 0 and self.cut else (self.own if at == 0 else ref)
-
-    def up(self, k):
+    def mine(self):
+        return self.own.at[self.cut] if self.cut else self.own
+
+    def columns(self):
         z, x, y, c = spot()
-        at = self.order.index("z")
-        ref = self.block(at, z=z - (k - 1))
-        src = self.source(at, ref) if k == 1 else ref
-        return (z < 3) & (z >= k - 1), self.remote(src, ref, k - 1, device(z + 1, x, y, c))
-
-    def down(self, k):
+        return [self.remote(self.mine(), self.block(""), n - 1, device(z ^ n, x, y, c)) for n in range(1, 4)]
+
+    def swap(self, k):
         z, x, y, c = spot()
-        at = self.order.index("z")
-        ref = self.block(at, z=z + (k - 1))
-        src = self.source(at, ref) if k == 1 else ref
-        return (z > 0) & (z + k - 1 <= 3), self.remote(src, ref, 2 + k, device(z - 1, x, y, c))
-
-    def came_up(self, k):
+        axis = (self.order + "c")[k]
+        ref = self.block("z" + self.order[:k])
+        to = {"x": device(z, 1 - x, y, c), "y": device(z, x, 1 - y, c), "c": device(z, x, y, 1 - c)}[axis]
+        return self.remote(ref, ref, 3 + k, to)
+
+    def swapped(self, k):
         z, x, y, c = spot()
-        ref = self.block(self.order.index("z"), z=z - k)
-        return z >= k, self.landed(ref, k - 1)
-
-    def came_down(self, k):
-        z, x, y, c = spot()
-        ref = self.block(self.order.index("z"), z=z + k)
-        return z + k <= 3, self.landed(ref, 2 + k)
-
-    def swap(self, axis, at):
-        z, x, y, c = spot()
-        ref = self.block(at)
-        to = {"x": device(z, 1 - x, y, c), "y": device(z, x, 1 - y, c), "c": device(z, x, y, 1 - c)}[axis]
-        return self.remote(self.source(at, ref), ref, 6 + "xyc".index(axis), to)
-
-    def came_over(self, axis, at):
-        z, x, y, c = spot()
-        other = {"x": 1 - x, "y": 1 - y, "c": 1 - c}[axis]
-        return self.landed(self.block(at, **{axis: other}), 6 + "xyc".index(axis))
-
-    def start(self, step):
-        axis, k = step
-        if axis == "z":
-            for ok, copy in (self.up(k), self.down(k)):
-                pl.when(ok)(copy.start)
-        else:
-            self.swap(axis, k).start()
-
-    def end(self, step):
-        axis, k = step
-        if axis == "z":
-            for ok, copy in (self.came_up(k), self.came_down(k)):
-                pl.when(ok)(copy.wait_recv)
-        else:
-            self.came_over(axis, k).wait_recv()
+        axis = (self.order + "c")[k]
+        return self.landed(self.block("z" + self.order[:k], **{axis: {"x": 1 - x, "y": 1 - y, "c": 1 - c}[axis]}), 3 + k)
 
     def stage(self, n):
         z, x, y, c = spot()
         if n < 2:
-            local = pltpu.make_async_copy(self.source(0, None), self.block(0), self.recv.at[9])
+            local = pltpu.make_async_copy(self.mine(), self.block(""), self.recv.at[6])
             local.start() if n == 0 else local.wait()
-        if n > 0:
-            self.end(self.steps[n - 1])
-        if n < len(self.steps):
-            self.start(self.steps[n])
-
-    stages = 7
+        if n == 0:
+            for copy in self.columns():
+                copy.start()
+        elif n == 1:
+            for m in range(1, 4):
+                self.landed(self.block("", z=z ^ m), m - 1).wait_recv()
+            self.swap(0).start()
+        else:
+            self.swapped(n - 2).wait_recv()
+            if n < 4:
+                self.swap(n - 1).start()
 
     def finish(self):
-        for axis, k in self.steps:
-            if axis == "z":
-                for ok, copy in (self.up(k), self.down(k)):
-                    pl.when(ok)(copy.wait_send)
-            else:
-                self.swap(axis, k).wait_send()
+        for copy in self.columns() + [self.swap(k) for k in range(3)]:
+            copy.wait_send()
 
 
 def add_rows(dst, src):
@@ -493,12 +454,11 @@
 
 
 class Collect(Unit):
+    heavy = (0, 1, 2, 3, 4)
+
     def __init__(self, parts, out, cut, order, own, rc, r1, r2, rz, send, recv):
         self.parts, self.out, self.cut, self.order, self.send, self.recv = parts, out, cut, order, send, recv
         self.own, self.rc, self.r1, self.r2, self.rz = own, rc, r1, r2, rz
-        self.steps = [("c", 0)]
-        for at, axis in enumerate(order):
-            self.steps += [("z", 1), ("z", 2), ("z", 3)] if axis == "z" else [(axis, at)]
 
     def block(self, *lead):
         if self.own is None:
@@ -506,116 +466,80 @@
             return self.parts.at[tuple(lead) + (c,) + self.cut]
         return self.own.at[tuple(lead)]
 
-    def lead(self, at, **given):
+    def core(self):
         z, x, y, c = spot()
-        here = {"z": z, "x": x, "y": y}
-        done = self.order[:at]
-        return tuple(given[a] if a in given else (here[a] if a in done else EVERY) for a in "zxy")
-
-    def swap(self, axis, at):
-        z, x, y, c = spot()
-        if axis == "c":
-            return self.remote(self.parts.at[(EVERY, EVERY, EVERY, 1 - c) + self.cut], self.rc, 0, device(z, x, y, 1 - c))
-        other = {"x": 1 - x, "y": 1 - y}[axis]
-        to = {"x": device(z, 1 - x, y, c), "y": device(z, x, 1 - y, c)}[axis]
-        return self.remote(self.block(*self.lead(at, **{axis: other})), self.r1 if at == 0 else self.r2, 1 + min(at, 1), to)
+        return self.remote(self.parts.at[(EVERY, EVERY, EVERY, 1 - c) + self.cut], self.rc, 0, device(z, x, y, 1 - c))
 
     def load(self):
         z, x, y, c = spot()
-        return pltpu.make_async_copy(self.parts.at[(EVERY, EVERY, EVERY, c) + self.cut], self.own, self.recv.at[9])
-
-    def hop(self, k, rising):
+        return pltpu.make_async_copy(self.parts.at[(EVERY, EVERY, EVERY, c) + self.cut], self.own, self.recv.at[6])
+
+    def first(self):
         z, x, y, c = spot()
-        at = self.order.index("z")
-        d = z + (4 - k) if rising else z - (4 - k)
-        ok = d <= 3 if rising else d >= 0
-        slot = 2 + k if rising else k - 1
-        to = device(z + 1, x, y, c) if rising else device(z - 1, x, y, c)
-        return ok, self.remote(self.block(*self.lead(at, z=jnp.clip(d, 0, 3))), self.rz.at[slot], 3 + slot, to)
-
-    def hopped(self, k, rising):
+        if self.order[0] == "x":
+            return self.remote(self.block(EVERY, 1 - x, EVERY), self.r1, 1, device(z, 1 - x, y, c))
+        return self.remote(self.block(EVERY, EVERY, 1 - y), self.r1, 1, device(z, x, 1 - y, c))
+
+    def second(self):
         z, x, y, c = spot()
-        d = z + (3 - k) if rising else z - (3 - k)
-        ok = (z > 0) & (d <= 3) if rising else (z < 3) & (d >= 0)
-        slot = 2 + k if rising else k - 1
-        return ok, jnp.clip(d, 0, 3), self.rz.at[slot], self.landed(self.rz.at[slot], 3 + slot)
-
-    def start(self, step):
-        axis, k = step
-        if axis == "z":
-            for rising in (False, True):
-                ok, copy = self.hop(k, rising)
-                pl.when(ok)(copy.start)
-        else:
-            self.swap(axis, k).start()
-            if axis == "c" and self.own is not None:
+        if self.order[0] == "x":
+            return self.remote(self.block(EVERY, x, 1 - y), self.r2, 2, device(z, x, 1 - y, c))
+        return self.remote(self.block(EVERY, 1 - x, y), self.r2, 2, device(z, 1 - x, y, c))
+
+    def columns(self):
+        z, x, y, c = spot()
+        return [self.remote(self.block(z ^ n, x, y), self.rz.at[n - 1], 2 + n, device(z ^ n, x, y, c)) for n in range(1, 4)]
+
+    def stage(self, n):
+        z, x, y, c = spot()
+        if n == 0:
+            self.core().start()
+            if self.own is not None:
                 self.load().start()
-
-    def end(self, step, last):
-        z, x, y, c = spot()
-        axis, k = step
-        if axis == "z":
-            at = self.order.index("z")
-            pair = "x" if "x" not in self.order[:at] else ("y" if "y" not in self.order[:at] else None)
-            for rising in (False, True):
-                ok, d, ref, copy = self.hopped(k, rising)
-
-                @pl.when(ok)
-                def _(d=d, ref=ref, copy=copy):
-                    copy.wait_recv()
-                    for n in range(2 if pair else 1):
-                        given = {"z": d, pair: n} if pair else {"z": d}
-                        add_rows(self.block(*self.lead(at, **given)), ref.at[n] if pair else ref)
-        elif axis == "c":
+        elif n == 1:
             self.landed(self.rc, 0).wait_recv()
             if self.own is not None:
                 self.load().wait()
 
             def one(i, unused):
-                for n in range(2):
+                for k in range(2):
                     for m in range(2):
-                        add_rows(self.block(i, n, m), self.rc.at[i, n, m])
+                        add_rows(self.block(i, k, m), self.rc.at[i, k, m])
                 return unused
 
             lax.fori_loop(0, 4, one, 0)
+            self.first().start()
+        elif n == 2:
+            self.landed(self.r1, 1).wait_recv()
+
+            def one(i, unused):
+                for k in range(2):
+                    add_rows(self.block(i, x, k) if self.order[0] == "x" else self.block(i, k, y), self.r1.at[i, k])
+                return unused
+
+            lax.fori_loop(0, 4, one, 0)
+            self.second().start()
+        elif n == 3:
+            self.landed(self.r2, 2).wait_recv()
+
+            def one(i, unused):
+                add_rows(self.block(i, x, y), self.r2.at[i])
+                return unused
+
+            lax.fori_loop(0, 4, one, 0)
+            for copy in self.columns():
+                copy.start()
         else:
-            ref = self.r1 if k == 0 else self.r2
-            self.landed(ref, 1 + min(k, 1)).wait_recv()
-            here = {"x": x, "y": y}[axis]
-            rest = [a for a in "zxy" if a not in self.order[: k + 1]]
-            if not rest:
-                add_rows(self.block(z, x, y), ref)
-            else:
-
-                def one(i, unused):
-                    for n in range(2 if len(rest) == 2 else 1):
-                        given = {"z": i, axis: here}
-                        if len(rest) == 2:
-                            given[rest[1]] = n
-                        add_rows(self.block(*self.lead(k, **given)), ref.at[i, n] if len(rest) == 2 else ref.at[i])
-                    return unused
-
-                lax.fori_loop(0, 4, one, 0)
-        if last:
+            total = self.block(z, x, y)[...].astype(jnp.float32)
+            for m in range(1, 4):
+                self.landed(self.rz.at[m - 1], 2 + m).wait_recv()
+                total = total + self.rz[m - 1].astype(jnp.float32)
             out = self.out.at[self.cut] if self.cut else self.out
-            out[...] = self.block(z, x, y)[...].astype(jnp.float32)
-
-    stages = 7
-
-    def stage(self, n):
-        if n > 0:
-            self.end(self.steps[n - 1], n == len(self.steps))
-        if n < len(self.steps):
-            self.start(self.steps[n])
+            out[...] = total
 
     def finish(self):
-        for axis, k in self.steps:
-            if axis == "z":
-                for rising in (False, True):
-                    ok, copy = self.hop(k, rising)
-                    pl.when(ok)(copy.wait_send)
-            else:
-                self.swap(axis, k).wait_send()
+        for copy in [self.core(), self.first(), self.second()] + self.columns():
+            copy.wait_send()
 
 
 def unit_shape(shape, cut):
@@ -628,7 +552,7 @@
     for i, cut, order in plan:
         m = unit_shape(shapes[i], cut)
         leads = [] if i in inside else [(4, 2, 2)]
-        leads += [(4, 2, 2), (4, 2), () if order[1] == "z" else (4,), (6, 2) if order[1] == "z" else (6,)]
+        leads += [(4, 2, 2), (4, 2), (4,), (3,)]
         scratch += [pltpu.VMEM(lead + m, dtype) for lead in leads]
     return scratch
 
@@ -641,11 +565,14 @@
     return units
 
 
+STAGES = 5
+
+
 def waves(units, width=2):
     rows = [units[i : i + width] for i in range(0, len(units), width)]
     steps = []
-    for t in range(len(rows) + 6):
-        steps.append([(unit, n) for n in (3, 4, 5, 6, 2, 1, 0) if 0 <= t - n < len(rows) for unit in rows[t - n]])
+    for t in range(len(rows) + STAGES - 1 if rows else 0):
+        steps.append([(unit, n) for n in units[0].heavy for unit in (rows[t - n] if 0 <= t - n < len(rows) else [])])
     return steps
 
 
@@ -741,9 +668,9 @@
 def open_kernel(plan, n_in, early, *refs):
     cut_ref, frames_ref = refs[:2]
     owns = refs[2 : 2 + n_in]
-    out_ref, win_ref = refs[2 + n_in : 4 + n_in]
+    out_ref, cols_ref = refs[2 + n_in : 4 + n_in]
     wholes = refs[4 + n_in : 4 + 2 * n_in]
-    cols_s, low_s, w_s, wp_s, send, recv, hsend, hrecv, wsem = refs[4 + 2 * n_in :]
+    win_ref, cols_s, low_s, w_s, wp_s, send, recv, hsend, hrecv, wsem, csem = refs[4 + 2 * n_in :]
     cut = cut_ref[0]
     greet(halo=True)
     halo_start(frames_ref, win_ref, hsend, hrecv)
@@ -780,14 +707,19 @@
         put_group(out_ref, g, pick_own(fold_out(z), cut))
         return unused
 
+    def keep(chunk):
+        span = pl.ds(4 * chunk, 4)
+        return pltpu.make_async_copy(cols_s.at[span], cols_ref.at[span], csem.at[chunk])
+
     t = 2
     for chunk in range(4):
         lax.fori_loop(4 * chunk, 4 * chunk + 4, columns, 0)
+        keep(chunk).start()
         go(steps[t])
         t += 1
     done = 0
     while t < len(steps) or done < 2:
-        if done < 2 and t - 1 - 6 >= early[done]:
+        if done < 2 and t - STAGES >= early[done]:
             for z in range(4):
                 load(done, z).start()
             for z in range(4):
@@ -802,6 +734,8 @@
             t += 1
     for unit in units:
         unit.finish()
+    for chunk in range(4):
+        keep(chunk).wait()
 
 
 def open_step(cut, frames, shards, plan, early, collective_id=1):
@@ -811,10 +745,11 @@
     return pl.pallas_call(
         functools.partial(open_kernel, plan, n, early),
         in_specs=[pl.BlockSpec(memory_space=pltpu.SMEM), vmem] + [anywhere] * n,
-        out_specs=[vmem, vmem] + [anywhere] * n,
-        out_shape=[jax.ShapeDtypeStruct((OWN, 768), jnp.float32), jax.ShapeDtypeStruct((WIN, 768), jnp.bfloat16)]
+        out_specs=[vmem, anywhere] + [anywhere] * n,
+        out_shape=[jax.ShapeDtypeStruct((OWN, 768), jnp.float32), jax.ShapeDtypeStruct((16, ZROWS, 768), jnp.bfloat16)]
         + [jax.ShapeDtypeStruct((4, 2, 2, 2) + s.shape, s.dtype) for s in shards],
         scratch_shapes=[
+            pltpu.VMEM((WIN, 768), jnp.bfloat16),
             pltpu.VMEM((16, ZROWS, 768), jnp.bfloat16),
             pltpu.VMEM((16, ZROWS, 256), jnp.float32),
             pltpu.VMEM((4, 2, 2, 2, 4, 24, 768), jnp.bfloat16),
@@ -823,6 +758,7 @@
             pltpu.SemaphoreType.DMA((len(plan), 10)),
             pltpu.SemaphoreType.DMA((2,)),
             pltpu.SemaphoreType.DMA((2,)),
+            pltpu.SemaphoreType.DMA((4,)),
             pltpu.SemaphoreType.DMA((4,)),
         ],
         compiler_params=pltpu.CompilerParams(collective_id=collective_id, has_side_effects=True, vmem_limit_bytes=56 * 2**20),
@@ -900,12 +836,11 @@
 
     own = pltpu.make_async_copy(packed_ref.at[pl.ds(me * ROWS_HERE, ROWS_HERE)], qkv_ref.at[:, 0:size], osem)
     own.start()
-    for h in range(HEADS_HERE):
-        for d in (2, 3, 1):
-            bring(h, d).start()
+    for d in (2, 3, 1):
+        bring(0, d).start()
     units = [Spread(owns[i], wholes[i], where, order, send.at[n], recv.at[n]) for n, (i, where, order) in enumerate(plan)]
     steps = waves(units)
-    go(steps[0])
+    go(steps[0] if steps else [])
     tiles = 4 * size // QF
     by_slot = spaced(steps[1:], HEADS_HERE * tiles)
     own.wait()
@@ -913,6 +848,12 @@
     def head(h, unused):
         for d in (1, 2, 3):
             bring(h, d).wait_recv()
+
+        @pl.when(h < HEADS_HERE - 1)
+        def _():
+            for d in (2, 3, 1):
+                bring(jnp.minimum(h + 1, HEADS_HERE - 1), d).start()
+
         fill_heads(seg_ref, qkv_ref, h, k_s, q_s)
 
         def tile(i, unused):
@@ -930,7 +871,7 @@
             go_at(h * tiles + i, by_slot)
             return unused
 
-        lax.fori_loop(0, tiles, tile, 0)
+        lax.fori_loop(0, tiles, tile, 0, unroll=True)
         for d in (2, 3, 1):
             give(h, d).start()
         ctx_ref[pl.ds(pl.multiple_of(me * 64 * HEADS_HERE + h * 64, 64), 64), :] = ctx_s[pl.ds(pl.multiple_of(h * 64, 64), 64), 0:size]
@@ -1011,7 +952,7 @@
             bring(h, d).start()
     units = collect_units(plan, parts, outs, bufs, (), send, recv)
     steps = waves(units)
-    go(steps[0])
+    go(steps[0] if steps else [])
     tiles = 4 * size // QT
     by_slot = spaced(steps[1:], HEADS_HERE * tiles)
     own.wait()
@@ -1086,7 +1027,7 @@
             pltpu.VMEM((64, 4 * size), jnp.float32),
             pltpu.VMEM((ROWS_HERE, 4 * size), jnp.bfloat16),
             sem((3, 3)), sem((3, 3)), sem((3, 3)), sem((3, 3)), sem,
-            sem((len(plan), 9)), sem((len(plan), 10)),
+            sem((max(len(plan), 1), 9)), sem((max(len(plan), 1), 10)),
         ]
         + collect_scratch(plan, shapes, jnp.bfloat16, ()),
         compiler_params=pltpu.CompilerParams(collective_id=collective_id, has_side_effects=True, vmem_limit_bytes=58 * 2**20),
@@ -1094,12 +1035,12 @@
 
 
 def close_kernel(side_plan, main_plan, n_in, *refs):
-    cut_ref, win_ref, grad_ref, conv_ref, tile_ref = refs[:5]
-    parts = refs[5 : 5 + n_in]
-    dx_ref, norm_ref, conv_out = refs[5 + n_in : 8 + n_in]
-    outs = refs[8 + n_in : 8 + 2 * n_in]
-    (gwin_s, taps_s, dw_s, w_s, wp_s, tiles, send, recv, msend, mrecv, hsend, hrecv, nsend, nrecv, wsem) = refs[8 + 2 * n_in : 23 + 2 * n_in]
-    bufs = refs[23 + 2 * n_in :]
+    cut_ref, cols_ref, grad_ref, conv_ref = refs[:4]
+    parts = refs[4 : 4 + n_in]
+    dx_ref, norm_ref, conv_out = refs[4 + n_in : 7 + n_in]
+    outs = refs[7 + n_in : 7 + 2 * n_in]
+    (gwin_s, taps_s, cols_s, dw_s, w_s, wp_s, send, recv, msend, mrecv, hsend, hrecv, wsem, csem) = refs[7 + 2 * n_in : 21 + 2 * n_in]
+    bufs = refs[21 + 2 * n_in :]
     cut, last = cut_ref[0], cut_ref[1]
     greet(plane=True)
     halo_start(grad_ref, gwin_s, hsend, hrecv)
@@ -1121,51 +1062,67 @@
     begin = jnp.where(cut <= HALF, 2 * HALF, HALF)
     end = jnp.where(last > 0, EXT, jnp.where(cut <= HALF + OWN, OWN + 2 * HALF, OWN + HALF))
 
-    def weights(g, unused):
-        taps = taps_of(take_rows(gwin_s, g, cut))
-        taps_s[g] = taps
-        row = lax.broadcasted_iota(jnp.int32, (ZROWS, 512), 0) + HALF
-        own = jnp.where((row >= begin) & (row < end), taps[HALF : HALF + ZROWS].astype(jnp.float32), 0.0).astype(jnp.bfloat16)
-        cols = im2col(take_rows(win_ref, g, cut), ZROWS)
-        dw = lax.dot_general(own, cols, (((0,), (0,)), ((), ())), preferred_element_type=jnp.float32).astype(jnp.bfloat16)
+    def pick(k):
+        return pltpu.make_async_copy(cols_ref.at[pl.ds(2 * k, 2)], cols_s.at[k % 2], csem.at[k % 2])
+
+    pick(0).start()
+    row = lax.broadcasted_iota(jnp.int32, (ZROWS, 256), 0) + HALF
+    owned = (row >= begin) & (row < end)
+    by_slot = spaced(side_steps[1:], 8)
+
+    def product(k, m, taps, half):
+        own = jnp.concatenate([taps[HALF : HALF + ZROWS, h * 256 + half * 128 : h * 256 + half * 128 + 128] for h in range(2)], axis=1)
+        own = jnp.where(owned, own.astype(jnp.float32), 0.0).astype(jnp.bfloat16)
+        dw = lax.dot_general(own, cols_s[k % 2, m], (((0,), (0,)), ((), ())), preferred_element_type=jnp.float32).astype(jnp.bfloat16)
         for h in range(2):
-            for a in range(8):
-                dw_s[g // 4, (g // 2) % 2, g % 2, h, a] = dw[h * 256 + a * 32 : h * 256 + a * 32 + 24]
+            for a in range(4):
+                dw_s[k // 2, k % 2, m, h, 4 * half + a] = dw[h * 128 + a * 32 : h * 128 + a * 32 + 24]
+
+    def weights_low(k, unused):
+        pick((k + 1) % 8).start()
+        pick(k).wait()
+        taps = [taps_of(take_rows(gwin_s, 2 * k + m, cut)) for m in range(2)]
+        for m in range(2):
+            taps_s[2 * k + m] = taps[m]
+            product(k, m, taps[m], 0)
+        go_at(k, by_slot)
         return unused
 
-    def inputs(g, unused):
-        z, x, y = g // 4, (g // 2) % 2, g % 2
-        for h in range(2):
-            for a in range(8):
-                wp_s[h * 256 + a * 32 : h * 256 + a * 32 + 24, :] = w_s[z % 2, x, y, h, a]
-        out = jnp.dot(taps_s[g], wp_s[...], preferred_element_type=jnp.float32)
-        put_group(dx_ref, g, pick_own(fold_back(out), cut))
+    lax.fori_loop(0, 8, weights_low, 0)
+    soon = max(len(main) // 4, 1)
+    by_slot = spaced(main_steps[:soon], 8)
+
+    def weights_high(k, unused):
+        go_at(k, by_slot)
+        pl.when(k < 7)(lambda: pick(k + 1).start())
+        pick(k).wait()
+        for m in range(2):
+            product(k, m, taps_s[2 * k + m], 1)
         return unused
 
-    by_slot = spaced(side_steps[1:], 8)
-    for k in range(8):
-        lax.fori_loop(2 * k, 2 * k + 2, weights, 0)
-        for step in by_slot[k]:
-            go(step)
-    by_slot = spaced(main_steps, 8)
-    for k in range(8):
-        for step in by_slot[k]:
-            go(step)
-        if k % 2 == 0:
-            load(k // 2).wait()
-        lax.fori_loop(2 * k, 2 * k + 2, inputs, 0)
-        if k % 2 == 1 and k < 4:
-            load(k // 2 + 2).start()
+    lax.fori_loop(0, 8, weights_high, 0)
+    more = spaced(main_steps[soon:], 8)
+
+    def inputs(k, unused):
+        go_at(k, more)
+        pl.when(k % 2 == 0)(lambda: load(k // 2).wait())
+        for m in range(2):
+            for h in range(2):
+                for a in range(8):
+                    wp_s[m, h * 256 + a * 32 : h * 256 + a * 32 + 24, :] = w_s[(k // 2) % 2, k % 2, m, h, a]
+        outs = [jnp.dot(taps_s[2 * k + m], wp_s[m], preferred_element_type=jnp.float32) for m in range(2)]
+        for m in range(2):
+            put_group(dx_ref, 2 * k + m, pick_own(fold_back(outs[m]), cut))
+        pl.when((k % 2 == 1) & (k < 4))(lambda: load(k // 2 + 2).start())
+        return unused
+
+    lax.fori_loop(0, 8, inputs, 0)
     for unit in side + main:
         unit.finish()
-    z, x, y, c = spot()
-    mine = tiles.at[x * 4 + y * 2 + c]
-    square_sum([conv_out] + list(outs), mine)
-    mine[...] += tile_ref[...]
-    total_square(norm_ref, tiles, nsend, nrecv)
-
-
-def close_step(cut, window, grad, conv, tile, parts, side_plan, main_plan, collective_id=2):
+    square_sum([conv_out] + list(outs), norm_ref)
+
+
+def close_step(cut, columns, grad, conv, parts, side_plan, main_plan, collective_id=2):
     n = len(parts)
     shapes = [p.shape[4:] for p in parts]
     vmem = pl.BlockSpec(memory_space=pltpu.VMEM)
@@ -1174,7 +1131,7 @@
     low = jnp.bfloat16
     return pl.pallas_call(
         functools.partial(close_kernel, side_plan, main_plan, n),
-        in_specs=[pl.BlockSpec(memory_space=pltpu.SMEM), vmem, vmem, anywhere, vmem] + [anywhere] * n,
+        in_specs=[pl.BlockSpec(memory_space=pltpu.SMEM), anywhere, vmem, anywhere] + [anywhere] * n,
         out_specs=[vmem] * (3 + n),
         out_shape=[
             jax.ShapeDtypeStruct((OWN, 768), jnp.float32),
@@ -1185,17 +1142,40 @@
         scratch_shapes=[
             pltpu.VMEM((WIN, 768), low),
             pltpu.VMEM((16, EXT, 512), low),
+            pltpu.VMEM((2, 2, ZROWS, 768), low),
             pltpu.VMEM(conv.shape, low),
             pltpu.VMEM((2,) + conv.shape[1:], low),
-            pltpu.VMEM((512, 768), low),
-            pltpu.VMEM((12, 8, 128), jnp.float32),
+            pltpu.VMEM((2, 512, 768), low),
             sem((len(side_plan), 9)), sem((len(side_plan), 10)), sem((len(main_plan), 9)), sem((len(main_plan), 10)),
-            sem((2,)), sem((2,)), sem((11,)), sem((11,)), sem((2,)),
+            sem((2,)), sem((2,)), sem((2,)), sem((2,)),
         ]
         + collect_scratch(side_plan, shapes, low, ())
         + collect_scratch(main_plan, [conv.shape[4:]], low, (0,)),
         compiler_params=pltpu.CompilerParams(collective_id=collective_id, has_side_effects=True, vmem_limit_bytes=60 * 2**20),
-    )(cut, window, grad, conv, tile, *parts)
+    )(cut, columns, grad, conv, *parts)
+
+
+def norm_kernel(n_in, *refs):
+    ins, norm_ref, tiles, send, recv = refs[:n_in], refs[n_in], refs[n_in + 1], refs[n_in + 2], refs[n_in + 3]
+    greet(plane=True)
+    z, x, y, c = spot()
+    mine = tiles.at[x * 4 + y * 2 + c]
+    square_sum(ins[1:], mine)
+    mine[...] += ins[0][...]
+    total_square(norm_ref, tiles, send, recv)
+
+
+def norm_step(tile, sums, collective_id=5):
+    n = 1 + len(sums)
+    vmem = pl.BlockSpec(memory_space=pltpu.VMEM)
+    return pl.pallas_call(
+        functools.partial(norm_kernel, n),
+        in_specs=[vmem] * n,
+        out_specs=vmem,
+        out_shape=jax.ShapeDtypeStruct((8, 128), jnp.float32),
+        scratch_shapes=[pltpu.VMEM((12, 8, 128), jnp.float32), pltpu.SemaphoreType.DMA((11,)), pltpu.SemaphoreType.DMA((11,))],
+        compiler_params=pltpu.CompilerParams(collective_id=collective_id, has_side_effects=True, vmem_limit_bytes=32 * 2**20),
+    )(tile, *sums)
 
 
 S = slice
@@ -1208,28 +1188,31 @@
     ]
 
 
-GATHER = ("zxy", "zyx", "xzy", "yzx")
-REDUCE = ("yxz", "xyz", "yzx", "xzy")
-
-
 def open_plan():
-    return sliced(0, 0, 8, 8, GATHER) + sliced(1, 1, 2304, 2, GATHER) + [(3, (), "zxy"), (2, (), "yzx")]
+    even = ("xy", "yx")
+    return sliced(0, 0, 8, 8, even) + sliced(1, 1, 2304, 2, even) + [(3, (), "xy"), (2, (), "yx")]
 
 
 def attend_plan():
-    return sliced(0, 1, 3072, 4, GATHER) + sliced(1, 0, 96, 3, GATHER[1:])
+    return sliced(0, 1, 3072, 4, ("yx",)) + sliced(1, 0, 96, 3, ("yx",))
 
 
 def attend_back_plan():
-    return sliced(2, 0, 96, 3, REDUCE) + sliced(1, 1, 3072, 4, REDUCE, 3) + [(0, (), "yxz")]
+    plan = []
+    for a in range(3):
+        plan += [(1, (S(32 * a, 32 * a + 32), S(384 * i, 384 * i + 384)), ("xy", "yx")[i]) for i in range(2)]
+    return plan + [(0, (), "xy")]
 
 
 def side_plan():
-    return sliced(0, 1, 2304, 3, REDUCE) + [(1, (), "xyz")]
+    return sliced(0, 1, 2304, 2, ("xy", "yx")) + [(1, (), "xy")]
 
 
 def main_plan():
-    return sliced(0, 0, 8, 8, REDUCE)
+    plan = []
+    for a in range(8):
+        plan += [(0, (S(a, a + 1), S(None), S(384 * i, 384 * i + 384)), ("xy", "yx")[i]) for i in range(2)]
+    return plan
 
 
 def by_chips():
@@ -1295,9 +1278,10 @@
     cut = jnp.stack([cut, (head_index == head_groups - 1).astype(jnp.int32)]).astype(jnp.int32)
     if by_chips():
         early = own_parts[:3] + own_parts[5:]
-        conv_pre, window, *parts = open_step(cut, frames, early, open_plan(), (1, 3))
+        conv_pre, conv_columns, *parts = open_step(cut, frames, early, open_plan(), (1, 3))
         all_conv, all_qkv, all_proj, all_small = [w.reshape((32,) + w.shape[4:]) for w in parts]
         whole_conv = parts[0]
+        all_up, all_down = gather_weights(own_parts[3:5])
     else:
         all_conv, all_qkv, all_proj, all_up, all_down, all_small = gather_weights(own_parts)
     full_qkv = all_qkv.reshape(model_width, -1)
@@ -1324,7 +1308,7 @@
         lax.dot_general(full_qkv, attn_in, (((0,), (1,)), ((), ())), preferred_element_type=f32) + qkv_bias[:, None]
     ).astype(low_type)
     if by_chips():
-        heads_qkv, context, log_sums, context_wide, all_up, all_down = attend(seg_rows, packed, own_parts[3:5], attend_plan())
+        heads_qkv, context, log_sums, context_wide = attend(seg_rows, packed, [], [])
     else:
         blocks = trade(by_partner(packed.reshape(head_groups, -1, row_count)))
         fwd = attn_fwd(seg_rows, blocks)
@@ -1356,8 +1340,9 @@
         g.reshape((count,) + w.shape) for g, w in ((grad_proj, proj_weight), (grad_up, up_weight), (grad_down, down_weight))
     ]
     if by_chips():
-        grad_packed, square_tile, sum_proj, sum_up, sum_down = attend_back(
-            seg_rows, heads_qkv, log_sums, context_wide, grad_context, [by_owner(g) for g in (grad_proj, grad_up, grad_down)], attend_back_plan()
+        sum_up = lax.psum_scatter(grad_up, ("seq", "head"), scatter_dimension=0, tiled=False).astype(f32)
+        grad_packed, square_tile, sum_proj, sum_down = attend_back(
+            seg_rows, heads_qkv, log_sums, context_wide, grad_context, [by_owner(grad_proj), by_owner(grad_down)], attend_back_plan()
         )
     else:
         grad_blocks = trade(by_partner(grad_context.reshape(head_groups, -1, row_count)))
@@ -1384,9 +1369,9 @@
     grad_qkv = grad_qkv.reshape((count,) + qkv_weight.shape)
     if by_chips():
         grad_frames_conv, norm_tile, sum_conv, sum_qkv, sum_small = close_step(
-            cut, window, grad_conv_low, whole_conv, square_tile, [by_owner(grad_qkv), by_owner(grad_small)], side_plan(), main_plan()
+            cut, conv_columns, grad_conv_low, whole_conv, [by_owner(grad_qkv), by_owner(grad_small)], side_plan(), main_plan()
         )
-        square_total = jnp.sum(norm_tile)
+        square_total = jnp.sum(norm_step(norm_tile + square_tile, [sum_up]))
     else:
         grad_window = with_halo(grad_conv_low, (("head", 0),), half_kernel)
         grad_frames_conv, grad_conv = conv_bwd(cut, window, grad_window, full_conv)

time: 535 us -> 499 us (0.933)
  Pallas kernels: 400 us -> 360 us
  between operations: 4.32 us -> 17.4 us
  local copies, waits for them, and re-layouts: 24.5 us -> 14 us
    pallas_call x1, Pallas kernels: 83 us -> 56.1 us  [attend(): pl.pallas_call(functools.partial(attend_kernel, plan, n), in_specs=[vmem,...]
    pallas_call x1, Pallas kernels: 126 us -> 102 us  [close_step(): pl.pallas_call(functools.partial(close_kernel, side_plan, main_plan, n),...]
    pallas_call x1, Pallas kernels: 91.6 us -> 108 us  [open_step(): pl.pallas_call(functools.partial(open_kernel, plan, n, early), in_specs=[...]
    pallas_call x1, Pallas kernels: 99.5 us -> 85.2 us  [attend_back(): pl.pallas_call(functools.partial(attend_back_kernel, plan, n), in_specs=[...]
    pallas_call x0 -> x1, Pallas kernels: none -> 8.9 us  [norm_step(): pl.pallas_call(functools.partial(norm_kernel, n), in_specs=[vmem] * n, ou...]
    unnamed x149 -> x107, local copies, waits for them, and re-layouts: 13.1 us -> 7.07 us
  transfers between devices with their start and end apart: 0 -> 3, of which waited for: 0 -> 0; matrix products, arithmetic and copies ran while one was open for 0% -> 16% of each run, Pallas kernels for 0% -> 71%
where the time goes in v3:
time: 499 us; the launch traced here: 496 us
  Pallas kernels  360 us (72%)
  matrix products  71 us (14%)
  other arithmetic  32.5 us (7%)
  between operations  17.4 us (3%)
  local copies, waits for them, and re-layouts  14 us (3%)
    pallas_call x1, Pallas kernels, open_step(): pl.pallas_call(functools.partial(open_kernel, plan, n, early), in_specs=[...  108 us
    pallas_call x1, Pallas kernels, close_step(): pl.pallas_call(functools.partial(close_kernel, side_plan, main_plan, n),...  102 us
    pallas_call x1, Pallas kernels, attend_back(): pl.pallas_call(functools.partial(attend_back_kernel, plan, n), in_specs=[...  85.2 us
    pallas_call x1, Pallas kernels, attend(): pl.pallas_call(functools.partial(attend_kernel, plan, n), in_specs=[vmem,...  56.1 us
    dot_general x1, matrix products, shards(): jnp.dot(ffn_in, full_up, preferred_element_type=f32) + full_ffn  20.2 us
  transfers between devices with their start and end apart: 3, of which 0 were waited for; matrix products, arithmetic and copies ran while one was open for 16% of the time, Pallas kernels for 71%

profile of v3, /device:TPU:0, one launch (start us, length us, event | category | flops | bytes accessed | tf_op | source)
XLA Modules:
  0.0 495.5 jit_solution(11586393014490205784)
XLA Ops:
  7.2 1.7 convert_element_type.117
  9.0 1.6 convert_element_type.119
  11.2 2.0 fusion.41
  19.2 108.0 %shard_map.415 = (f32[512,768]{1,0:T(8,128)}, bf16[16,584,768]{2,1,0:T(8,128)(2,1)}, bf16[4,2,2,2,8,24,768]{6,5,4,3,2,1,0:T(8,128)(2,1)}, bf16[4,2,2,2,24,2304]{...) custom-call(s32[2]{0:T(128)} %pad_add_fusion.1.refs_0_, ...), custom_call_target="tpu_custom_call" | custom-call | tf_op jit(solution)/shard_map/pallas_call | solution.py:745
  130.4 4.6 multiply_add_fusion.1
  135.0 3.7 fusion.6.refs_1_
  138.7 56.1 %shard_map.416 = (bf16[576,2048]{1,0:T(8,128)(2,1)}, bf16[768,512]{1,0:T(8,128)(2,1)S(1)}, f32[3,1,2048]{2,1,0:T(1,128)S(1)}, f32[192,2048]{1,0:T(8,128)S(1)}) custom-call(s32[1,2048]{1,0:T(1,128)S(1)} %pad_add_fusion.refs_0_, bf16[2304,512]{1,0:T(8,128)(2,1)} %fusion.6.refs_1_), custom_call_target="tpu_custom_call" | custom-call | tf_op jit(solution)/shard_map/pallas_call | solution.py:896
  196.4 20.2 %multiply_convert_fusion = (bf16[512,3072]{1,0:T(8,128)(2,1)}, f32[512,3072]{1,0:T(8,128)}, f32[512,3072]{1,0:T(8,128)}) fusion(f32[3072]{0:T(1024)S(1)} %add.258, bf16[768,3072]{1,0:T(8,128)(2,1)} %all-gather.5.cloned.1.call-done, f32[512,768]{1,0:T(8,128)S(1)} %get-tuple-element.195, f32[768]{0:T(1024)S(1)} %add.255, f32[768]{0:T(1024)S(1)} %mul.501, ...), kind=kOutput, calls=%fused_computation.3 | convolution fusion | flops 2521694208 | bytes 22042624 | tf_op jit(solution)/shard_map/dot_general | solution.py:1321
  216.6 6.2 %fusion.59 = (f32[512]{0:T(512)S(1)}, f32[512,768]{1,0:T(8,128)S(1)}) fusion(f32[768]{0:T(1024)S(1)} %add.262, bf16[512,3072]{1,0:T(8,128)(2,1)} %get-tuple-element.176, bf16[3072,768]{1,0:T(8,128)(2,1)} %all-gather.7.cloned.1.call-done, f32[768]{0:T(1024)S(1)} %add.255, f32[768]{0:T(1024)S(1)} %mul.501, f32[512]{0:T(512)S(1)} %fusion.35, ...), kind=kOutput, calls=%fused_computation.147 | convolution fusion | flops 2418671104 | bytes 11025408 | tf_op jit(solution)/shard_map/dot_general | solution.py:1323
  227.7 7.0 %fusion.52 = (bf16[3072]{0:T(1024)(128)(2,1)S(1)}, bf16[512,3072]{1,0:T(8,128)(2,1)S(1)}) fusion(f32[512,3072]{1,0:T(8,128)S(1)} %copy-done.46, f32[512,3072]{1,0:T(8,128)} %get-tuple-element.196, f32[3072]{0:T(1024)S(1)} %add.258, bf16[512,768]{1,0:T(8,128)(2,1)S(1)} %get-tuple-element.165, bf16[3072,768]{1,0:T(8,128)(2,1)S(1)} %copy-done.40), kind=kOutput, calls=%fused_computation.142 | convolution fusion | flops 2441081856 | bytes 21252096 | tf_op jit(solution)/shard_map/td,fd->tf/dot_general | solution.py:1329
  234.7 5.0 %convolution_convert_fusion = bf16[768,3072]{1,0:T(8,128)(2,1)} fusion(bf16[512,3072]{1,0:T(8,128)(2,1)S(1)} %get-tuple-element.171, f32[512,768]{1,0:T(8,128)S(1)} %get-tuple-element.195, f32[768]{0:T(1024)S(1)} %add.255, f32[768]{0:T(1024)S(1)} %mul.501, f32[512]{0:T(512)S(1)} %fusion.35, f32[512]{0:T(512)S(1)} %broadcast_multiply_fusion.2), kind=kOutput, calls=%fused_computation.17 | convolution fusion | flops 2420244480 | bytes 9447424 | tf_op jit(solution)/shard_map/td,tf->df/dot_general | solution.py:1331
  240.1 6.8 %multiply_reduce_fusion = (bf16[768]{0:T(1024)(128)(2,1)S(1)}, f32[512]{0:T(512)S(1)}, bf16[768]{0:T(1024)(128)(2,1)S(1)}, f32[512,768]{1,0:T(8,128)S(1)}) fusion(f32[512,768]{1,0:T(8,128)S(1)} %get-tuple-element.195, f32[512]{0:T(512)S(1)} %fusion.35, f32[512]{0:T(512)S(1)} %broadcast_multiply_fusion.2, f32[768]{0:T(1024)S(1)} %mul.501, ...), kind=kOutput, calls=%fused_computation.32 | convolution fusion | flops 2419849216 | bytes 12597248 | tf_op jit(solution)/shard_map/tf,df->td/dot_general | solution.py:1333
  247.9 1.6 copy-done.43
  249.5 1.7 convolution_convert_fusion.4.refs_4_
  251.2 1.8 convolution_convert_fusion.3
  253.0 4.3 convolution_convert_fusion.2
  257.3 85.2 %shard_map.417 = (bf16[2304,512]{1,0:T(8,128)(2,1)}, f32[8,128]{1,0:T(8,128)}, f32[24,768]{1,0:T(8,128)}, f32[96,768]{1,0:T(8,128)}) custom-call(s32[1,2048]{1,0:T(1,128)} %copy-done.1, bf16[576,2048]{1,0:T(8,128)(2,1)} %get-tuple-element.48.refs_1_, f32[3,1,2048]{2,1,0:T(1,128)} %copy-done.2, f32[192,2048]{1,0:T(8,128)} %copy-done, ...), custom_call_target="tpu_custom_call" | custom-call | tf_op jit(solution)/shard_map/pallas_call | solution.py:1014
  342.5 2.2 reduce.6
  344.7 7.3 %fusion.51 = (bf16[768]{0:T(1024)(128)(2,1)S(1)}, bf16[512,768]{1,0:T(8,128)(2,1)}, f32[512,768]{1,0:T(8,128)}) fusion(f32[512,768]{1,0:T(8,128)} %get-tuple-element.179, f32[512,768]{1,0:T(8,128)S(1)} %copy-done.11, f32[768]{0:T(1024)S(1)} %add.239, bf16[2304,512]{1,0:T(8,128)(2,1)} %get-tuple-element.51, bf16[768,2304]{1,0:T(8,128)(2,1)} %bitcast.85, ...), kind=kOutput, calls=%fused_computation.141 | convolution fusion | flops 1819016448 | bytes 12982784 | tf_op jit(solution)/shard_map/dot_general | solution.py:1354
  354.0 6.0 %convolution_convert_fusion.1 = bf16[768,2304]{1,0:T(8,128)(2,1)} fusion(bf16[2304,512]{1,0:T(8,128)(2,1)} %get-tuple-element.51, f32[512,768]{1,0:T(8,128)} %copy-done.12), kind=kOutput, calls=%fused_computation.18 | convolution fusion | flops 1814102016 | bytes 7471104 | tf_op jit(solution)/shard_map/dot_general | solution.py:1350
  360.1 102.2 %shard_map.418 = (f32[512,768]{1,0:T(8,128)}, f32[8,128]{1,0:T(8,128)}, f32[8,24,768]{2,1,0:T(8,128)}, f32[24,2304]{1,0:T(8,128)}, f32[16,128]{1,0:T(8,128)}) custom-call(s32[2]{0:T(128)} %pad_add_fusion.1.refs_0_, bf16[16,584,768]{2,1,0:T(8,128)(2,1)} %get-tuple-element.52.refs_1_, bf16[512,768]{1,0:T(8,128)(2,1)} %get-tuple-element.169.refs_2_, ...), custom_call_target="tpu_custom_call" | custom-call | tf_op jit(solution)/shard_map/pallas_call | solution.py:1132
  462.3 2.8 add.271
  466.1 8.9 %shard_map.419 = f32[8,128]{1,0:T(8,128)S(1)} custom-call(f32[8,128]{1,0:T(8,128)S(1)} %add.272.refs_0_, f32[24,3072]{1,0:T(8,128)S(1)} %bitcast_convert_fusion.refs_1_), custom_call_target="tpu_custom_call" | custom-call | tf_op jit(solution)/shard_map/pallas_call | solution.py:1171
  480.5 2.1 multiply_subtract_fusion.3
  (201 shorter events, 29.0 us)
Async XLA Ops:
  7.2 6.7 %copy-start.8 = (f32[128,24,48]{0,2,1:T(8,128)S(1)}, f32[128,24,48]{0,2,1:T(8,128)}, u32[]{:S(2)}) copy-start(f32[128,24,48]{0,2,1:T(8,128)} %param.31) | copy-start | bytes 1769476
  7.2 189.1 %all-gather.5.cloned.1.call-start = ((), (), s32[]{:S(2)}) async-start(), calls=%async_computation.2 | async-start | bytes 4866048 | tf_op jit(solution)/shard_map/all_gather | solution.py:1223
  9.0 207.6 %all-gather.7.cloned.1.call-start = ((), (), s32[]{:S(2)}) async-start(), calls=%async_computation.3 | async-start | bytes 4866048 | tf_op jit(solution)/shard_map/all_gather | solution.py:1223
  10.7 454.5 %reduce-scatter.2.cloned.1.call-start = ((), (), s32[]{:S(2)}) async-start(), calls=%async_computation.1 | async-start | bytes 4866048 | tf_op jit(solution)/shard_map/reduce_scatter | solution.py:1343
  16.5 113.8 %copy-start.7 = (bf16[512,768]{1,0:T(8,128)(2,1)S(1)}, bf16[512,768]{1,0:T(8,128)(2,1)}, u32[]{:S(2)}) copy-start(bf16[512,768]{1,0:T(8,128)(2,1)} %refs_1_.1) | copy-start | bytes 2359300
  130.3 8.3 %copy-start.1 = (s32[1,2048]{1,0:T(1,128)}, s32[1,2048]{1,0:T(1,128)S(1)}, u32[]{:S(2)}) copy-start(s32[1,2048]{1,0:T(1,128)S(1)} %pad_add_fusion.refs_0_) | copy-start | bytes 24580
  130.4 4.6 copy-start.41
  135.0 59.9 %copy-start.12 = (f32[512,768]{1,0:T(8,128)}, f32[512,768]{1,0:T(8,128)S(1)}, u32[]{:S(2)}) copy-start(f32[512,768]{1,0:T(8,128)S(1)} %get-tuple-element.178) | copy-start | bytes 4718596
  138.7 56.2 %copy-start.42 = (bf16[4,2,2,2,24,768]{5,4,3,2,1,0:T(8,128)(2,1)S(1)}, bf16[4,2,2,2,24,768]{5,4,3,2,1,0:T(8,128)(2,1)}, u32[]{:S(2)}) copy-start(bf16[4,2,2,2,24,768]{5,4,3,2,1,0:T(8,128)(2,1)} %get-tuple-element.47) | copy-start | bytes 3538948
  216.6 11.1 %copy-start.46 = (f32[512,3072]{1,0:T(8,128)S(1)}, f32[512,3072]{1,0:T(8,128)}, u32[]{:S(2)}) copy-start(f32[512,3072]{1,0:T(8,128)} %get-tuple-element.177) | copy-start | bytes 18874372
  227.7 7.0 %copy-start.17 = (bf16[512,768]{1,0:T(8,128)(2,1)}, bf16[512,768]{1,0:T(8,128)(2,1)S(1)}, u32[]{:S(2)}) copy-start(bf16[512,768]{1,0:T(8,128)(2,1)S(1)} %get-tuple-element.165) | copy-start | bytes 2359300
  234.7 5.0 %copy-start.44 = (bf16[512,3072]{1,0:T(8,128)(2,1)}, bf16[512,3072]{1,0:T(8,128)(2,1)S(1)}, u32[]{:S(2)}) copy-start(bf16[512,3072]{1,0:T(8,128)(2,1)S(1)} %get-tuple-element.171) | copy-start | bytes 9437188
  247.6 3.6 copy-start.4
  249.5 3.5 copy-start.45
  257.3 87.4 %copy-start.11 = (f32[512,768]{1,0:T(8,128)S(1)}, f32[512,768]{1,0:T(8,128)}, u32[]{:S(2)}) copy-start(f32[512,768]{1,0:T(8,128)} %get-tuple-element.43) | copy-start | bytes 4718596
  360.1 102.2 %copy-start.13 = (f32[512,768]{1,0:T(8,128)S(1)}, f32[512,768]{1,0:T(8,128)}, u32[]{:S(2)}) copy-start(f32[512,768]{1,0:T(8,128)} %get-tuple-element.200) | copy-start | bytes 4718596
  462.3 14.0 %copy-start.20 = (f32[8,24,768]{2,1,0:T(8,128)S(1)}, f32[8,24,768]{2,1,0:T(8,128)}, u32[]{:S(2)}) copy-start(f32[8,24,768]{2,1,0:T(8,128)} %get-tuple-element.60) | copy-start | bytes 1769476
  477.7 4.8 copy-start.29
  477.8 4.8 copy-start.30
  478.2 4.3 copy-start.31
  478.2 5.0 %copy-start.14 = (f32[96,768]{1,0:T(8,128)S(1)}, f32[96,768]{1,0:T(8,128)}, u32[]{:S(2)}) copy-start(f32[96,768]{1,0:T(8,128)} %param.30) | copy-start | bytes 884740
  478.3 5.0 %copy-start.23 = (f32[96,768]{1,0:T(8,128)S(1)}, f32[96,768]{1,0:T(8,128)}, u32[]{:S(2)}) copy-start(f32[96,768]{1,0:T(8,128)} %param.37) | copy-start | bytes 884740
  478.3 5.0 %copy-start.24 = (f32[96,768]{1,0:T(8,128)S(1)}, f32[96,768]{1,0:T(8,128)}, u32[]{:S(2)}) copy-start(f32[96,768]{1,0:T(8,128)} %param.44) | copy-start | bytes 884740
  478.3 5.0 %copy-start.25 = (f32[96,768]{1,0:T(8,128)S(1)}, f32[96,768]{1,0:T(8,128)}, u32[]{:S(2)}) copy-start(f32[96,768]{1,0:T(8,128)} %get-tuple-element.59) | copy-start | bytes 884740
  (26 other events, 53.8 us)
Sparse Core Ops, SparseCore 0:
  11.5 78.5 all-gather.4
  93.6 72.3 all-gather.6
  239.9 122.6 reduce-scatter.1

commit v4 on v3

--- a/solution.py
+++ b/solution.py
@@ -1176,6 +1176,114 @@
         scratch_shapes=[pltpu.VMEM((12, 8, 128), jnp.float32), pltpu.SemaphoreType.DMA((11,)), pltpu.SemaphoreType.DMA((11,))],
         compiler_params=pltpu.CompilerParams(collective_id=collective_id, has_side_effects=True, vmem_limit_bytes=32 * 2**20),
     )(tile, *sums)
+
+
+FCH = 512
+
+
+def norm_of(h, gain, shift):
+    center = h - jnp.mean(h, axis=1, keepdims=True)
+    r = lax.rsqrt(jnp.mean(center * center, axis=1, keepdims=True) + norm_eps)
+    z = center * r
+    return z, r, z * gain + shift
+
+
+def norm_back(g, z, r, gain):
+    gz = g * gain
+    return r * (gz - jnp.mean(gz, axis=1, keepdims=True) - z * jnp.mean(gz * z, axis=1, keepdims=True))
+
+
+def gelu_both(v):
+    phi = 0.5 + 0.5 * lax.erf(v * (0.5**0.5))
+    return v * phi, phi + v * (jnp.exp(-0.5 * v * v) * 0.3989422804014327)
+
+
+def ffn_kernel(
+    ctx_ref, proj_ref, up_ref, down_ref, h1_ref, og_ref, vec_ref, fb_ref,
+    out_ref, mid_ref, gup_ref, gffn_ref, fin_ref, gtwo_ref, gattn_ref, gctx_ref, gvec_ref, gfb_ref,
+    proj_s, up_s, down_s, slope_s, z_s, acc_s, g3_s, sem,
+):
+    f32, low = jnp.float32, jnp.bfloat16
+    chunks = fb_ref.shape[1] // FCH
+    nt = (((1,), (1,)), ((), ()))
+
+    def fetch(k):
+        if k == 0:
+            return pltpu.make_async_copy(proj_ref, proj_s, sem.at[0])
+        j = (k - 1) // 2
+        if k % 2:
+            return pltpu.make_async_copy(up_ref.at[:, j * FCH : j * FCH + FCH], up_s.at[j], sem.at[k])
+        return pltpu.make_async_copy(down_ref.at[j * FCH : j * FCH + FCH, :], down_s.at[j], sem.at[k])
+
+    for k in range(1 + 2 * chunks):
+        fetch(k).start()
+    row = lambda n: vec_ref[n : n + 1, :]
+    fetch(0).wait()
+    attn = lax.dot_general(ctx_ref[...], proj_s[...], (((0,), (0,)), ((), ())), preferred_element_type=f32)
+    z1, r1, n1 = norm_of(h1_ref[...] + (attn + row(3)), row(4), row(5))
+    z_s[...] = z1
+    acc_s[...] = n1 + row(6)
+    fin_ref[...] = n1.astype(low)
+    for j in range(chunks):
+        fetch(1 + 2 * j).wait()
+        at = slice(j * FCH, j * FCH + FCH)
+        pre = jnp.dot(fin_ref[...], up_s[j], preferred_element_type=f32) + fb_ref[:, at]
+        act, slope = gelu_both(pre)
+        slope_s[:, at] = slope
+        mid_ref[:, at] = act.astype(low)
+        fetch(2 + 2 * j).wait()
+        acc_s[...] += jnp.dot(mid_ref[:, at], down_s[j], preferred_element_type=f32)
+    z3, r3, out = norm_of(acc_s[...], row(7), row(8))
+    out_ref[...] = out.astype(low)
+    og = og_ref[...].astype(f32)
+    gvec_ref[7:8, :] = jnp.sum(og * z3, axis=0, keepdims=True)
+    gvec_ref[8:9, :] = jnp.sum(og, axis=0, keepdims=True)
+    g3 = norm_back(og, z3, r3, row(7))
+    g3_s[...] = g3
+    gffn_ref[...] = g3.astype(low)
+    gvec_ref[6:7, :] = jnp.sum(gffn_ref[...].astype(f32), axis=0, keepdims=True)
+    for j in range(chunks):
+        at = slice(j * FCH, j * FCH + FCH)
+        gu = (lax.dot_general(gffn_ref[...], down_s[j], nt, preferred_element_type=f32) * slope_s[:, at]).astype(low)
+        gup_ref[:, at] = gu
+        gfb_ref[:, at] = jnp.sum(gu.astype(f32), axis=0, keepdims=True)
+        g3_s[...] += lax.dot_general(gu, up_s[j], nt, preferred_element_type=f32)
+    gn = g3_s[...]
+    z1 = z_s[...]
+    gvec_ref[4:5, :] = jnp.sum(gn * z1, axis=0, keepdims=True)
+    gvec_ref[5:6, :] = jnp.sum(gn, axis=0, keepdims=True)
+    g2 = norm_back(gn, z1, r1, row(4))
+    gtwo_ref[...] = g2
+    gattn_ref[...] = g2.astype(low)
+    gvec_ref[3:4, :] = jnp.sum(gattn_ref[...].astype(f32), axis=0, keepdims=True)
+    gctx_ref[...] = lax.dot_general(proj_s[...], gattn_ref[...], nt, preferred_element_type=f32).astype(low)
+
+
+def ffn_step(context, proj, up, down, hidden_one, output_grad, vectors, ffn_bias):
+    rows, width = hidden_one.shape
+    hidden = up.shape[1]
+    low, f32 = jnp.bfloat16, jnp.float32
+    vmem = pl.BlockSpec(memory_space=pltpu.VMEM)
+    anywhere = pl.BlockSpec(memory_space=pl.ANY)
+    shape = jax.ShapeDtypeStruct
+    chunks = hidden // FCH
+    return pl.pallas_call(
+        ffn_kernel,
+        in_specs=[vmem, anywhere, anywhere, anywhere, vmem, vmem, vmem, vmem],
+        out_specs=[vmem] * 10,
+        out_shape=[
+            shape((rows, width), low), shape((rows, hidden), low), shape((rows, hidden), low), shape((rows, width), low),
+            shape((rows, width), low), shape((rows, width), f32), shape((rows, width), low), shape((width, rows), low),
+            shape((9, width), f32), shape((1, hidden), f32),
+        ],
+        scratch_shapes=[
+            pltpu.VMEM((width, width), low), pltpu.VMEM((chunks, width, FCH), low), pltpu.VMEM((chunks, FCH, width), low),
+            pltpu.VMEM((rows, hidden), f32), pltpu.VMEM((rows, width), f32), pltpu.VMEM((rows, width), f32), pltpu.VMEM((rows, width), f32),
+            pltpu.SemaphoreType.DMA((1 + 2 * chunks,)),
+        ],
+        compiler_params=pltpu.CompilerParams(vmem_limit_bytes=56 * 2**20),
+        cost_estimate=pl.CostEstimate(flops=2 * rows * width * (4 * hidden + 2 * width), bytes_accessed=24_000_000, transcendentals=2 * rows * hidden),
+    )(context, proj, up, down, hidden_one, output_grad, vectors, ffn_bias)
 
 
 S = slice
@@ -1315,27 +1423,12 @@
         context = from_partner(trade(fwd[:4]))
     full_up = all_up.reshape(model_width, -1)
     full_down = all_down.reshape(-1, model_width)
-    attn_out = lax.dot_general(context, full_proj, (((0,), (0,)), ((), ())), preferred_element_type=f32) + vectors[3]
-    normed_one, norm_one_back = jax.vjp(layer_norm, hidden_one + attn_out, vectors[4], vectors[5])
-    ffn_in = normed_one.astype(low_type)
-    up_act, up_back = jax.vjp(gelu_exact, jnp.dot(ffn_in, full_up, preferred_element_type=f32) + full_ffn)
-    hidden_mid = up_act.astype(low_type)
-    hidden_three = normed_one + jnp.dot(hidden_mid, full_down, preferred_element_type=f32) + vectors[6]
-    layer_out_full, norm_two_back = jax.vjp(layer_norm, hidden_three, vectors[7], vectors[8])
-    grad_three, grad_gain_two, grad_shift_two = norm_two_back(output_grad.astype(f32))
-    grad_ffn = grad_three.astype(low_type)
+    (
+        layer_out, hidden_mid, grad_up_low, grad_ffn, ffn_in, grad_two, grad_attn, grad_context, grad_rows, grad_ffn_bias
+    ) = ffn_step(context, full_proj, full_up, full_down, hidden_one, output_grad, vectors, full_ffn[None])
     grad_down = jnp.einsum("tf,td->fd", hidden_mid, grad_ffn, preferred_element_type=f32).astype(low_type)
-    grad_down_bias = jnp.sum(grad_ffn.astype(f32), axis=0)
-    (grad_up_pre,) = up_back(jnp.einsum("td,fd->tf", grad_ffn, full_down, preferred_element_type=f32))
-    grad_up_low = grad_up_pre.astype(low_type)
     grad_up = jnp.einsum("td,tf->df", ffn_in, grad_up_low, preferred_element_type=f32).astype(low_type)
-    grad_ffn_bias = jnp.sum(grad_up_low.astype(f32), axis=0)
-    grad_normed = grad_three + jnp.einsum("tf,df->td", grad_up_low, full_up, preferred_element_type=f32)
-    grad_two, grad_gain_one, grad_shift_one = norm_one_back(grad_normed)
-    grad_attn = grad_two.astype(low_type)
     grad_proj = jnp.dot(context, grad_attn, preferred_element_type=f32).astype(low_type)
-    grad_proj_bias = jnp.sum(grad_attn.astype(f32), axis=0)
-    grad_context = lax.dot_general(full_proj, grad_attn, (((1,), (1,)), ((), ())), preferred_element_type=f32).astype(low_type)
     grad_proj, grad_up, grad_down = [
         g.reshape((count,) + w.shape) for g, w in ((grad_proj, proj_weight), (grad_up, up_weight), (grad_down, down_weight))
     ]
@@ -1355,13 +1448,7 @@
     (grad_conv_pre,) = conv_act_back(grad_hidden_one)
     grad_conv_low = grad_conv_pre.astype(low_type)
     grad_conv_bias = jnp.sum(grad_conv_low.astype(f32), axis=0)
-    grad_vectors = jnp.stack(
-        [
-            grad_conv_bias, grad_query_bias, grad_value_bias, grad_proj_bias, grad_gain_one, grad_shift_one,
-            grad_down_bias, grad_gain_two, grad_shift_two,
-        ],
-        axis=0,
-    )
+    grad_vectors = jnp.concatenate([jnp.stack([grad_conv_bias, grad_query_bias, grad_value_bias], axis=0), grad_rows[3:]], axis=0)
     grad_small = jnp.concatenate(
         [grad_vectors.reshape(vec_rows, count, vec_cols).transpose(1, 0, 2).reshape(count, -1), grad_ffn_bias.reshape(count, ffn_cols)], axis=1
     )
@@ -1399,7 +1486,7 @@
         news.append(new_weight)
         first_news.append(first_new)
         second_news.append(second_new)
-    return (layer_out_full.astype(low_type), frames_grad, grad_norm, *news, *first_news, *second_news)
+    return (layer_out, frames_grad, grad_norm, *news, *first_news, *second_news)
 
 
 def solution(mesh):

time: 499 us -> 463 us (0.928)
  matrix products: 71 us -> 29.8 us
  Pallas kernels: 360 us -> 368 us
    dot_general x6 -> x0, matrix products: 42.9 us -> none  [the longest x1 20.2 us: shards(): jnp.dot(ffn_in, full_up, preferred_element_type=f32) + full_ffn]
    pallas_call x0 -> x1, Pallas kernels: none -> 23.9 us  [ffn_step(): pl.pallas_call(ffn_kernel, in_specs=[vmem, anywhere, anywhere, anywhere,...]
    pallas_call x1, Pallas kernels: 85.2 us -> 73.5 us  [attend_back(): pl.pallas_call(functools.partial(attend_back_kernel, plan, n), in_specs=[...]
    pallas_call x1, Pallas kernels: 56.1 us -> 48.3 us  [attend(): pl.pallas_call(functools.partial(attend_kernel, plan, n), in_specs=[vmem,...]
  transfers between devices with their start and end apart: 3 -> 3, of which waited for: 0 -> 0; matrix products, arithmetic and copies ran while one was open for 16% -> 11% of each run, Pallas kernels for 71% -> 73%
where the time goes in v4:
time: 463 us; the launch traced here: 459 us
  Pallas kernels  368 us (79%)
  other arithmetic  29.8 us (6%)
  matrix products  29.8 us (6%)
  between operations  17.1 us (4%)
  local copies, waits for them, and re-layouts  14.6 us (3%)
    pallas_call x1, Pallas kernels, open_step(): pl.pallas_call(functools.partial(open_kernel, plan, n, early), in_specs=[...  111 us
    pallas_call x1, Pallas kernels, close_step(): pl.pallas_call(functools.partial(close_kernel, side_plan, main_plan, n),...  102 us
    pallas_call x1, Pallas kernels, attend_back(): pl.pallas_call(functools.partial(attend_back_kernel, plan, n), in_specs=[...  73.5 us
    pallas_call x1, Pallas kernels, attend(): pl.pallas_call(functools.partial(attend_kernel, plan, n), in_specs=[vmem,...  48.3 us
    pallas_call x1, Pallas kernels, ffn_step(): pl.pallas_call(ffn_kernel, in_specs=[vmem, anywhere, anywhere, anywhere,...  23.9 us
  transfers between devices with their start and end apart: 3, of which 0 were waited for; matrix products, arithmetic and copies ran while one was open for 11% of the time, Pallas kernels for 73%

profile of v4, /device:TPU:0, one launch (start us, length us, event | category | flops | bytes accessed | tf_op | source)
XLA Modules:
  0.0 459.2 jit_solution(17251767150108085482)
XLA Ops:
  7.2 1.7 convert_element_type.83
  9.0 1.6 convert_element_type.84
  12.7 2.0 fusion.19
  15.4 1.5 convert_element_type.75.refs_4_
  16.9 1.6 convert_element_type.74.refs_3_
  19.6 1.5 reshape.125.refs_2_
  22.3 111.4 %shard_map.415 = (f32[512,768]{1,0:T(8,128)}, bf16[16,584,768]{2,1,0:T(8,128)(2,1)}, bf16[4,2,2,2,8,24,768]{6,5,4,3,2,1,0:T(8,128)(2,1)}, bf16[4,2,2,2,24,2304]{...) custom-call(s32[2]{0:T(128)} %pad_add_fusion.1.refs_0_, ...), custom_call_target="tpu_custom_call" | custom-call | tf_op jit(solution)/shard_map/pallas_call | solution.py:745
  137.2 5.8 %multiply_add_fusion = (f32[512,768]{1,0:T(8,128)S(1)}, f32[512,768]{1,0:T(8,128)}) fusion(bf16[512,768]{1,0:T(8,128)(2,1)S(1)} %copy-done.5, f32[512,768]{1,0:T(8,128)} %get-tuple-element.54, f32[768]{0:T(1024)S(1)} %add.164), kind=kLoop, calls=%fused_computation.8 | loop fusion | flops 26345472 | bytes 5508096 | tf_op jit(solution)/shard_map/add | solution.py:1409
  143.1 3.8 fusion.refs_1_
  146.9 48.3 %shard_map.416 = (bf16[576,2048]{1,0:T(8,128)(2,1)}, bf16[768,512]{1,0:T(8,128)(2,1)S(1)}, f32[3,1,2048]{2,1,0:T(1,128)S(1)}, f32[192,2048]{1,0:T(8,128)S(1)}) custom-call(s32[1,2048]{1,0:T(1,128)S(1)} %pad_add_fusion.refs_0_, bf16[2304,512]{1,0:T(8,128)(2,1)} %fusion.refs_1_), custom_call_target="tpu_custom_call" | custom-call | tf_op jit(solution)/shard_map/pallas_call | solution.py:896
  195.2 1.2 copy-done
  197.9 23.9 %shard_map.417 = (bf16[512,768]{1,0:T(8,128)(2,1)}, bf16[512,3072]{1,0:T(8,128)(2,1)}, bf16[512,3072]{1,0:T(8,128)(2,1)}, bf16[512,768]{1,0:T(8,128)(2,1)}, bf16...) custom-call(bf16[768,512]{1,0:T(8,128)(2,1)} %copy-done.3, ...), custom_call_target="tpu_custom_call" | custom-call | flops 10871635968 | bytes 24000000 | tf_op jit(solution)/shard_map/pallas_call | solution.py:1270
  221.8 6.9 %convolution_convert_fusion = bf16[768,3072]{1,0:T(8,128)(2,1)} fusion(bf16[512,768]{1,0:T(8,128)(2,1)} %get-tuple-element.75, bf16[512,3072]{1,0:T(8,128)(2,1)} %get-tuple-element.76), kind=kOutput, calls=%fused_computation | convolution fusion | flops 2418278400 | bytes 8650752 | tf_op jit(solution)/shard_map/td,tf->df/dot_general | solution.py:1430
  230.6 1.8 convolution_convert_fusion.3
  232.8 4.3 convolution_convert_fusion.2
  237.1 73.5 %shard_map.418 = (bf16[2304,512]{1,0:T(8,128)(2,1)}, f32[8,128]{1,0:T(8,128)}, f32[24,768]{1,0:T(8,128)}, f32[96,768]{1,0:T(8,128)}) custom-call(s32[1,2048]{1,0:T(1,128)} %copy-done.1, bf16[576,2048]{1,0:T(8,128)(2,1)} %get-tuple-element.60.refs_1_, f32[3,1,2048]{2,1,0:T(1,128)} %copy-done.2, f32[192,2048]{1,0:T(8,128)} %copy-done, ...), custom_call_target="tpu_custom_call" | custom-call | tf_op jit(solution)/shard_map/pallas_call | solution.py:1014
  310.6 7.8 %fusion.32 = (bf16[768]{0:T(1024)(128)(2,1)S(1)}, bf16[512,768]{1,0:T(8,128)(2,1)}, f32[512,768]{1,0:T(8,128)}) fusion(f32[512,768]{1,0:T(8,128)} %get-tuple-element.158, f32[512,768]{1,0:T(8,128)S(1)} %copy-done.9, f32[768]{0:T(1024)S(1)} %add.164, f32[512,768]{1,0:T(8,128)} %get-tuple-element.59, bf16[2304,512]{1,0:T(8,128)(2,1)} %get-tuple-element.67, ...), kind=kOutput, calls=%fused_computation.83 | convolution fusion | flops 1818623232 | bytes 12980736 | tf_op jit(solution)/shard_map/dot_general | solution.py:1447
  320.2 5.2 %convolution_convert_fusion.1 = bf16[768,2304]{1,0:T(8,128)(2,1)} fusion(bf16[2304,512]{1,0:T(8,128)(2,1)S(1)} %copy-done.6, f32[512,768]{1,0:T(8,128)} %copy-done.10), kind=kOutput, calls=%fused_computation.1 | convolution fusion | flops 1814102016 | bytes 7471104 | tf_op jit(solution)/shard_map/dot_general | solution.py:1443
  325.5 102.3 %shard_map.419 = (f32[512,768]{1,0:T(8,128)}, f32[8,128]{1,0:T(8,128)}, f32[8,24,768]{2,1,0:T(8,128)}, f32[24,2304]{1,0:T(8,128)}, f32[16,128]{1,0:T(8,128)}) custom-call(s32[2]{0:T(128)} %pad_add_fusion.1.refs_0_, bf16[16,584,768]{2,1,0:T(8,128)(2,1)} %get-tuple-element.68.refs_1_, bf16[512,768]{1,0:T(8,128)(2,1)} %get-tuple-element.156.refs_2_, ...), custom_call_target="tpu_custom_call" | custom-call | tf_op jit(solution)/shard_map/pallas_call | solution.py:1132
  427.8 2.8 add.172
  431.6 8.2 %shard_map.420 = f32[8,128]{1,0:T(8,128)S(1)} custom-call(f32[8,128]{1,0:T(8,128)S(1)} %add.173.refs_0_, f32[24,3072]{1,0:T(8,128)S(1)} %bitcast_convert_fusion.refs_1_), custom_call_target="tpu_custom_call" | custom-call | tf_op jit(solution)/shard_map/pallas_call | solution.py:1171
  443.9 1.4 multiply_subtract_fusion.6
  448.8 1.5 multiply_subtract_fusion
  450.3 1.1 multiply_subtract_fusion.2
  (153 shorter events, 21.0 us)
Async XLA Ops:
  7.2 11.3 %copy-start.7 = (f32[128,24,48]{0,2,1:T(8,128)S(1)}, f32[128,24,48]{0,2,1:T(8,128)}, u32[]{:S(2)}) copy-start(f32[128,24,48]{0,2,1:T(8,128)} %param.31) | copy-start | bytes 1769476
  7.2 190.7 %all-gather.5.cloned.1.call-start = ((), (), s32[]{:S(2)}) async-start(), calls=%async_computation.2 | async-start | bytes 4866048 | tf_op jit(solution)/shard_map/all_gather | solution.py:1331
  9.0 188.9 %all-gather.7.cloned.1.call-start = ((), (), s32[]{:S(2)}) async-start(), calls=%async_computation.3 | async-start | bytes 4866048 | tf_op jit(solution)/shard_map/all_gather | solution.py:1331
  10.7 420.0 %reduce-scatter.2.cloned.1.call-start = ((), (), s32[]{:S(2)}) async-start(), calls=%async_computation.1 | async-start | bytes 4866048 | tf_op jit(solution)/shard_map/reduce_scatter | solution.py:1436
  21.0 116.1 %copy-start.5 = (bf16[512,768]{1,0:T(8,128)(2,1)S(1)}, bf16[512,768]{1,0:T(8,128)(2,1)}, u32[]{:S(2)}) copy-start(bf16[512,768]{1,0:T(8,128)(2,1)} %refs_1_.1) | copy-start | bytes 2359300
  137.2 9.7 %copy-start.1 = (s32[1,2048]{1,0:T(1,128)}, s32[1,2048]{1,0:T(1,128)S(1)}, u32[]{:S(2)}) copy-start(s32[1,2048]{1,0:T(1,128)S(1)} %pad_add_fusion.refs_0_) | copy-start | bytes 24580
  137.2 5.9 %copy-start.40 = (bf16[4,2,2,2,24,2304]{5,4,3,2,1,0:T(8,128)(2,1)S(1)}, bf16[4,2,2,2,24,2304]{5,4,3,2,1,0:T(8,128)(2,1)}, u32[]{:S(2)}) copy-start(bf16[4,2,2,2,24,2304]{5,4,3,2,1,0:T(8,128)(2,1)} %get-tuple-element.53) | copy-start | bytes 10616836
  143.1 3.8 copy-start.10
  228.8 3.6 copy-start.43
  237.1 73.5 %copy-start.9 = (f32[512,768]{1,0:T(8,128)S(1)}, f32[512,768]{1,0:T(8,128)}, u32[]{:S(2)}) copy-start(f32[512,768]{1,0:T(8,128)} %get-tuple-element.54) | copy-start | bytes 4718596
  310.6 7.9 %copy-start.6 = (bf16[2304,512]{1,0:T(8,128)(2,1)S(1)}, bf16[2304,512]{1,0:T(8,128)(2,1)}, u32[]{:S(2)}) copy-start(bf16[2304,512]{1,0:T(8,128)(2,1)} %get-tuple-element.67) | copy-start | bytes 7077892
  325.4 102.3 %copy-start.11 = (f32[512,768]{1,0:T(8,128)S(1)}, f32[512,768]{1,0:T(8,128)}, u32[]{:S(2)}) copy-start(f32[512,768]{1,0:T(8,128)} %get-tuple-element.166) | copy-start | bytes 4718596
  427.8 2.8 copy-start.35
  427.8 2.8 copy-start.36
  427.8 13.3 %copy-start.16 = (f32[8,24,768]{2,1,0:T(8,128)S(1)}, f32[8,24,768]{2,1,0:T(8,128)}, u32[]{:S(2)}) copy-start(f32[8,24,768]{2,1,0:T(8,128)} %get-tuple-element.80) | copy-start | bytes 1769476
  443.3 2.6 copy-start.22
  443.3 3.3 copy-start.14
  443.3 3.3 copy-start.25
  443.3 3.3 copy-start.26
  443.4 3.3 copy-start.27
  443.9 3.8 copy-start.12
  443.9 3.8 copy-start.19
  443.9 3.8 copy-start.20
  443.9 3.8 copy-start.21
  (23 other events, 37.4 us)
Sparse Core Ops, SparseCore 0:
  11.5 81.3 all-gather.4
  96.4 65.3 all-gather.6
  228.9 115.3 reduce-scatter.1

commit v5 on v3

--- a/solution.py
+++ b/solution.py
@@ -400,71 +400,78 @@
     heavy = (2, 1, 0, 3, 4)
 
     def __init__(self, own, whole, cut, order, send, recv):
-        self.own, self.whole, self.cut, self.order, self.send, self.recv = own, whole, cut, order, send, recv
-
-    def block(self, done, **given):
+        self.own, self.whole, self.cut, self.order, self.send, self.recv = own, whole, cut, order + "c", send, recv
+
+    def block(self, k, **given):
         z, x, y, c = spot()
         here = {"z": z, "x": x, "y": y, "c": c}
-        lead = tuple(given[a] if a in given else (EVERY if a in done else here[a]) for a in "zxyc")
+        lead = tuple(given[a] if a in given else (EVERY if a in self.order[:k] else here[a]) for a in "zxyc")
         return self.whole.at[lead + self.cut]
 
     def mine(self):
         return self.own.at[self.cut] if self.cut else self.own
 
-    def columns(self):
+    def copies(self, k):
         z, x, y, c = spot()
-        return [self.remote(self.mine(), self.block(""), n - 1, device(z ^ n, x, y, c)) for n in range(1, 4)]
-
-    def swap(self, k):
+        axis = self.order[k]
+        ref = self.block(k)
+        src = self.mine() if k == 0 else ref
+        if axis == "z":
+            return [self.remote(src, ref, n - 1, device(z ^ n, x, y, c)) for n in range(1, 4)]
+        to = {"x": device(z, 1 - x, y, c), "y": device(z, x, 1 - y, c), "c": device(z, x, y, 1 - c)}[axis]
+        return [self.remote(src, ref, 3 + "xyc".index(axis), to)]
+
+    def arrive(self, k):
         z, x, y, c = spot()
-        axis = (self.order + "c")[k]
-        ref = self.block("z" + self.order[:k])
-        to = {"x": device(z, 1 - x, y, c), "y": device(z, x, 1 - y, c), "c": device(z, x, y, 1 - c)}[axis]
-        return self.remote(ref, ref, 3 + k, to)
-
-    def swapped(self, k):
-        z, x, y, c = spot()
-        axis = (self.order + "c")[k]
-        return self.landed(self.block("z" + self.order[:k], **{axis: {"x": 1 - x, "y": 1 - y, "c": 1 - c}[axis]}), 3 + k)
+        axis = self.order[k]
+        if axis == "z":
+            for n in range(1, 4):
+                self.landed(self.block(k, z=z ^ n), n - 1).wait_recv()
+        else:
+            self.landed(self.block(k, **{axis: {"x": 1 - x, "y": 1 - y, "c": 1 - c}[axis]}), 3 + "xyc".index(axis)).wait_recv()
 
     def stage(self, n):
-        z, x, y, c = spot()
         if n < 2:
-            local = pltpu.make_async_copy(self.mine(), self.block(""), self.recv.at[6])
+            local = pltpu.make_async_copy(self.mine(), self.block(0), self.recv.at[6])
             local.start() if n == 0 else local.wait()
-        if n == 0:
-            for copy in self.columns():
+        if n > 0:
+            self.arrive(n - 1)
+        if n < 4:
+            for copy in self.copies(n):
                 copy.start()
-        elif n == 1:
-            for m in range(1, 4):
-                self.landed(self.block("", z=z ^ m), m - 1).wait_recv()
-            self.swap(0).start()
-        else:
-            self.swapped(n - 2).wait_recv()
-            if n < 4:
-                self.swap(n - 1).start()
 
     def finish(self):
-        for copy in self.columns() + [self.swap(k) for k in range(3)]:
-            copy.wait_send()
+        for k in range(4):
+            for copy in self.copies(k):
+                copy.wait_send()
 
 
 def add_rows(dst, src):
     dst[...] = (dst[...].astype(jnp.float32) + src[...].astype(jnp.float32)).astype(dst.dtype)
 
 
+def rest_of(order, k):
+    return [(a, {"z": 4, "x": 2, "y": 2}[a]) for a in "zxy" if a not in order[: k + 1]]
+
+
+def recv_shapes(order):
+    return [((3,) if order[k] == "z" else ()) + tuple(n for a, n in rest_of(order, k)) for k in range(3)]
+
+
 class Collect(Unit):
     heavy = (0, 1, 2, 3, 4)
 
-    def __init__(self, parts, out, cut, order, own, rc, r1, r2, rz, send, recv):
+    def __init__(self, parts, out, cut, order, own, rc, r0, r1, r2, send, recv):
         self.parts, self.out, self.cut, self.order, self.send, self.recv = parts, out, cut, order, send, recv
-        self.own, self.rc, self.r1, self.r2, self.rz = own, rc, r1, r2, rz
-
-    def block(self, *lead):
+        self.own, self.rc, self.r = own, rc, (r0, r1, r2)
+
+    def block(self, k, **given):
+        z, x, y, c = spot()
+        here = {"z": z, "x": x, "y": y}
+        lead = tuple(given[a] if a in given else (here[a] if a in self.order[:k] else EVERY) for a in "zxy")
         if self.own is None:
-            z, x, y, c = spot()
-            return self.parts.at[tuple(lead) + (c,) + self.cut]
-        return self.own.at[tuple(lead)]
+            return self.parts.at[lead + (c,) + self.cut]
+        return self.own.at[lead]
 
     def core(self):
         z, x, y, c = spot()
@@ -472,31 +479,55 @@
 
     def load(self):
         z, x, y, c = spot()
-        return pltpu.make_async_copy(self.parts.at[(EVERY, EVERY, EVERY, c) + self.cut], self.own, self.recv.at[6])
-
-    def first(self):
+        return pltpu.make_async_copy(self.parts.at[(EVERY, EVERY, EVERY, c) + self.cut], self.own, self.recv.at[7])
+
+    def copies(self, k):
         z, x, y, c = spot()
-        if self.order[0] == "x":
-            return self.remote(self.block(EVERY, 1 - x, EVERY), self.r1, 1, device(z, 1 - x, y, c))
-        return self.remote(self.block(EVERY, EVERY, 1 - y), self.r1, 1, device(z, x, 1 - y, c))
-
-    def second(self):
+        axis = self.order[k]
+        if axis == "z":
+            return [self.remote(self.block(k, z=z ^ n), self.r[k].at[n - 1], 3 + n, device(z ^ n, x, y, c)) for n in range(1, 4)]
+        to = {"x": device(z, 1 - x, y, c), "y": device(z, x, 1 - y, c)}[axis]
+        return [self.remote(self.block(k, **{axis: {"x": 1 - x, "y": 1 - y}[axis]}), self.r[k], 1 + k, to)]
+
+    def arrive(self, k):
         z, x, y, c = spot()
-        if self.order[0] == "x":
-            return self.remote(self.block(EVERY, x, 1 - y), self.r2, 2, device(z, x, 1 - y, c))
-        return self.remote(self.block(EVERY, 1 - x, y), self.r2, 2, device(z, 1 - x, y, c))
-
-    def columns(self):
-        z, x, y, c = spot()
-        return [self.remote(self.block(z ^ n, x, y), self.rz.at[n - 1], 2 + n, device(z ^ n, x, y, c)) for n in range(1, 4)]
+        axis = self.order[k]
+        own = {axis: {"z": z, "x": x, "y": y}[axis]}
+        if axis == "z":
+            sources = [self.r[k].at[n] for n in range(3)]
+            for n in range(3):
+                self.landed(sources[n], 4 + n).wait_recv()
+        else:
+            sources = [self.r[k]]
+            self.landed(self.r[k], 1 + k).wait_recv()
+        if k == 2:
+            total = self.block(k, **own)[...].astype(jnp.float32)
+            for source in sources:
+                total = total + source[...].astype(jnp.float32)
+            out = self.out.at[self.cut] if self.cut else self.out
+            out[...] = total.reshape(out.shape)
+            return
+        rest = rest_of(self.order, k)
+
+        def add(at):
+            given = dict(zip([a for a, n in rest], at))
+            for source in sources:
+                add_rows(self.block(k, **own, **given), source.at[tuple(at)])
+
+        def one(i, unused):
+            for n in range(rest[1][1] if len(rest) == 2 else 1):
+                add((i, n) if len(rest) == 2 else (i,))
+            return unused
+
+        lax.fori_loop(0, rest[0][1], one, 0)
 
     def stage(self, n):
-        z, x, y, c = spot()
         if n == 0:
             self.core().start()
             if self.own is not None:
                 self.load().start()
-        elif n == 1:
+            return
+        if n == 1:
             self.landed(self.rc, 0).wait_recv()
             if self.own is not None:
                 self.load().wait()
@@ -504,42 +535,21 @@
             def one(i, unused):
                 for k in range(2):
                     for m in range(2):
-                        add_rows(self.block(i, k, m), self.rc.at[i, k, m])
+                        add_rows(self.block(0, z=i, x=k, y=m), self.rc.at[i, k, m])
                 return unused
 
             lax.fori_loop(0, 4, one, 0)
-            self.first().start()
-        elif n == 2:
-            self.landed(self.r1, 1).wait_recv()
-
-            def one(i, unused):
-                for k in range(2):
-                    add_rows(self.block(i, x, k) if self.order[0] == "x" else self.block(i, k, y), self.r1.at[i, k])
-                return unused
-
-            lax.fori_loop(0, 4, one, 0)
-            self.second().start()
-        elif n == 3:
-            self.landed(self.r2, 2).wait_recv()
-
-            def one(i, unused):
-                add_rows(self.block(i, x, y), self.r2.at[i])
-                return unused
-
-            lax.fori_loop(0, 4, one, 0)
-            for copy in self.columns():
+        else:
+            self.arrive(n - 2)
+        if n < 4:
+            for copy in self.copies(n - 1):
                 copy.start()
-        else:
-            total = self.block(z, x, y)[...].astype(jnp.float32)
-            for m in range(1, 4):
-                self.landed(self.rz.at[m - 1], 2 + m).wait_recv()
-                total = total + self.rz[m - 1].astype(jnp.float32)
-            out = self.out.at[self.cut] if self.cut else self.out
-            out[...] = total
 
     def finish(self):
-        for copy in [self.core(), self.first(), self.second()] + self.columns():
-            copy.wait_send()
+        self.core().wait_send()
+        for k in range(3):
+            for copy in self.copies(k):
+                copy.wait_send()
 
 
 def unit_shape(shape, cut):
@@ -552,7 +562,7 @@
     for i, cut, order in plan:
         m = unit_shape(shapes[i], cut)
         leads = [] if i in inside else [(4, 2, 2)]
-        leads += [(4, 2, 2), (4, 2), (4,), (3,)]
+        leads += [(4, 2, 2)] + recv_shapes(order)
         scratch += [pltpu.VMEM(lead + m, dtype) for lead in leads]
     return scratch
 
@@ -568,11 +578,11 @@
 STAGES = 5
 
 
-def waves(units, width=2):
-    rows = [units[i : i + width] for i in range(0, len(units), width)]
+def waves(units, width=2, first=2, lag=1):
+    rows = [units[:first]] + [units[i : i + width] for i in range(first, len(units), width)] if units else []
     steps = []
-    for t in range(len(rows) + STAGES - 1 if rows else 0):
-        steps.append([(unit, n) for n in units[0].heavy for unit in (rows[t - n] if 0 <= t - n < len(rows) else [])])
+    for t in range(len(rows) + lag * (STAGES - 1) if rows else 0):
+        steps.append([(unit, n) for n in units[0].heavy for unit in (rows[t - lag * n] if 0 <= t - lag * n < len(rows) else [])])
     return steps
 
 
@@ -623,6 +633,211 @@
         copy.wait_send()
 
 
+FCH = 768
+PACK = 4
+
+
+def norm_of(h, gain, shift):
+    center = h - jnp.mean(h, axis=1, keepdims=True)
+    r = lax.rsqrt(jnp.mean(center * center, axis=1, keepdims=True) + norm_eps)
+    z = center * r
+    return z, r, z * gain + shift
+
+
+def norm_back(g, z, r, gain):
+    gz = g * gain
+    return r * (gz - jnp.mean(gz, axis=1, keepdims=True) - z * jnp.mean(gz * z, axis=1, keepdims=True))
+
+
+def gelu_both(v):
+    phi = 0.5 + 0.5 * lax.erf(v * (0.5**0.5))
+    return v * phi, phi + v * (jnp.exp(-0.5 * v * v) * 0.3989422804014327)
+
+
+def ffn_kernel(
+    ctx_ref, proj_ref, up_ref, down_ref, h1_ref, og_ref, vec_ref, fb_ref,
+    out_ref, gtwo_ref, gctx_ref, gvec_ref, gfb_ref, gproj_ref, gup_ref, gdown_ref,
+    proj_s, up_s, down_s, proj_p, up_p, down_p, mid_s, gup_s, gffn_s, fin_s, gattn_s, slope_s, z_s, acc_s, g3_s, sem,
+):
+    f32, low = jnp.float32, jnp.bfloat16
+    chunks = fb_ref.shape[1] // FCH
+    nt = (((1,), (1,)), ((), ()))
+    tn = (((0,), (0,)), ((), ()))
+
+    def ends(k, proj, up, down):
+        if k == 0:
+            return proj, proj_p
+        j = (k - 1) // 2
+        if k % 2:
+            return up.at[:, j], up_p.at[j]
+        return down.at[8 * j : 8 * j + 8], down_p.at[j]
+
+    def fetch(k):
+        src, dst = ends(k, proj_ref, up_ref, down_ref)
+        return pltpu.make_async_copy(src, dst, sem.at[k])
+
+    def keep(k):
+        dst, src = ends(k, gproj_ref, gup_ref, gdown_ref)
+        return pltpu.make_async_copy(src, dst, sem.at[k])
+
+    def block(k, n):
+        j = (k - 1) // 2
+        if k == 0:
+            return proj_p.at[n]
+        return up_p.at[j, n] if k % 2 else down_p.at[j, n // 4, n % 4]
+
+    def flatten(k, flat):
+        fetch(k).wait()
+
+        def two(m, unused):
+            pair = [block(k, 2 * m + i)[...].astype(f32) for i in range(2)]
+            flat[pl.ds(pl.multiple_of(48 * m, 16), 48), :] = jnp.concatenate(pair, axis=0).astype(low)
+            return unused
+
+        lax.fori_loop(0, 16, two, 0, unroll=4)
+
+    def give(k, product):
+        for n in range(32):
+            block(k, n)[...] = product[24 * n : 24 * n + 24].astype(low)
+        keep(k).start()
+
+    for k in range(1 + 2 * chunks):
+        fetch(k).start()
+    row = lambda n: vec_ref[n : n + 1, :]
+    flatten(0, proj_s)
+    attn = lax.dot_general(ctx_ref[...], proj_s[...], tn, preferred_element_type=f32)
+    z1, r1, n1 = norm_of(h1_ref[...] + (attn + row(3)), row(4), row(5))
+    z_s[...] = z1
+    acc_s[...] = n1 + row(6)
+    fin_s[...] = n1.astype(low)
+    for j in range(chunks):
+        at = slice(j * FCH, j * FCH + FCH)
+        flatten(1 + 2 * j, up_s.at[j])
+        pre = jnp.dot(fin_s[...], up_s[j], preferred_element_type=f32) + fb_ref[:, at]
+        act, slope = gelu_both(pre)
+        slope_s[:, at] = slope
+        mid_s[:, at] = act.astype(low)
+        flatten(2 + 2 * j, down_s.at[j])
+        acc_s[...] += jnp.dot(mid_s[:, at], down_s[j], preferred_element_type=f32)
+    z3, r3, out = norm_of(acc_s[...], row(7), row(8))
+    out_ref[...] = out.astype(low)
+    og = og_ref[...].astype(f32)
+    gvec_ref[7:8, :] = jnp.sum(og * z3, axis=0, keepdims=True)
+    gvec_ref[8:9, :] = jnp.sum(og, axis=0, keepdims=True)
+    g3 = norm_back(og, z3, r3, row(7))
+    g3_s[...] = g3
+    gffn_s[...] = g3.astype(low)
+    gvec_ref[6:7, :] = jnp.sum(gffn_s[...].astype(f32), axis=0, keepdims=True)
+    for j in range(chunks):
+        at = slice(j * FCH, j * FCH + FCH)
+        give(2 + 2 * j, lax.dot_general(mid_s[:, at], gffn_s[...], tn, preferred_element_type=f32))
+        gu = (lax.dot_general(gffn_s[...], down_s[j], nt, preferred_element_type=f32) * slope_s[:, at]).astype(low)
+        gup_s[:, at] = gu
+        gfb_ref[:, at] = jnp.sum(gu.astype(f32), axis=0, keepdims=True)
+        g3_s[...] += lax.dot_general(gu, up_s[j], nt, preferred_element_type=f32)
+    gn = g3_s[...]
+    z1 = z_s[...]
+    gvec_ref[4:5, :] = jnp.sum(gn * z1, axis=0, keepdims=True)
+    gvec_ref[5:6, :] = jnp.sum(gn, axis=0, keepdims=True)
+    g2 = norm_back(gn, z1, r1, row(4))
+    gtwo_ref[...] = g2
+    gattn_s[...] = g2.astype(low)
+    gvec_ref[3:4, :] = jnp.sum(gattn_s[...].astype(f32), axis=0, keepdims=True)
+    for j in range(chunks):
+        at = slice(j * FCH, j * FCH + FCH)
+        give(1 + 2 * j, lax.dot_general(fin_s[...], gup_s[:, at], tn, preferred_element_type=f32))
+    gctx_ref[...] = lax.dot_general(proj_s[...], gattn_s[...], nt, preferred_element_type=f32).astype(low)
+    give(0, jnp.dot(ctx_ref[...], gattn_s[...], preferred_element_type=f32))
+    for k in range(1 + 2 * chunks):
+        keep(k).wait()
+
+
+def ffn_step(context, proj, up, down, hidden_one, output_grad, vectors, ffn_bias):
+    rows, width = hidden_one.shape
+    hidden = ffn_bias.shape[1]
+    low, f32 = jnp.bfloat16, jnp.float32
+    vmem = pl.BlockSpec(memory_space=pltpu.VMEM)
+    anywhere = pl.BlockSpec(memory_space=pl.ANY)
+    shape = jax.ShapeDtypeStruct
+    chunks = hidden // FCH
+    return pl.pallas_call(
+        ffn_kernel,
+        in_specs=[vmem, anywhere, anywhere, anywhere, vmem, vmem, vmem, vmem],
+        out_specs=[vmem] * 5 + [anywhere] * 3,
+        out_shape=[
+            shape((rows, width), low), shape((rows, width), f32), shape((width, rows), low),
+            shape((9, width), f32), shape((1, hidden), f32), shape(proj.shape, low), shape(up.shape, low), shape(down.shape, low),
+        ],
+        scratch_shapes=[
+            pltpu.VMEM((width, width), low), pltpu.VMEM((chunks, width, FCH), low), pltpu.VMEM((chunks, FCH, width), low),
+            pltpu.VMEM((32, 24, width), low), pltpu.VMEM((chunks, 32, 24, FCH), low), pltpu.VMEM((chunks, 8, 4, 24, width), low),
+            pltpu.VMEM((rows, hidden), low), pltpu.VMEM((rows, hidden), low),
+            pltpu.VMEM((rows, width), low), pltpu.VMEM((rows, width), low), pltpu.VMEM((rows, width), low),
+            pltpu.VMEM((rows, hidden), f32), pltpu.VMEM((rows, width), f32), pltpu.VMEM((rows, width), f32), pltpu.VMEM((rows, width), f32),
+            pltpu.SemaphoreType.DMA((1 + 2 * chunks,)),
+        ],
+        compiler_params=pltpu.CompilerParams(vmem_limit_bytes=60 * 2**20),
+        cost_estimate=pl.CostEstimate(flops=6 * rows * width * (2 * hidden + width), bytes_accessed=30_000_000, transcendentals=2 * rows * hidden),
+    )(context, proj, up, down, hidden_one, output_grad, vectors, ffn_bias)
+
+
+def prep_kernel(qkv_i, proj_i, up_i, down_i, conv_i, bias, ffn, qkv_o, proj_o, up_o, down_o, conv_o, small_o, qkv, proj, up, down, conv, sem):
+    low = jnp.bfloat16
+    copies = [
+        pltpu.make_async_copy(src, dst, sem.at[n])
+        for n, (src, dst) in enumerate(((up_i, up), (down_i, down), (proj_i, proj), (qkv_i, qkv), (conv_i, conv)))
+    ]
+    for copy in copies:
+        copy.start()
+    copies[0].wait()
+    for j in range(4):
+        up_o[j] = up[:, 768 * j : 768 * j + 768].astype(low)
+    copies[1].wait()
+    for j in range(4):
+        down_o[j] = down[24 * j : 24 * j + 24].astype(low)
+    copies[2].wait()
+    proj_o[...] = proj[...].astype(low)
+    copies[3].wait()
+    qkv_o[...] = qkv[...].astype(low)
+    copies[4].wait()
+    rows = conv.shape[1]
+    lane = lax.broadcasted_iota(jnp.int32, (rows, 128), 1)
+    zero = jnp.zeros((rows, 128 - CGW), jnp.float32)
+
+    def tap(a, unused):
+        cols = [None] * 6
+        for r in range(16):
+            piece = jnp.concatenate([conv[8 * r + a], zero], axis=1)
+            lo = CGW * r
+            tile, off = lo // 128, lo % 128
+            piece = right(piece, off) if off else piece
+            cols[tile] = piece if cols[tile] is None else jnp.where(lane >= off, piece, cols[tile])
+            if off + CGW > 128:
+                cols[tile + 1] = piece
+        conv_o[a] = jnp.concatenate(cols, axis=1).astype(low)
+        return unused
+
+    lax.fori_loop(0, 8, tap, 0)
+    small_o[...] = jnp.zeros_like(small_o)
+    n = bias.shape[0]
+    small_o[0:n, 0 : bias.shape[1]] = bias[...].astype(low)
+    small_o[n : n + 1, 0 : ffn.shape[1]] = ffn[...].astype(low)
+
+
+def prep_step(qkv, proj, up, down, conv, bias, ffn):
+    vmem = pl.BlockSpec(memory_space=pltpu.VMEM)
+    anywhere = pl.BlockSpec(memory_space=pl.ANY)
+    shapes = [qkv.shape, proj.shape, (PACK, 24, 768), (PACK, 24, 768), (8, conv.shape[1], 768), (16, 128)]
+    return pl.pallas_call(
+        prep_kernel,
+        in_specs=[anywhere] * 5 + [vmem] * 2,
+        out_specs=[vmem] * 6,
+        out_shape=[jax.ShapeDtypeStruct(s, jnp.bfloat16) for s in shapes],
+        scratch_shapes=[pltpu.VMEM(w.shape, jnp.float32) for w in (qkv, proj, up, down, conv)] + [pltpu.SemaphoreType.DMA((5,))],
+        compiler_params=pltpu.CompilerParams(vmem_limit_bytes=60 * 2**20),
+    )(qkv, proj, up, down, conv, bias, ffn)
+
+
 def take_rows(win_ref, g, cut):
     return gapped(take_group(win_ref, g), cut)
 
@@ -665,17 +880,34 @@
         pl.when(ok)(copy.wait_send)
 
 
+def unpack_small(small_s, vec_ref, fb_ref):
+    lane = lax.broadcasted_iota(jnp.int32, (16, 128), 1)
+    vec, fb = [None] * 6, [None] * 24
+    for n in range(32):
+        piece = small_s[n // 8, (n // 4) % 2, (n // 2) % 2, n % 2].astype(jnp.float32)
+        for out, width in ((vec, 24), (fb, 96)):
+            tile, off = width * n // 128, width * n % 128
+            turned = right(piece, off) if off else piece
+            out[tile] = turned if out[tile] is None else jnp.where(lane >= off, turned, out[tile])
+            if off + width > 128:
+                out[tile + 1] = turned
+    for i, v in enumerate(vec):
+        vec_ref[:, 128 * i : 128 * i + 128] = v
+    for i, v in enumerate(fb):
+        fb_ref[:, 128 * i : 128 * i + 128] = v[9:10]
+
+
 def open_kernel(plan, n_in, early, *refs):
     cut_ref, frames_ref = refs[:2]
     owns = refs[2 : 2 + n_in]
-    out_ref, cols_ref = refs[2 + n_in : 4 + n_in]
-    wholes = refs[4 + n_in : 4 + 2 * n_in]
-    win_ref, cols_s, low_s, w_s, wp_s, send, recv, hsend, hrecv, wsem, csem = refs[4 + 2 * n_in :]
+    hidden_ref, slope_ref, low_ref, vec_ref, fb_ref, cols_ref = refs[2 + n_in : 8 + n_in]
+    wholes = refs[8 + n_in : 8 + 2 * n_in]
+    out_ref, win_ref, cols_s, low_s, w_s, wp_s, small_s, send, recv, hsend, hrecv, wsem, csem = refs[8 + 2 * n_in :]
     cut = cut_ref[0]
     greet(halo=True)
     halo_start(frames_ref, win_ref, hsend, hrecv)
     units = [Spread(owns[i], wholes[i], where, order, send.at[n], recv.at[n]) for n, (i, where, order) in enumerate(plan)]
-    steps = waves(units)
+    steps = waves(units, first=3)
     go(steps[0])
     win_ref[HALF : HALF + OWN, :] = frames_ref[...]
     out_ref[...] = jnp.zeros_like(out_ref)
@@ -717,9 +949,23 @@
         keep(chunk).start()
         go(steps[t])
         t += 1
+    def finish():
+        copy = pltpu.make_async_copy(wholes[-1], small_s, wsem.at[0])
+        copy.start()
+        copy.wait()
+        unpack_small(small_s, vec_ref, fb_ref)
+        act, slope = gelu_both(out_ref[...] + vec_ref[0:1, :])
+        hidden = frames_ref[...].astype(jnp.float32) + act
+        hidden_ref[...] = hidden
+        low_ref[...] = hidden.astype(jnp.bfloat16)
+        slope_ref[...] = slope
+
     done = 0
-    while t < len(steps) or done < 2:
-        if done < 2 and t - STAGES >= early[done]:
+    while t < len(steps) or done < 3:
+        if done == 2:
+            finish()
+            done += 1
+        elif done < 2 and t - STAGES >= early[done]:
             for z in range(4):
                 load(done, z).start()
             for z in range(4):
@@ -745,15 +991,24 @@
     return pl.pallas_call(
         functools.partial(open_kernel, plan, n, early),
         in_specs=[pl.BlockSpec(memory_space=pltpu.SMEM), vmem] + [anywhere] * n,
-        out_specs=[vmem, anywhere] + [anywhere] * n,
-        out_shape=[jax.ShapeDtypeStruct((OWN, 768), jnp.float32), jax.ShapeDtypeStruct((16, ZROWS, 768), jnp.bfloat16)]
+        out_specs=[vmem] * 5 + [anywhere] + [anywhere] * n,
+        out_shape=[
+            jax.ShapeDtypeStruct((OWN, 768), jnp.float32),
+            jax.ShapeDtypeStruct((OWN, 768), jnp.float32),
+            jax.ShapeDtypeStruct((OWN, 768), jnp.bfloat16),
+            jax.ShapeDtypeStruct((16, 768), jnp.float32),
+            jax.ShapeDtypeStruct((1, 3072), jnp.float32),
+            jax.ShapeDtypeStruct((16, ZROWS, 768), jnp.bfloat16),
+        ]
         + [jax.ShapeDtypeStruct((4, 2, 2, 2) + s.shape, s.dtype) for s in shards],
         scratch_shapes=[
+            pltpu.VMEM((OWN, 768), jnp.float32),
             pltpu.VMEM((WIN, 768), jnp.bfloat16),
             pltpu.VMEM((16, ZROWS, 768), jnp.bfloat16),
             pltpu.VMEM((16, ZROWS, 256), jnp.float32),
             pltpu.VMEM((4, 2, 2, 2, 4, 24, 768), jnp.bfloat16),
             pltpu.VMEM((256, 768), jnp.bfloat16),
+            pltpu.VMEM((4, 2, 2, 2, 16, 128), jnp.bfloat16),
             pltpu.SemaphoreType.DMA((len(plan), 9)),
             pltpu.SemaphoreType.DMA((len(plan), 10)),
             pltpu.SemaphoreType.DMA((2,)),
@@ -1034,6 +1289,9 @@
     )(seg, qkv, lse, o, gc, *parts)
 
 
+SIDE_SLOTS = 16
+
+
 def close_kernel(side_plan, main_plan, n_in, *refs):
     cut_ref, cols_ref, grad_ref, conv_ref = refs[:4]
     parts = refs[4 : 4 + n_in]
@@ -1068,7 +1326,7 @@
     pick(0).start()
     row = lax.broadcasted_iota(jnp.int32, (ZROWS, 256), 0) + HALF
     owned = (row >= begin) & (row < end)
-    by_slot = spaced(side_steps[1:], 8)
+    by_slot = spaced(side_steps[1:], SIDE_SLOTS)
 
     def product(k, m, taps, half):
         own = jnp.concatenate([taps[HALF : HALF + ZROWS, h * 256 + half * 128 : h * 256 + half * 128 + 128] for h in range(2)], axis=1)
@@ -1090,10 +1348,11 @@
 
     lax.fori_loop(0, 8, weights_low, 0)
     soon = max(len(main) // 4, 1)
-    by_slot = spaced(main_steps[:soon], 8)
+    early = spaced(main_steps[:soon], 8)
 
     def weights_high(k, unused):
-        go_at(k, by_slot)
+        go_at(k + 8, by_slot)
+        go_at(k, early)
         pl.when(k < 7)(lambda: pick(k + 1).start())
         pick(k).wait()
         for m in range(2):
@@ -1189,29 +1448,26 @@
 
 
 def open_plan():
-    even = ("xy", "yx")
-    return sliced(0, 0, 8, 8, even) + sliced(1, 1, 2304, 2, even) + [(3, (), "xy"), (2, (), "yx")]
-
-
-def attend_plan():
-    return sliced(0, 1, 3072, 4, ("yx",)) + sliced(1, 0, 96, 3, ("yx",))
+    even = ("zxy", "zyx")
+    plan = sliced(0, 0, 8, 8, even)
+    return plan[:1] + [(3, (), "zxy")] + plan[1:] + sliced(1, 1, 2304, 2, even) + [(2, (), "zyx")]
 
 
 def attend_back_plan():
     plan = []
-    for a in range(3):
-        plan += [(1, (S(32 * a, 32 * a + 32), S(384 * i, 384 * i + 384)), ("xy", "yx")[i]) for i in range(2)]
-    return plan + [(0, (), "xy")]
+    for a in range(4):
+        plan += [(1, (S(a, a + 1), S(None), S(384 * i, 384 * i + 384)), ("xyz", "yxz")[i]) for i in range(2)]
+    return plan + [(0, (), "xyz")]
 
 
 def side_plan():
-    return sliced(0, 1, 2304, 2, ("xy", "yx")) + [(1, (), "xy")]
+    return sliced(0, 1, 2304, 6, ("xyz", "yxz")) + [(1, (), "xyz")]
 
 
 def main_plan():
     plan = []
     for a in range(8):
-        plan += [(0, (S(a, a + 1), S(None), S(384 * i, 384 * i + 384)), ("xy", "yx")[i]) for i in range(2)]
+        plan += [(0, (S(a, a + 1), S(None), S(384 * i, 384 * i + 384)), ("xyz", "yxz")[i]) for i in range(2)]
     return plan
 
 
@@ -1233,6 +1489,12 @@
 
 def by_owner(part):
     return part.reshape((4, 2, 2, 2) + part.shape[1:])
+
+
+def as_small(rows, ffn):
+    n, count, width = rows.shape
+    rows = jnp.pad(rows, ((0, 0), (0, 16 - count), (0, 128 - width)))
+    return rows + jnp.pad(ffn[:, None], ((0, 0), (count, 15 - count), (0, 128 - ffn.shape[1])))
 
 
 def trade(pieces):
@@ -1265,41 +1527,43 @@
     kernel_len, conv_rows, group_width = conv_weight.shape
     vec_rows, vec_cols = bias_gains.shape
     ffn_cols = ffn_bias.shape[0]
-    conv_low = conv_weight.astype(low_type).reshape(16, 8, conv_rows, group_width).transpose(1, 2, 0, 3).reshape(8, conv_rows, 768)
-    small = jnp.concatenate([bias_gains.astype(low_type).reshape(-1), ffn_bias.astype(low_type)])
-    small = jnp.pad(small, (0, 2048 - small.shape[0])).reshape(16, 128)
-    own_parts = [
-        conv_low, qkv_weight.astype(low_type), proj_weight.astype(low_type), up_weight.astype(low_type), down_weight.astype(low_type), small
-    ]
+    if by_chips():
+        qkv_low, proj_low, up_low, down_low, conv_low, small = prep_step(
+            qkv_weight, proj_weight, up_weight, down_weight, conv_weight, bias_gains, ffn_bias[None]
+        )
+    else:
+        qkv_low, proj_low, up_low, down_low = [w.astype(low_type) for w in (qkv_weight, proj_weight, up_weight, down_weight)]
+        conv_low = conv_weight.astype(low_type).reshape(16, 8, conv_rows, group_width).transpose(1, 2, 0, 3).reshape(8, conv_rows, 768)
+        small = as_small(bias_gains.astype(low_type)[None], ffn_bias.astype(low_type)[None])[0]
     seg_group = segment_ids[0]
     half_kernel = kernel_len // 2
     boundary = jnp.sum((seg_group == 0).astype(jnp.int32))
     cut = jnp.clip(boundary - head_index * row_count + half_kernel, 0, row_count + kernel_len)
     cut = jnp.stack([cut, (head_index == head_groups - 1).astype(jnp.int32)]).astype(jnp.int32)
     if by_chips():
-        early = own_parts[:3] + own_parts[5:]
-        conv_pre, conv_columns, *parts = open_step(cut, frames, early, open_plan(), (1, 3))
-        all_conv, all_qkv, all_proj, all_small = [w.reshape((32,) + w.shape[4:]) for w in parts]
+        hidden_one, conv_slope, attn_in, vectors, full_ffn, conv_columns, *parts = open_step(
+            cut, frames, [conv_low, qkv_low, proj_low, small], open_plan(), (1, 3)
+        )
+        all_conv, all_qkv, all_proj = [w.reshape((32,) + w.shape[4:]) for w in parts[:3]]
         whole_conv = parts[0]
-        all_up, all_down = gather_weights(own_parts[3:5])
+        all_up, all_down = gather_weights([up_low, down_low])
     else:
-        all_conv, all_qkv, all_proj, all_up, all_down, all_small = gather_weights(own_parts)
+        all_conv, all_qkv, all_proj, all_up, all_down, all_small = gather_weights([conv_low, qkv_low, proj_low, up_low, down_low, small])
+        all_up = all_up.reshape(32, 24, 4, model_width).transpose(0, 2, 1, 3)
+        all_down = all_down.reshape(32, 4, 24, model_width)
+        all_proj = all_proj.reshape(32, 24, model_width)
     full_qkv = all_qkv.reshape(model_width, -1)
-    full_proj = all_proj.reshape(model_width, -1)
     full_conv = all_conv.reshape(16, 2, 24 // conv_rows, 8, conv_rows, 768).transpose(0, 1, 3, 2, 4, 5).reshape(16, 2, 8, 24, 768)
-    all_small = all_small.reshape(count, 2048).astype(f32)
-    vectors = all_small[:, : vec_rows * vec_cols].reshape(count, vec_rows, vec_cols).transpose(1, 0, 2).reshape(vec_rows, model_width)
-    full_ffn = all_small[:, vec_rows * vec_cols : vec_rows * vec_cols + ffn_cols].reshape(-1)
-
+    if not by_chips():
+        vectors = all_small[:, :vec_rows, :vec_cols].astype(f32).transpose(1, 0, 2).reshape(vec_rows, model_width)
+        full_ffn = all_small[:, vec_rows, :ffn_cols].astype(f32).reshape(1, -1)
     seg_rows = jnp.concatenate(by_partner(seg_group.reshape(head_groups, 1, row_count)), axis=1)
 
     if not by_chips():
         window = with_halo(frames, (("head", 0),), half_kernel)
-        conv_pre = conv_fwd(cut, window, full_conv)
-    conv_pre = conv_pre + vectors[0]
-    conv_act, conv_act_back = jax.vjp(gelu_exact, conv_pre)
-    hidden_one = frames.astype(f32) + conv_act
-    attn_in = hidden_one.astype(low_type)
+        conv_act, conv_slope = gelu_both(conv_fwd(cut, window, full_conv) + vectors[0])
+        hidden_one = frames.astype(f32) + conv_act
+        attn_in = hidden_one.astype(low_type)
     zero_part = jnp.zeros((HEADS, HEAD_DIM), f32)
     qkv_bias = jnp.stack(
         [vectors[1].reshape(HEADS, HEAD_DIM), zero_part, vectors[2].reshape(HEADS, HEAD_DIM)], axis=1
@@ -1313,32 +1577,9 @@
         blocks = trade(by_partner(packed.reshape(head_groups, -1, row_count)))
         fwd = attn_fwd(seg_rows, blocks)
         context = from_partner(trade(fwd[:4]))
-    full_up = all_up.reshape(model_width, -1)
-    full_down = all_down.reshape(-1, model_width)
-    attn_out = lax.dot_general(context, full_proj, (((0,), (0,)), ((), ())), preferred_element_type=f32) + vectors[3]
-    normed_one, norm_one_back = jax.vjp(layer_norm, hidden_one + attn_out, vectors[4], vectors[5])
-    ffn_in = normed_one.astype(low_type)
-    up_act, up_back = jax.vjp(gelu_exact, jnp.dot(ffn_in, full_up, preferred_element_type=f32) + full_ffn)
-    hidden_mid = up_act.astype(low_type)
-    hidden_three = normed_one + jnp.dot(hidden_mid, full_down, preferred_element_type=f32) + vectors[6]
-    layer_out_full, norm_two_back = jax.vjp(layer_norm, hidden_three, vectors[7], vectors[8])
-    grad_three, grad_gain_two, grad_shift_two = norm_two_back(output_grad.astype(f32))
-    grad_ffn = grad_three.astype(low_type)
-    grad_down = jnp.einsum("tf,td->fd", hidden_mid, grad_ffn, preferred_element_type=f32).astype(low_type)
-    grad_down_bias = jnp.sum(grad_ffn.astype(f32), axis=0)
-    (grad_up_pre,) = up_back(jnp.einsum("td,fd->tf", grad_ffn, full_down, preferred_element_type=f32))
-    grad_up_low = grad_up_pre.astype(low_type)
-    grad_up = jnp.einsum("td,tf->df", ffn_in, grad_up_low, preferred_element_type=f32).astype(low_type)
-    grad_ffn_bias = jnp.sum(grad_up_low.astype(f32), axis=0)
-    grad_normed = grad_three + jnp.einsum("tf,df->td", grad_up_low, full_up, preferred_element_type=f32)
-    grad_two, grad_gain_one, grad_shift_one = norm_one_back(grad_normed)
-    grad_attn = grad_two.astype(low_type)
-    grad_proj = jnp.dot(context, grad_attn, preferred_element_type=f32).astype(low_type)
-    grad_proj_bias = jnp.sum(grad_attn.astype(f32), axis=0)
-    grad_context = lax.dot_general(full_proj, grad_attn, (((1,), (1,)), ((), ())), preferred_element_type=f32).astype(low_type)
-    grad_proj, grad_up, grad_down = [
-        g.reshape((count,) + w.shape) for g, w in ((grad_proj, proj_weight), (grad_up, up_weight), (grad_down, down_weight))
-    ]
+    layer_out, grad_two, grad_context, grad_rows, grad_ffn_bias, grad_proj, grad_up, grad_down = ffn_step(
+        context, all_proj, all_up, all_down, hidden_one, output_grad, vectors, full_ffn
+    )
     if by_chips():
         sum_up = lax.psum_scatter(grad_up, ("seq", "head"), scatter_dimension=0, tiled=False).astype(f32)
         grad_packed, square_tile, sum_proj, sum_down = attend_back(
@@ -1352,44 +1593,40 @@
     grad_query_bias = grad_split[:, 0].reshape(model_width)
     grad_value_bias = grad_split[:, 2].reshape(model_width)
     grad_hidden_one = grad_two + lax.dot_general(grad_packed, full_qkv, (((0,), (1,)), ((), ())), preferred_element_type=f32)
-    (grad_conv_pre,) = conv_act_back(grad_hidden_one)
-    grad_conv_low = grad_conv_pre.astype(low_type)
+    grad_conv_low = (grad_hidden_one * conv_slope).astype(low_type)
     grad_conv_bias = jnp.sum(grad_conv_low.astype(f32), axis=0)
-    grad_vectors = jnp.stack(
-        [
-            grad_conv_bias, grad_query_bias, grad_value_bias, grad_proj_bias, grad_gain_one, grad_shift_one,
-            grad_down_bias, grad_gain_two, grad_shift_two,
-        ],
-        axis=0,
+    grad_vectors = jnp.concatenate([jnp.stack([grad_conv_bias, grad_query_bias, grad_value_bias], axis=0), grad_rows[3:]], axis=0)
+    grad_small = as_small(
+        grad_vectors.reshape(vec_rows, count, vec_cols).transpose(1, 0, 2).astype(low_type), grad_ffn_bias.reshape(count, ffn_cols).astype(low_type)
     )
-    grad_small = jnp.concatenate(
-        [grad_vectors.reshape(vec_rows, count, vec_cols).transpose(1, 0, 2).reshape(count, -1), grad_ffn_bias.reshape(count, ffn_cols)], axis=1
-    )
-    grad_small = jnp.pad(grad_small, ((0, 0), (0, 2048 - grad_small.shape[1]))).astype(low_type).reshape(count, 16, 128)
     grad_qkv = grad_qkv.reshape((count,) + qkv_weight.shape)
     if by_chips():
         grad_frames_conv, norm_tile, sum_conv, sum_qkv, sum_small = close_step(
             cut, conv_columns, grad_conv_low, whole_conv, [by_owner(grad_qkv), by_owner(grad_small)], side_plan(), main_plan()
         )
-        square_total = jnp.sum(norm_step(norm_tile + square_tile, [sum_up]))
+        norm_tile = norm_step(norm_tile + square_tile, [sum_up])
+        square_total = jnp.sum(norm_tile)
+        sum_down = sum_down.reshape(down_weight.shape)
+        sum_up = sum_up.transpose(1, 0, 2).reshape(up_weight.shape)
     else:
         grad_window = with_halo(grad_conv_low, (("head", 0),), half_kernel)
         grad_frames_conv, grad_conv = conv_bwd(cut, window, grad_window, full_conv)
         grad_conv = grad_conv.reshape(16, 2, 8, 24 // conv_rows, conv_rows, 768).transpose(0, 1, 3, 2, 4, 5).reshape(count, 8, conv_rows, 768)
+        grad_down, grad_proj = [g.reshape((count,) + w.shape) for g, w in ((grad_down, down_weight), (grad_proj, proj_weight))]
+        grad_up = grad_up.transpose(0, 2, 1, 3).reshape((count,) + up_weight.shape)
         (sum_conv, sum_qkv, sum_proj, sum_up, sum_down, sum_small), square_total = collect_grads(
             [grad_conv, grad_qkv, grad_proj, grad_up, grad_down, grad_small]
         )
     frames_grad = grad_hidden_one + grad_frames_conv
-    sum_conv = sum_conv.reshape(8, conv_rows, 16, group_width).transpose(2, 0, 1, 3).reshape(conv_weight.shape)
-    sum_small = sum_small.reshape(-1)
-    sum_vectors = sum_small[: vec_rows * vec_cols].reshape(vec_rows, vec_cols)
-    sum_ffn_bias = sum_small[vec_rows * vec_cols : vec_rows * vec_cols + ffn_cols]
-    summed = (sum_qkv, sum_proj, sum_up, sum_down, sum_conv, sum_vectors, sum_ffn_bias)
+    sum_vectors = sum_small[:vec_rows, :vec_cols]
+    sum_ffn_bias = sum_small[vec_rows, :ffn_cols]
     grad_norm = jnp.sqrt(square_total)
-    factor = jnp.minimum(1.0, clip_bound / grad_norm)
     masters = (qkv_weight, proj_weight, up_weight, down_weight, conv_weight, bias_gains, ffn_bias)
     firsts = (qkv_first, proj_first, up_first, down_first, conv_first, bias_gains_first, ffn_bias_first)
     seconds = (qkv_second, proj_second, up_second, down_second, conv_second, bias_gains_second, ffn_bias_second)
+    sum_conv = sum_conv.reshape(8, conv_rows, 16, group_width).transpose(2, 0, 1, 3).reshape(conv_weight.shape)
+    summed = (sum_qkv, sum_proj, sum_up, sum_down, sum_conv, sum_vectors, sum_ffn_bias)
+    factor = jnp.minimum(1.0, clip_bound / grad_norm)
     news, first_news, second_news = [], [], []
     for index in range(7):
         decay = matrix_decay if index < 5 else 0.0
@@ -1399,7 +1636,7 @@
         news.append(new_weight)
         first_news.append(first_new)
         second_news.append(second_new)
-    return (layer_out_full.astype(low_type), frames_grad, grad_norm, *news, *first_news, *second_news)
+    return (layer_out, frames_grad, grad_norm, *news, *first_news, *second_news)
 
 
 def solution(mesh):

time: 499 us -> 453 us (0.908)
  matrix products: 71 us -> 16.7 us
  Pallas kernels: 360 us -> 382 us
  other arithmetic: 32.5 us -> 18.2 us
    dot_general x9 -> x0, matrix products: 54 us -> none  [the longest x1 20.2 us: shards(): jnp.dot(ffn_in, full_up, preferred_element_type=f32) + full_ffn]
    pallas_call x0 -> x2, Pallas kernels: none -> 35.4 us  [the longest x1 31.4 us: ffn_step(): pl.pallas_call(ffn_kernel, in_specs=[vmem, anywhere, anywhere, anywhere,...]
    pallas_call x1, Pallas kernels: 102 us -> 90 us  [close_step(): pl.pallas_call(functools.partial(close_kernel, side_plan, main_plan, n),...]
  transfers between devices with their start and end apart: 3 -> 3, of which waited for: 0 -> 0; matrix products, arithmetic and copies ran while one was open for 16% -> 6% of each run, Pallas kernels for 71% -> 76%
where the time goes in v5:
time: 453 us; the launch traced here: 446 us
  Pallas kernels  382 us (84%)
  other arithmetic  18.2 us (4%)
  between operations  17.3 us (4%)
  matrix products  16.7 us (4%)
  local copies, waits for them, and re-layouts  11 us (2%)
    pallas_call x1, Pallas kernels, open_step(): pl.pallas_call(functools.partial(open_kernel, plan, n, early), in_specs=[...  110 us
    pallas_call x1, Pallas kernels, close_step(): pl.pallas_call(functools.partial(close_kernel, side_plan, main_plan, n),...  90 us
    pallas_call x1, Pallas kernels, attend_back(): pl.pallas_call(functools.partial(attend_back_kernel, plan, n), in_specs=[...  82 us
    pallas_call x1, Pallas kernels, attend(): pl.pallas_call(functools.partial(attend_kernel, plan, n), in_specs=[vmem,...  56.1 us
    pallas_call x1, Pallas kernels, ffn_step(): pl.pallas_call(ffn_kernel, in_specs=[vmem, anywhere, anywhere, anywhere,...  31.4 us
    sub x7, other arithmetic, adam_update(): weight - rate * (first_hat / (jnp.sqrt(second_hat) + adam_eps) + decay *...  10.5 us
  transfers between devices with their start and end apart: 3, of which 0 were waited for; matrix products, arithmetic and copies ran while one was open for 6% of the time, Pallas kernels for 76%

profile of v5, /device:TPU:0, one launch (start us, length us, event | category | flops | bytes accessed | tf_op | source)
XLA Modules:
  0.0 446.0 jit_solution(1072363533113980881)
XLA Ops:
  7.2 2.7 copy.76.conv_i
  9.9 4.0 shard_map.415
  15.3 1.3 fusion.8
  17.8 110.2 %shard_map.416 = (f32[512,768]{1,0:T(8,128)}, f32[512,768]{1,0:T(8,128)}, bf16[512,768]{1,0:T(8,128)(2,1)}, f32[16,768]{1,0:T(8,128)}, f32[1,3072]{1,0:T(1,128)}...) custom-call(s32[2]{0:T(128)} %pad_add_fusion.2.refs_0_, ...), custom_call_target="tpu_custom_call" | custom-call | tf_op jit(solution)/shard_map/pallas_call | solution.py:991
  128.1 0.8 slice_reduce_fusion.3
  129.3 6.0 %fusion.refs_1_ = bf16[2304,512]{1,0:T(8,128)(2,1)} fusion(bf16[768,2304]{1,0:T(8,128)(2,1)} %bitcast.63, bf16[512,768]{1,0:T(8,128)(2,1)} %get-tuple-element.65, f32[2304]{0:T(1024)S(1)} %add.154), kind=kOutput, calls=%fused_computation.2 | convolution fusion | flops 1814298624 | bytes 6693888 | tf_op jit(solution)/shard_map/dot_general | solution.py:1572
  135.3 56.1 %shard_map.417 = (bf16[576,2048]{1,0:T(8,128)(2,1)}, bf16[768,512]{1,0:T(8,128)(2,1)S(1)}, f32[3,1,2048]{2,1,0:T(1,128)S(1)}, f32[192,2048]{1,0:T(8,128)S(1)}) custom-call(s32[1,2048]{1,0:T(1,128)S(1)} %pad_add_fusion.1.refs_0_, bf16[2304,512]{1,0:T(8,128)(2,1)} %fusion.refs_1_), custom_call_target="tpu_custom_call" | custom-call | tf_op jit(solution)/shard_map/pallas_call | solution.py:1151
  191.5 1.1 copy-done
  193.2 0.9 copy-done.3
  194.1 31.4 %shard_map.418 = (bf16[512,768]{1,0:T(8,128)(2,1)}, f32[512,768]{1,0:T(8,128)}, bf16[768,512]{1,0:T(8,128)(2,1)}, f32[9,768]{1,0:T(8,128)}, f32[1,3072]{1,0:T(1,...) custom-call(bf16[768,512]{1,0:T(8,128)(2,1)} %copy-done.3, ...), custom_call_target="tpu_custom_call" | custom-call | flops 16307453952 | bytes 30000000 | tf_op jit(solution)/shard_map/pallas_call | solution.py:763
  225.5 82.0 %shard_map.419 = (bf16[2304,512]{1,0:T(8,128)(2,1)}, f32[8,128]{1,0:T(8,128)}, f32[24,768]{1,0:T(8,128)}, f32[4,24,768]{2,1,0:T(8,128)}) custom-call(s32[1,2048]{1,0:T(1,128)} %copy-done.1, bf16[576,2048]{1,0:T(8,128)(2,1)} %get-tuple-element.75.refs_1_, f32[3,1,2048]{2,1,0:T(1,128)} %copy-done.2, f32[192,2048]{1,0:T(8,128)} %copy-done, ...), custom_call_target="tpu_custom_call" | custom-call | tf_op jit(solution)/shard_map/pallas_call | solution.py:1269
  307.6 6.8 %fusion.20 = (bf16[768]{0:T(1024)(128)(2,1)S(1)}, bf16[512,768]{1,0:T(8,128)(2,1)}, f32[512,768]{1,0:T(8,128)}) fusion(f32[512,768]{1,0:T(8,128)S(1)} %copy-done.28, f32[512,768]{1,0:T(8,128)} %get-tuple-element.74, bf16[2304,512]{1,0:T(8,128)(2,1)} %get-tuple-element.81, bf16[768,2304]{1,0:T(8,128)(2,1)} %bitcast.64), kind=kOutput, calls=%fused_computation.58 | convolution fusion | flops 1813511424 | bytes 11404800 | tf_op jit(solution)/shard_map/dot_general | solution.py:1595
  315.3 0.8 slice.49
  317.0 3.9 convolution_convert_fusion
  320.9 90.0 %shard_map.420 = (f32[512,768]{1,0:T(8,128)}, f32[8,128]{1,0:T(8,128)}, f32[8,24,768]{2,1,0:T(8,128)}, f32[24,2304]{1,0:T(8,128)}, f32[16,128]{1,0:T(8,128)}) custom-call(s32[2]{0:T(128)} %pad_add_fusion.2.refs_0_, bf16[16,584,768]{2,1,0:T(8,128)(2,1)} %get-tuple-element.82.refs_1_, bf16[512,768]{1,0:T(8,128)(2,1)} %get-tuple-element.172.refs_2_, ...), custom_call_target="tpu_custom_call" | custom-call | tf_op jit(solution)/shard_map/pallas_call | solution.py:1391
  410.9 2.8 add.159
  413.8 1.0 bitcast_convert_fusion.refs_1_
  414.8 8.3 %shard_map.421 = f32[8,128]{1,0:T(8,128)S(1)} custom-call(f32[8,128]{1,0:T(8,128)S(1)} %add.160.refs_0_, f32[4,24,768]{2,1,0:T(8,128)S(1)} %bitcast_convert_fusion.refs_1_), custom_call_target="tpu_custom_call" | custom-call | tf_op jit(solution)/shard_map/pallas_call | solution.py:1430
  427.2 1.3 multiply_subtract_fusion.6
  429.2 1.7 multiply_subtract_fusion.4
  430.8 2.2 multiply_subtract_fusion.3
  433.1 2.2 multiply_subtract_fusion.2
  435.3 1.0 multiply_subtract_fusion.1
  436.4 1.5 multiply_subtract_fusion
  (100 shorter events, 8.7 us)
Async XLA Ops:
  7.2 8.1 %copy-start.23 = (s32[1,2048]{1,0:T(1,128)S(1)}, s32[1,2048]{1,0:T(1,128)}, u32[]{:S(2)}) copy-start(s32[1,2048]{1,0:T(1,128)} %param.26) | copy-start | bytes 24580
  7.2 186.9 %all-gather.5.cloned.1.call-start = ((), (), s32[]{:S(2)}) async-start(), calls=%async_computation.2 | async-start | bytes 4866048 | tf_op jit(solution)/shard_map/all_gather | solution.py:1479
  13.9 180.2 %all-gather.7.cloned.1.call-start = ((), (), s32[]{:S(2)}) async-start(), calls=%async_computation.3 | async-start | bytes 4866048 | tf_op jit(solution)/shard_map/all_gather | solution.py:1479
  14.7 399.1 %reduce-scatter.2.cloned.1.call-start = ((), (), s32[]{:S(2)}) async-start(), calls=%async_computation.1 | async-start | bytes 4866048 | tf_op jit(solution)/shard_map/reduce_scatter | solution.py:1584
  129.3 6.0 %copy-start.1 = (s32[1,2048]{1,0:T(1,128)}, s32[1,2048]{1,0:T(1,128)S(1)}, u32[]{:S(2)}) copy-start(s32[1,2048]{1,0:T(1,128)S(1)} %pad_add_fusion.1.refs_0_) | copy-start | bytes 24580
  225.5 82.0 %copy-start.28 = (f32[512,768]{1,0:T(8,128)S(1)}, f32[512,768]{1,0:T(8,128)}, u32[]{:S(2)}) copy-start(f32[512,768]{1,0:T(8,128)} %get-tuple-element.83) | copy-start | bytes 4718596
  307.6 6.9 %copy-start.4 = (bf16[2304,512]{1,0:T(8,128)(2,1)S(1)}, bf16[2304,512]{1,0:T(8,128)(2,1)}, u32[]{:S(2)}) copy-start(bf16[2304,512]{1,0:T(8,128)(2,1)} %get-tuple-element.81) | copy-start | bytes 7077892
  314.4 2.7 copy-start.29
  320.9 90.0 %copy-start.6 = (f32[512,768]{1,0:T(8,128)S(1)}, f32[512,768]{1,0:T(8,128)}, u32[]{:S(2)}) copy-start(f32[512,768]{1,0:T(8,128)} %get-tuple-element.177) | copy-start | bytes 4718596
  410.9 2.9 copy-start.24
  410.9 2.8 copy-start.25
  410.9 13.5 %copy-start.15 = (f32[4,24,768]{2,1,0:T(8,128)S(1)}, f32[4,24,768]{2,1,0:T(8,128)}, u32[]{:S(2)}) copy-start(f32[4,24,768]{2,1,0:T(8,128)} %get-tuple-element.93) | copy-start | bytes 884740
  410.9 14.3 %copy-start.10 = (f32[8,24,768]{2,1,0:T(8,128)S(1)}, f32[8,24,768]{2,1,0:T(8,128)}, u32[]{:S(2)}) copy-start(f32[8,24,768]{2,1,0:T(8,128)} %get-tuple-element.94) | copy-start | bytes 1769476
  413.8 11.5 %copy-start.11 = (bf16[1,4,24,768]{3,2,1,0:T(8,128)(2,1)S(1)}, bf16[1,4,24,768]{3,2,1,0:T(8,128)(2,1)}, u32[]{:S(2)}) copy-start(bf16[1,4,24,768]{3,2,1,0:T(8,128)(2,1)} %reduce-scatter.2.cloned.1.call-done) | copy-start | bytes 442372
  426.1 2.4 copy-start.18
  426.2 3.0 copy-start.14
  426.7 6.4 %copy-start.8 = (f32[24,3072]{1,0:T(8,128)S(1)}, f32[24,3072]{1,0:T(8,128)}, u32[]{:S(2)}) copy-start(f32[24,3072]{1,0:T(8,128)} %up_i.1) | copy-start | bytes 884740
  427.2 8.1 %copy-start.7 = (f32[4,24,768]{2,1,0:T(8,128)S(1)}, f32[4,24,768]{2,1,0:T(8,128)}, u32[]{:S(2)}) copy-start(f32[4,24,768]{2,1,0:T(8,128)} %broadcast_multiply_fusion.1) | copy-start | bytes 884740
  427.2 8.1 %copy-start.9 = (f32[96,768]{1,0:T(8,128)S(1)}, f32[96,768]{1,0:T(8,128)}, u32[]{:S(2)}) copy-start(f32[96,768]{1,0:T(8,128)} %down_i.1) | copy-start | bytes 884740
  427.2 8.1 %copy-start.16 = (f32[96,768]{1,0:T(8,128)S(1)}, f32[96,768]{1,0:T(8,128)}, u32[]{:S(2)}) copy-start(f32[96,768]{1,0:T(8,128)} %param.37) | copy-start | bytes 884740
  427.2 8.1 %copy-start.17 = (f32[96,768]{1,0:T(8,128)S(1)}, f32[96,768]{1,0:T(8,128)}, u32[]{:S(2)}) copy-start(f32[96,768]{1,0:T(8,128)} %param.44) | copy-start | bytes 884740
  433.0 3.3 copy-start.5
  433.0 3.3 copy-start.12
  433.0 3.3 copy-start.13
  (9 other events, 11.5 us)
Sparse Core Ops, SparseCore 0:
  14.1 81.0 all-gather.4
  98.7 67.6 all-gather.6
  225.7 118.7 reduce-scatter.1
